TPU v7x, 32 devices: a whole 2x2x4 slice. The times are simulated.
32 devices in a mesh: traj: 4 (over y, x), strip: 8 (over z, core).
Axes of the slice: x: 2, y: 2, z: 4, core: 2. Of those that a mesh axis runs over, the one named last changes fastest.
Arguments:
- velocity: float32 [8, 2, 128, 128], P('traj', None, 'strip'), may hold values from -6 to 6
- lengths: int32 [8], P('traj'), may hold values from 1 to 2
- cotangent: float32 [8, 2, 128, 128], P('traj', None, 'strip'), may hold values from -6 to 6
- first_kernel: bfloat16 [9, 64, 2], replicated, may hold values from -1.5 to 1.5
- first_bias: float32 [64], replicated, may hold values from -3 to 3
- middle_kernels: bfloat16 [5, 9, 64, 64], replicated, may hold values from -0.25 to 0.25
- middle_biases: float32 [5, 64], replicated, may hold values from -3 to 3
- last_kernel: bfloat16 [9, 64, 64], replicated, may hold values from -0.0625 to 0.0625
- last_bias: float32 [64], replicated, may hold values from -1.2 to 1.2
Outputs:
- final_velocity: float32 [8, 2, 128, 128], P('traj', None, 'strip')
- velocity_grad: float32 [8, 2, 128, 128], P('traj', None, 'strip')
- grad_first_kernel: float32 [9, 64, 2], replicated
- grad_first_bias: float32 [64], replicated
- grad_middle_kernels: float32 [5, 9, 64, 64], replicated
- grad_middle_biases: float32 [5, 64], replicated
- grad_last_kernel: float32 [9, 64, 64], replicated
- grad_last_bias: float32 [64], replicated
All inputs are finite; a program needn't handle non-finite values.
Results may differ from a plain program's by a relative error of at most 0.025.
Values may be sent and summed in bfloat16 or wider, within the bound.
No kernel may reach another device: no remote copies, remote signals or barrier semaphores. Data moves between devices by JAX's collectives and lax.ppermute only.
A program may use at most 192 MiB of HBM per device.

v0:
```python
import functools
import math

import jax
import jax.numpy as jnp
import numpy as np
from jax import lax
from jax.experimental import pallas as pl
from jax.experimental.pallas import tpu as pltpu
from jax.sharding import PartitionSpec as P

STEPS = 2
DT = 0.25
MARGIN = 16
MID = 8
RAW = 2
CH = 64
LAYERS = 6
N = 128
bf16 = jnp.bfloat16
f32 = jnp.float32
NT = (((1,), (1,)), ((), ()))
VMEM_BYTES = 36 * 2**20


def reach(layer):
    return 12 - layer


def lanes(x, s):
    return x if s == 0 else pltpu.roll(x, (-s) % x.shape[1], 1)


def rows(x, s):
    return x if s == 0 else pltpu.roll(x, (-s) % x.shape[0], 0)


def poisson_tables(length):
    k = np.arange(length)
    angle = 2.0 * math.pi * ((k[:, None] * k[None, :]) % length) / length
    table = (np.cos(angle) + np.sin(angle)) / math.sqrt(length)
    eigen = 2.0 - 2.0 * np.cos(2.0 * math.pi * k / length)
    total = eigen[:, None] + eigen[None, :]
    total[0, 0] = 1.0
    weight = 1.0 / total
    weight[0, 0] = 0.0
    return np.stack([table, weight]).astype(np.float32)


def split(x):
    high = x.astype(bf16)
    return high, (x - high.astype(f32)).astype(bf16)


def times_right(x, right):
    high, low = split(x)
    return jnp.dot(jnp.concatenate([high, low, high], axis=1), right[...], preferred_element_type=f32)


def times_left(x, left):
    high, low = split(x)
    return jnp.dot(left[...], jnp.concatenate([high, high, low], axis=0), preferred_element_type=f32)


def project(fields, right, left, weight):
    count = len(fields)
    source = [u - lanes(u, -1) + (v - rows(v, -1)) for u, v in fields]
    x = times_right(jnp.concatenate(source, axis=0), right)
    x = jnp.concatenate([x[i * N : (i + 1) * N] for i in range(count)], axis=1)
    x = times_left(x, left) * jnp.concatenate([weight[...]] * count, axis=1)
    x = times_left(x, left)
    x = jnp.concatenate([x[:, i * N : (i + 1) * N] for i in range(count)], axis=0)
    x = times_right(x, right)
    out = []
    for i, (u, v) in enumerate(fields):
        p = -x[i * N : (i + 1) * N]
        out.append((u - (lanes(p, 1) - p), v - (rows(p, 1) - p)))
    return out


def local(x, count):
    return jnp.concatenate([x[N - MARGIN :], x[: count + MARGIN]], axis=0)


def fold(o):
    third = o.shape[0] // 3
    return lanes(o[:third], -1) + o[third : 2 * third] + lanes(o[2 * third :], 1)


def conv_rows(window, kernel, low, high, emit, between=lambda: None):
    starts = list(range(low, high, 2))
    for k in range(0, len(starts), 2):
        group = starts[k : k + 2]
        o = jnp.dot(
            kernel[...],
            jnp.concatenate([window(r) for r in group], axis=1),
            preferred_element_type=f32,
        )
        half = o.shape[0] // 2
        for i, r in enumerate(group):
            part = o[:, i * N : (i + 1) * N]
            emit(r, part[:half])
            emit(r + 1, part[half:])
        between()


def first_window(us, vs, r):
    a = r - 1 + MARGIN
    return jnp.concatenate(
        [us[1, a : a + 4, :], vs[1, a : a + 4, :], jnp.zeros((8, N), f32)], axis=0
    ).astype(bf16)


def row_window(ref, low):
    return lambda r: ref[(r - 1 - low) * CH : (r + 3 - low) * CH, :]


def gelu_value(z):
    c = math.sqrt(2.0 / math.pi)
    zz = z * z
    h = 0.5 + 0.5 * jnp.tanh(z * (c + (c * 0.044715) * zz))
    return z * h, h, zz


def gelu_slope(f, h, zz):
    c = math.sqrt(2.0 / math.pi)
    return h + (f - f * h) * (2.0 * c + (6.0 * c * 0.044715) * zz)


def spread_columns(u, v, us, vs):
    for j in range(4):
        us[j] = lanes(u, j - 1)
        vs[j] = lanes(v, j - 1)


def network_forward(count, us, vs, w_first, w_hidden, bias, feats, slopes, raw, raw_done):
    for m in range(1, LAYERS + 1):
        low = -reach(m)

        def emit(r, o, m=m, low=low):
            value, h, zz = gelu_value(fold(o) + bias[m - 1])
            feats[m - 1][(r - low) * CH : (r - low + 1) * CH, :] = value.astype(bf16)
            if -m <= r < count + m:
                slopes[m - 1][(r + m) * CH : (r + m + 1) * CH, :] = gelu_slope(value, h, zz).astype(bf16)

        if m == 1:
            conv_rows(functools.partial(first_window, us, vs), w_first, low, count - low, emit)
        else:
            conv_rows(
                row_window(feats[m - 2], -reach(m - 1)), w_hidden.at[m - 2], low, count - low, emit
            )

    def emit_raw(r, o):
        raw[(r + MID) * CH : (r + MID + 1) * CH, :] = fold(o) + bias[LAYERS]
        raw_done(r)

    conv_rows(
        row_window(feats[-1], -reach(LAYERS)), w_hidden.at[LAYERS - 1], -RAW, count + RAW, emit_raw
    )


TARGETS = ((0.0, -0.5), (-0.5, 0.0), (0.0, -0.5), (-0.5, 0.0))


def moments(values):
    cols = [values[j] + values[4 + j] + (values[8 + j] + values[12 + j]) for j in range(4)]
    lines = [values[4 * i] + values[4 * i + 1] + (values[4 * i + 2] + values[4 * i + 3]) for i in range(4)]
    mean = (cols[0] + cols[1] + (cols[2] + cols[3])) * (1.0 / 16.0)
    mx = (1.5 * (cols[3] - cols[0]) + 0.5 * (cols[2] - cols[1])) * (1.0 / 20.0)
    my = (1.5 * (lines[3] - lines[0]) + 0.5 * (lines[2] - lines[1])) * (1.0 / 20.0)
    return mean, mx, my


def less(values, mean, mx, my):
    by_col = [mean + mx * (j - 1.5) for j in range(4)]
    by_line = [my * (i - 1.5) for i in range(4)]
    return [values[p] - (by_col[p % 4] + by_line[p // 4]) for p in range(16)]


def total_of(terms):
    while len(terms) > 1:
        terms = [a + b for a, b in zip(terms[::2], terms[1::2])] + terms[len(terms) // 2 * 2 :]
    return terms[0]


def patches(src, q):
    a = MARGIN - MID + 8 * q
    return [src[p % 4, a + p // 4 - 1 : a + p // 4 + 7, :] for p in range(16)]


def raw_rows(raw, k, q):
    return [raw[pl.ds(8 * q * CH + k * 16 + p, 8, stride=CH), :] for p in range(16)]


def interpolate(q, sources, raw, interp):
    for which, src in enumerate(sources):
        patch = patches(src, q)
        mean, mx, my = moments(patch)
        clear = less(patch, mean, mx, my)
        for k in (2 * which, 2 * which + 1):
            tx, ty = TARGETS[k]
            value = total_of([a * b for a, b in zip(raw_rows(raw, k, q), clear)])
            interp[k, 8 * q : 8 * q + 8, :] = value + (mean + (tx * mx if tx else ty * my))


def raw_gradient(q, sources, ginterp, graw32, graw):
    at = slice(8 * q, 8 * q + 8)
    for which, src in enumerate(sources):
        patch = patches(src, q)
        clear = less(patch, *moments(patch))
        for k in (2 * which, 2 * which + 1):
            g = ginterp[k, at, :]
            for p in range(16):
                graw32[pl.ds(8 * q * CH + k * 16 + p, 8, stride=CH), :] = clear[p] * g
    at = slice(8 * q * CH, 8 * (q + 1) * CH)
    graw[at, :] = graw32[at, :].astype(bf16)


def spread_back(q, which, raw, ginterp, lines):
    k = 2 * which
    at = slice(8 * q, 8 * q + 8)
    g, h = ginterp[k, at, :], ginterp[k + 1, at, :]
    values = [a * g + b * h for a, b in zip(raw_rows(raw, k, q), raw_rows(raw, k + 1, q))]
    mean, mx, my = moments(values)
    values = less(values, mean - (g + h) * (1.0 / 16.0), mx + h * (0.5 / 20.0), my + g * (0.5 / 20.0))
    for i in range(4):
        lines[which, i, at, :] = total_of([lanes(values[4 * i + j], 1 - j) for j in range(4)])


def carriers(u, v):
    return (
        0.5 * (u + lanes(u, 1)),
        0.5 * (v + lanes(v, 1)),
        0.5 * (u + rows(u, 1)),
        0.5 * (v + rows(v, 1)),
    )


def middle(x, count):
    return x[MARGIN - MID : MARGIN + MID + count]


def provisional(count, u, v, interp):
    flux = [middle(x, count) * interp[k] for k, x in enumerate(carriers(u, v))]
    u, v = middle(u, count), middle(v, count)
    su = u - DT * (flux[0] - lanes(flux[0], -1) + (flux[1] - rows(flux[1], -1)))
    sv = v - DT * (flux[2] - lanes(flux[2], -1) + (flux[3] - rows(flux[3], -1)))
    return su[MID : MID + count], sv[MID : MID + count]


def flux_gradients(count, gu, gv):
    return [
        middle(x, count) * (-DT)
        for x in (gu - lanes(gu, 1), gu - rows(gu, 1), gv - lanes(gv, 1), gv - rows(gv, 1))
    ]


def interp_gradients(count, gu, gv, u, v, ginterp):
    for k, (g, x) in enumerate(zip(flux_gradients(count, gu, gv), carriers(u, v))):
        ginterp[k] = g * middle(x, count)


def velocity_gradients(count, gu, gv, interp, lines):
    half = [0.5 * g * interp[k] for k, g in enumerate(flux_gradients(count, gu, gv))]
    out = []
    for which, g in enumerate((gu, gv)):
        along, across = half[which], half[2 + which]
        x = middle(g, count) + (along + lanes(along, -1)) + (across + rows(across, -1))
        x = x[MID : MID + count]
        for i in range(4):
            x = x + lines[which, i, MID + 1 - i : MID + 1 - i + count, :]
        out.append(x)
    return out


def network_backward(count, w_hidden, slopes, graw, grads, between=lambda: None):
    for m in range(LAYERS, 0, -1):
        source = row_window(graw, -MID) if m == LAYERS else row_window(grads[m], -(m + 1))

        def emit(r, o, m=m):
            at = slice((r + m) * CH, (r + m + 1) * CH)
            grads[m - 1][at, :] = (fold(o) * slopes[m - 1][at, :].astype(f32)).astype(bf16)

        conv_rows(source, w_hidden.at[m - 1], -m, count + m, emit, between)


def input_gradient(count, w_first, grad, gvel):
    window = row_window(grad, -1)
    starts = list(range(0, count, 2))
    for k in range(0, len(starts), 2):
        group = starts[k : k + 2]
        o = jnp.dot(
            w_first[...],
            jnp.concatenate([window(r) for r in group], axis=1),
            preferred_element_type=f32,
        )
        for i, r in enumerate(group):
            part = o[:, i * N : (i + 1) * N]
            both = lanes(part, -1)[0:4] + part[4:8] + lanes(part, 1)[8:12]
            gvel[0, r : r + 2, :] = both[0:2]
            gvel[1, r : r + 2, :] = both[2:4]


def weight_gradients(count, us, vs, feats, graw, grads, buffer, previous):
    starts = list(range(0, count, 2))

    def product(m):
        ref, low = (graw, -MID) if m == LAYERS + 1 else (grads[m - 1], -m)
        left, total = [], None
        for r in starts:
            g = [ref[(r + k - low) * CH : (r + k + 1 - low) * CH, :] for k in range(2)]
            left.append(jnp.concatenate([lanes(x, -e) for x in g for e in (-1, 0, 1)], axis=0))
            for x in g:
                x = x.astype(f32)
                total = x if total is None else total + x
        if m == 1:
            right = [first_window(us, vs, r) for r in starts]
        else:
            right = [row_window(feats[m - 2], -reach(m - 1))(r) for r in starts]
        out = lax.dot_general(
            jnp.concatenate(left, axis=1), jnp.concatenate(right, axis=1), NT, preferred_element_type=f32
        )
        return out, jnp.sum(total, axis=1, keepdims=True)

    def put(block, value):
        at = slice(block * 3 * CH, (block + 1) * 3 * CH)
        if previous is not None:
            value = value + previous[at, :]
        buffer[at, :] = value.astype(buffer.dtype)

    def folded(x):
        return x[: 3 * CH, : 3 * CH] + x[3 * CH :, CH:]

    lane = lax.broadcasted_iota(jnp.int32, (CH, N), 1)
    columns = jnp.zeros((CH, N), f32)
    for pair in range(2, -1, -1):
        upper, total = product(3 + 2 * pair)
        columns = jnp.where(lane == 34 + 2 * pair, total, columns)
        lower, total = product(2 + 2 * pair)
        columns = jnp.where(lane == 33 + 2 * pair, total, columns)
        wide = jnp.concatenate([folded(lower), folded(upper)], axis=1)
        for q in range(3):
            put(3 * pair + q, wide[:, q * N : (q + 1) * N])
    first, total = product(1)
    columns = jnp.where(lane == 32, total, columns)
    first = jnp.concatenate([first[: 3 * CH], first[3 * CH :], jnp.zeros((3 * CH, N - 32), f32)], axis=1)
    put(9, first + jnp.concatenate([columns, jnp.zeros((2 * CH, N), f32)], axis=0))


def prepare_kernel(core, *refs):
    own, f_first, f_hidden, b_first, b_hidden, bias, right, left, weight = refs[9:18]
    sems = refs[27]
    copies = [pltpu.make_async_copy(refs[i], refs[18 + i], sems.at[i]) for i in range(9)]
    for copy in copies:
        copy.start()
    for copy in copies:
        copy.wait()
    vel, cot, first, first_bias, middle, middle_bias, last, last_bias, tables = refs[18:27]
    upper = core[0] == 0
    own[0] = jnp.where(upper, vel[0], vel[1])
    own[1] = jnp.where(upper, cot[0], cot[1])
    zero = jnp.zeros((CH, CH), bf16)
    for m in range(LAYERS):
        tap = (lambda a, e: last[3 * a + e]) if m == LAYERS - 1 else (lambda a, e: middle[m, 3 * a + e])
        for two in range(2):
            for e in range(3):
                at = slice((two * 3 + e) * CH, (two * 3 + e + 1) * CH)
                taps = [tap(q - two, e) if 0 <= q - two < 3 else zero for q in range(4)]
                f_hidden[m, at, :] = jnp.concatenate(taps, axis=1)
                taps = [tap(2 - q + two, 2 - e) if 0 <= q - two < 3 else zero for q in range(4)]
                b_hidden[m, at, :] = jnp.concatenate(
                    [jnp.concatenate(taps[:2], axis=0).T, jnp.concatenate(taps[2:], axis=0).T], axis=1
                )
    lines = jnp.zeros((1, CH), f32)
    for two in range(2):
        for e in range(3):
            taps = [lines] * 16
            for a in range(3):
                for ch in range(2):
                    taps[4 * ch + a + two] = first[3 * a + e, ch : ch + 1, :].astype(f32)
            at = slice((two * 3 + e) * CH, (two * 3 + e + 1) * CH)
            f_first[at, :] = jnp.concatenate(taps, axis=0).T.astype(bf16)
    taps = []
    for e in range(3):
        for ch in range(2):
            for two in range(2):
                line = [
                    first[3 * (2 - q + two) + 2 - e, ch : ch + 1, :].astype(f32) if 0 <= q - two < 3 else lines
                    for q in range(4)
                ]
                taps.append(jnp.concatenate(line, axis=1))
    taps.append(jnp.zeros((4, 4 * CH), f32))
    b_first[...] = jnp.concatenate(taps, axis=0).astype(bf16)
    for m in range(LAYERS + 1):
        if 0 < m < LAYERS:
            line = middle_bias[m - 1 : m, :]
        else:
            line = (first_bias if m == 0 else last_bias)[...].reshape(1, CH)
        bias[m] = jnp.broadcast_to(line, (N, CH)).T
    high, low = split(tables[0])
    right[...] = jnp.concatenate([high, high, low], axis=0)
    left[...] = jnp.concatenate([high, low, high], axis=1)
    weight[...] = tables[1]


def forward_kernel(count, core, own, partner, cross, same, cot_partner, w_first, w_hidden, bias, *rest):
    block, ext, raw = rest[:3]
    feats, slopes = rest[3 : 3 + LAYERS], rest[3 + LAYERS : 3 + 2 * LAYERS]
    us, vs, interp = rest[3 + 2 * LAYERS :]
    upper = core[0] == 0
    above = jnp.where(upper, cross[0], same[1])[:, -MARGIN:]
    below = jnp.where(upper, same[0], cross[1])[:, :MARGIN]

    def pair(mine, other, i):
        other = jnp.where(upper, other[0, i], other[1, i])
        return [jnp.where(upper, mine[i], other), jnp.where(upper, other, mine[i])]

    for i in range(2):
        ext[i] = jnp.concatenate([above[i], *pair(own[0], partner, i), below[i]], axis=0)
        block[2 + i] = jnp.concatenate(pair(own[1], cot_partner, i), axis=0)
    u, v = ext[0], ext[1]
    spread_columns(u, v, us, vs)

    def raw_done(r):
        at = r + 1 + MID
        last = count + RAW
        if at % 8 == 0:
            interpolate(at // 8 - 1, (us, vs), raw, interp)
        elif r + 1 == last:
            interpolate(at // 8, (us, vs), raw, interp)

    network_forward(count, us, vs, w_first, w_hidden, bias, feats, slopes, raw, raw_done)
    su, sv = provisional(count, u, v, interp)
    block[0] = su
    block[1] = sv


def step_mask(lengths, core, step):
    return jnp.where(lengths[core[0]] > step, 1.0, 0.0).astype(f32)


def joined(gathered, i):
    return jnp.concatenate([g[i] for g in gathered], axis=0)


def middle_kernel(count, blocks, core, lengths, *refs):
    gathered, refs = refs[:blocks], refs[blocks:]
    vel, right, left, weight, w_first, w_hidden, bias, b_first, b_hidden = refs[:9]
    back, ext, graw = refs[9:12]
    feats, grads, refs = refs[12:18], refs[18:24], refs[24:]
    us, vs, raw, graw32, interp, ginterp, lines, gvel = refs[:8]
    slopes = refs[8:14]
    su, sv, cu, cv = [joined(gathered, i) for i in range(4)]
    m0, m1 = step_mask(lengths, core, 0), step_mask(lengths, core, 1)
    (nu, nv), (gu, gv) = project([(su, sv), (m1 * cu, m1 * cv)], right, left, weight)
    u = vel[0] + m0 * (local(nu, count) - vel[0])
    v = vel[1] + m0 * (local(nv, count) - vel[1])
    ext[0] = u
    ext[1] = v
    gu, gv = local(gu, count), local(gv, count)
    spread_columns(u, v, us, vs)
    interp_gradients(count, gu, gv, u, v, ginterp)
    chunks = (count + 2 * MID) // 8
    for q in range(chunks):
        raw_gradient(q, (us, vs), ginterp, graw32, graw)
    network_forward(count, us, vs, w_first, w_hidden, bias, feats, slopes, raw, lambda r: None)
    tasks = []
    for q in range(chunks):
        tasks.append(functools.partial(interpolate, q, (us, vs), raw, interp))
        tasks += [functools.partial(spread_back, q, which, raw, ginterp, lines) for which in range(2)]
    turn = [0]

    def between():
        turn[0] += 1
        if tasks and turn[0] % 2 == 0:
            tasks.pop(0)()

    network_backward(count, b_hidden, slopes, graw, grads, between)
    for task in tasks:
        task()
    su, sv = provisional(count, u, v, interp)
    back[0] = su
    back[1] = sv
    input_gradient(count, b_first, grads[0], gvel)
    du, dv = velocity_gradients(count, gu, gv, interp, lines)
    back[2] = (1.0 - m1) * cu[:count] + du + gvel[0]
    back[3] = (1.0 - m1) * cv[:count] + dv + gvel[1]


def weights_kernel(count, ext, graw, *refs):
    feats, grads, buffer, us, vs = refs[:6], refs[6:12], refs[12], refs[13], refs[14]
    spread_columns(ext[0], ext[1], us, vs)
    weight_gradients(count, us, vs, feats, graw, grads, buffer, None)


def backward_kernel(count, blocks, core, lengths, *refs):
    gathered, refs = refs[:blocks], refs[blocks:]
    vel, right, left, weight, b_hidden, previous = refs[:6]
    feats, slopes = refs[6:12], refs[12:18]
    gstar, buffer, grad_first, us, vs, graw32, graw, ginterp = refs[18:26]
    grads = (grad_first,) + refs[26:31]
    m0 = step_mask(lengths, core, 0)
    ((gu, gv),) = project([(m0 * joined(gathered, 2), m0 * joined(gathered, 3))], right, left, weight)
    u, v = vel[0], vel[1]
    gu, gv = local(gu, count), local(gv, count)
    gstar[0] = gu
    gstar[1] = gv
    spread_columns(u, v, us, vs)
    interp_gradients(count, gu, gv, u, v, ginterp)
    for q in range((count + 2 * MID) // 8):
        raw_gradient(q, (us, vs), ginterp, graw32, graw)
    network_backward(count, b_hidden, slopes, graw, grads)
    weight_gradients(count, us, vs, feats, graw, grads, buffer, previous)


def finish_kernel(count, blocks, core, lengths, *refs):
    gathered, refs = refs[:blocks], refs[blocks:]
    vel, now, gstar, raw, grad_first, right, left, weight, b_first, out = refs[:10]
    us, vs, interp, ginterp, lines, gvel = refs[10:]
    m0, m1 = step_mask(lengths, core, 0), step_mask(lengths, core, 1)
    ((nu, nv),) = project([(joined(gathered, 0), joined(gathered, 1))], right, left, weight)
    own = slice(MARGIN, MARGIN + count)
    out[0] = now[0, own] + m1 * (nu[:count] - now[0, own])
    out[1] = now[1, own] + m1 * (nv[:count] - now[1, own])
    u, v, gu, gv = vel[0], vel[1], gstar[0], gstar[1]
    spread_columns(u, v, us, vs)
    interp_gradients(count, gu, gv, u, v, ginterp)
    for q in range((count + 2 * MID) // 8):
        interpolate(q, (us, vs), raw, interp)
        for which in range(2):
            spread_back(q, which, raw, ginterp, lines)
    input_gradient(count, b_first, grad_first, gvel)
    du, dv = velocity_gradients(count, gu, gv, interp, lines)
    out[2] = (1.0 - m0) * gathered[0][2] + du + gvel[0]
    out[3] = (1.0 - m0) * gathered[0][3] + dv + gvel[1]


def unpack_kernel(core, mine, other, first, first_bias, middle, middle_bias, last, last_bias):
    upper = core[0] == 0
    half = mine.shape[0]

    def block(b):
        lines = []
        for low, high, a, c in ((0, half, mine, other), (half, 2 * half, other, mine)):
            start, stop = max(b * 3 * CH, low), min((b + 1) * 3 * CH, high)
            if start < stop:
                x = jnp.where(upper, a[start - low : stop - low, :], c[start - low : stop - low, :])
                lines.append(x.astype(f32))
        return lines[0] if len(lines) == 1 else jnp.concatenate(lines, axis=0)

    for pair in range(3):
        wide = jnp.concatenate([block(3 * pair + q) for q in range(3)], axis=1)
        for side in range(2):
            m = 2 * pair + side
            for a in range(3):
                at = (3 * side + a) * CH
                part = wide[:, at : at + CH]
                for e in range(3):
                    value = part[e * CH : (e + 1) * CH]
                    if m < LAYERS - 1:
                        middle[m, 3 * a + e] = value
                    else:
                        last[3 * a + e] = value
    rest = block(9)
    turned = [rest[e * CH : (e + 1) * CH].T for e in range(3)]
    for a in range(3):
        for e in range(3):
            for ch in range(2):
                low, high = 4 * ch + a, 16 + 4 * ch + a + 1
                first[3 * a + e, ch : ch + 1, :] = turned[e][low : low + 1] + turned[e][high : high + 1]
    turned = turned[0]
    first_bias[...] = turned[32]
    middle_bias[...] = turned[33 : 33 + LAYERS - 1]
    last_bias[...] = turned[32 + LAYERS]


VMEM = pl.BlockSpec(memory_space=pltpu.VMEM)
SMEM = pl.BlockSpec(memory_space=pltpu.SMEM)
PARAMS = pltpu.CompilerParams(vmem_limit_bytes=VMEM_BYTES)


def array(dtype, *shape):
    return jax.ShapeDtypeStruct(shape, dtype)


def cost(flops, moved):
    return pl.CostEstimate(flops=flops, bytes_accessed=moved, transcendentals=0)


def field(count, *lead):
    return pltpu.VMEM(lead + (count, N), f32)


def feature_arrays(count):
    return [array(bf16, (count + 2 * reach(m)) * CH, N) for m in range(1, LAYERS + 1)]


def slope_arrays(count):
    return [array(bf16, (count + 2 * m) * CH, N) for m in range(1, LAYERS + 1)]


def call(kernel, name, flops, smem, inputs, out, scratch=()):
    return pl.pallas_call(
        kernel,
        in_specs=[SMEM] * len(smem) + [VMEM] * len(inputs),
        out_specs=jax.tree.map(lambda _: VMEM, out),
        out_shape=out,
        scratch_shapes=list(scratch),
        compiler_params=PARAMS,
        cost_estimate=cost(flops, 10**6),
        name=name,
    )(*smem, *inputs)


def run_prepare(core, vel, cot, params):
    rc = vel.shape[2]
    out = [
        array(f32, 2, 2, rc, N),
        array(bf16, 6 * CH, 16),
        array(bf16, LAYERS, 6 * CH, 4 * CH),
        array(bf16, 16, 4 * CH),
        array(bf16, LAYERS, 6 * CH, 4 * CH),
        array(f32, LAYERS + 1, CH, N),
        array(bf16, 3 * N, N),
        array(bf16, N, 3 * N),
        array(f32, N, N),
    ]
    inputs = [vel, cot, *params, jnp.asarray(poisson_tables(N))]
    inputs = [pltpu.with_memory_space_constraint(x, pltpu.HBM) for x in inputs]
    return pl.pallas_call(
        prepare_kernel,
        in_specs=[SMEM] + [pl.BlockSpec(memory_space=pltpu.HBM)] * len(inputs),
        out_specs=[VMEM] * len(out),
        out_shape=out,
        scratch_shapes=[pltpu.VMEM(x.shape, x.dtype) for x in inputs]
        + [pltpu.SemaphoreType.DMA((len(inputs),))],
        compiler_params=PARAMS,
        cost_estimate=cost(10**9, 10**6),
        name="prepare",
    )(core, *inputs)


def run_forward(count, core, fields, w_first, w_hidden, bias):
    local_rows, mid = count + 2 * MARGIN, count + 2 * MID
    out = [array(f32, 4, count, N), array(f32, 2, local_rows, N), array(f32, mid * CH, N)]
    out += feature_arrays(count) + slope_arrays(count)
    return call(
        functools.partial(forward_kernel, count),
        "forward_first",
        4 * 10**9,
        [core],
        [*fields, w_first, w_hidden, bias],
        out,
        [field(local_rows, 4), field(local_rows, 4), field(mid, 4)],
    )


def run_middle(count, core, lengths, gathered, vel, tables, w_first, w_hidden, bias, b_first, b_hidden):
    local_rows, mid = count + 2 * MARGIN, count + 2 * MID
    out = [array(f32, 4, count, N), array(f32, 2, local_rows, N), array(bf16, mid * CH, N)]
    out += feature_arrays(count) + slope_arrays(count)
    scratch = [field(local_rows, 4), field(local_rows, 4), field(mid * CH), field(mid * CH)]
    scratch += [field(mid, 4), field(mid, 4), field(mid, 2, 4), field(count, 2)]
    scratch += [pltpu.VMEM(x.shape, x.dtype) for x in slope_arrays(count)]
    return call(
        functools.partial(middle_kernel, count, len(gathered)),
        "both_last",
        8 * 10**9,
        [core, lengths],
        [*gathered, vel, *tables, w_first, w_hidden, bias, b_first, b_hidden],
        out,
        scratch,
    )


def run_weights(count, ext, graw, feats, grads):
    return call(
        functools.partial(weights_kernel, count),
        "weights_last",
        3 * 10**9,
        [],
        [ext, graw, *feats, *grads],
        array(f32, 30 * CH, N),
        [field(count + 2 * MARGIN, 4)] * 2,
    )


def run_backward(count, core, lengths, gathered, vel, tables, b_hidden, previous, feats, slopes):
    local_rows, mid = count + 2 * MARGIN, count + 2 * MID
    out = [
        array(f32, 2, local_rows, N),
        array(bf16, 30 * CH, N),
        array(bf16, (count + 2) * CH, N),
    ]
    scratch = [field(local_rows, 4), field(local_rows, 4), field(mid * CH)]
    scratch += [pltpu.VMEM((mid * CH, N), bf16), field(mid, 4)]
    scratch += [pltpu.VMEM(x.shape, x.dtype) for x in slope_arrays(count)[1:]]
    return call(
        functools.partial(backward_kernel, count, len(gathered)),
        "backward_first",
        8 * 10**9,
        [core, lengths],
        [*gathered, vel, *tables, b_hidden, previous, *feats, *slopes],
        out,
        scratch,
    )


def run_finish(count, core, lengths, gathered, vel, now, gstar, raw, grad_first, tables, b_first):
    local_rows, mid = count + 2 * MARGIN, count + 2 * MID
    return call(
        functools.partial(finish_kernel, count, len(gathered)),
        "finish",
        10**9,
        [core, lengths],
        [*gathered, vel, now, gstar, raw, grad_first, *tables, b_first],
        array(f32, 4, count, N),
        [field(local_rows, 4), field(local_rows, 4), field(mid, 4), field(mid, 4), field(mid, 2, 4), field(count, 2)],
    )


def run_unpack(core, mine, other):
    return pl.pallas_call(
        unpack_kernel,
        in_specs=[SMEM] + [VMEM] * 2,
        out_specs=[VMEM] * 6,
        out_shape=[
            array(f32, 9, 2, CH),
            array(f32, CH),
            array(f32, LAYERS - 1, 9, CH, CH),
            array(f32, LAYERS - 1, CH),
            array(f32, 9, CH, CH),
            array(f32, CH),
        ],
        compiler_params=PARAMS,
        cost_estimate=cost(10**7, 2 * 10**6),
        name="unpack",
    )(core, mine, other)


def swap(x, axis, offset):
    count = lax.axis_size(axis)
    return lax.ppermute(x, axis, [(i, i ^ offset) for i in range(count)])


def from_group(x, ahead):
    count = lax.axis_size("strip")
    return lax.ppermute(x, "strip", [(i, (i - 2 * ahead) % count) for i in range(count)])


def gather_groups(x):
    return [x] + [from_group(x, k) for k in range(1, lax.axis_size("strip") // 2)]


def margins(velocity, partner, core):
    count = lax.axis_size("strip")
    if velocity.shape[2] < MARGIN:
        upper = core[0] == 0
        pair = jnp.where(
            upper,
            jnp.concatenate([velocity[0], partner[0]], axis=1),
            jnp.concatenate([partner[1], velocity[1]], axis=1),
        )
        above, below = from_group(pair[:, -MARGIN:], -1), from_group(pair[:, :MARGIN], 1)
        return jnp.stack([above, below]), jnp.stack([below, above])
    cross = [(i, (i - 1) % count if i % 2 == 0 else (i + 1) % count) for i in range(count)]
    same = [(i, (i - 2) % count if i % 2 == 0 else (i + 2) % count) for i in range(count)]
    return lax.ppermute(velocity, "strip", cross), lax.ppermute(velocity, "strip", same)


def sum_everywhere(x, core):
    t = lax.axis_index("traj")
    parts = lax.axis_size("traj")
    groups = lax.axis_size("strip") // 2
    pick = lambda y, i: lax.dynamic_index_in_dim(y, i, 0, False)
    other = swap(x, "strip", 1)
    x = pick(x.reshape(2, -1, N), core).astype(f32) + pick(other.reshape(2, -1, N), core).astype(f32)
    x = x.astype(bf16).reshape(parts, -1, N)
    total = pick(x, t).astype(f32)
    for k in range(1, parts):
        total = total + swap(pick(x, t ^ k), "traj", k).astype(f32)
    x = total.astype(bf16)
    total = x.astype(f32)
    for k in range(1, groups):
        total = total + swap(x, "strip", 2 * k).astype(f32)
    x = total.astype(bf16)
    whole = jnp.zeros((parts,) + x.shape, bf16)
    for k in range(parts):
        block = x if k == 0 else swap(x, "traj", k)
        whole = lax.dynamic_update_slice(whole, block[None], (t ^ k, 0, 0))
    x = whole.reshape(-1, N)
    return x, swap(x, "strip", 1)


def per_device(
    velocity, lengths, cotangent, first_kernel, first_bias, middle_kernels, middle_biases, last_kernel, last_bias
):
    rc = velocity.shape[2]
    count = 2 * rc
    index = lax.axis_index("strip") & 1
    core = index[None]
    pick = lambda y, i: lax.dynamic_index_in_dim(y, i, 0, False)

    partner = swap(velocity, "strip", 1)
    cross, same = margins(velocity, partner, core)
    cot_partner = swap(cotangent, "strip", 1)
    first_kernel = first_kernel.transpose(0, 2, 1)
    params = (first_kernel, first_bias, middle_kernels, middle_biases, last_kernel, last_bias)
    own, w_first, w_hidden, b_first, b_hidden, bias, *tables = run_prepare(core, velocity, cotangent, params)

    fields = (own, partner, cross, same, cot_partner)
    block, vel, raw, *kept = run_forward(count, core, fields, w_first, w_hidden, bias)
    feats, slopes = kept[:LAYERS], kept[LAYERS:]
    gathered = gather_groups(block)
    back, now, graw, *kept = run_middle(
        count, core, lengths, gathered, vel, tables, w_first, w_hidden, bias, b_first, b_hidden
    )
    gathered = gather_groups(back)
    buffer = run_weights(count, now, graw, kept[:LAYERS], kept[LAYERS:])
    gstar, buffer, grad_first = run_backward(
        count, core, lengths, gathered, vel, tables, b_hidden, buffer, feats, slopes
    )
    out = run_finish(count, core, lengths, gathered, vel, now, gstar, raw, grad_first, tables, b_first)

    strips = out.reshape(4, 2, rc, N).transpose(1, 0, 2, 3)
    mine, other = pick(strips, index)[None], swap(pick(strips, 1 - index), "strip", 1)[None]
    out = jnp.where(
        index == 0, jnp.concatenate([mine, other], axis=0), jnp.concatenate([other, mine], axis=0)
    )
    mine, other = sum_everywhere(buffer, index)
    first, *rest = run_unpack(core, mine, other)
    return (out[:, :2], out[:, 2:], first.transpose(0, 2, 1), *rest)


def solution(mesh):
    band = P("traj", None, "strip", None)
    return jax.shard_map(
        per_device,
        mesh=mesh,
        in_specs=(band, P("traj"), band) + (P(),) * 6,
        out_specs=(band, band) + (P(),) * 6,
        check_vma=False,
    )
```

profile of v0, /device:TPU:0, one launch (start us, length us, event | category | flops | bytes accessed | tf_op | source)
XLA Modules:
  0.0 106.0 jit_solution(17580795465942359476)
XLA Ops:
  1.2 4.7 %collective-permute-start.1 = (f32[2,2,16,128]{3,2,1,0:T(8,128)}, f32[2,2,16,128]{3,2,1,0:T(8,128)S(1)}, u32[]{:S(2)}, u32[]{:S(2)}) collective-permute-start(f32[2,2,16,128]{3,2,1,0:T(8,128)} %refs_0_.1), channel_id=1, source_target_pairs={{0,7},{1,2},{2,1},{3,4},{4,3},{5,6},{6,5},{7,0},{8,15},{9,10},{10,... | collective-permute-start | bytes 98312 | tf_op jit(solution)/shard_map/ppermute | solution.py:768
  6.3 2.4 %prepare.1 = (f32[2,2,16,128]{3,2,1,0:T(8,128)S(1)}, bf16[384,16]{1,0:T(8,128)(2,1)S(1)}, bf16[6,384,256]{2,1,0:T(8,128)(2,1)S(1)}, bf16[16,256]{1,0:T(8,128)(2,...) custom-call(s32[1]{0:T(128)} %bitcast.core, ...), custom_call_target="tpu_custom_call" | custom-call | flops 1000000000 | bytes 1000000 | tf_op jit(solution)/shard_map/prepare/pallas_call | solution.py:630
  8.7 1.3 %collective-permute-done.2.same = f32[2,2,16,128]{3,2,1,0:T(8,128)S(1)} collective-permute-done((f32[2,2,16,128]{3,2,1,0:T(8,128)}, f32[2,2,16,128]{3,2,1,0:T(8,128)S(1)}, u32[]{:S(2)}, u32[]{:S(2)}) %collective-permute-start.2) | collective-permute-done | bytes 32800 | tf_op jit(solution)/shard_map/ppermute | solution.py:768
  10.0 8.8 %forward_first.1 = (f32[4,32,128]{2,1,0:T(8,128)S(1)}, f32[2,64,128]{2,1,0:T(8,128)S(1)}, f32[3072,128]{1,0:T(8,128)S(1)}, bf16[3456,128]{1,0:T(8,128)(2,1)S(1)}...) custom-call(s32[1]{0:T(128)} %bitcast.core, ...), custom_call_target="tpu_custom_call" | custom-call | flops 4000000000 | bytes 1000000 | tf_op jit(solution)/shard_map/forward_first/pallas_call | solution.py:603
  18.8 2.3 %collective-permute-start.4 = (f32[4,32,128]{2,1,0:T(8,128)S(1)}, f32[4,32,128]{2,1,0:T(8,128)S(1)}, u32[]{:S(2)}, u32[]{:S(2)}) collective-permute-start(f32[4,32,128]{2,1,0:T(8,128)S(1)} %get-tuple-element.60.refs_0_), channel_id=1, source_target_pairs={{0,6},{1,7},{2,0},{3,1},{4,2},{5,3},{6,4},{7,5},{8,14},{9,15},{10,... | collective-permute-start | bytes 196616 | tf_op jit(solution)/shard_map/ppermute | solution.py:748
  21.9 1.4 %collective-permute-done.4.refs_1_ = f32[4,32,128]{2,1,0:T(8,128)S(1)} collective-permute-done((f32[4,32,128]{2,1,0:T(8,128)S(1)}, f32[4,32,128]{2,1,0:T(8,128)S(1)}, u32[]{:S(2)}, u32[]{:S(2)}) %collective-permute-start.4) | collective-permute-done | bytes 65568 | tf_op jit(solution)/shard_map/ppermute | solution.py:748
  23.4 4.2 %collective-permute-done.5.refs_2_ = f32[4,32,128]{2,1,0:T(8,128)S(1)} collective-permute-done((f32[4,32,128]{2,1,0:T(8,128)S(1)}, f32[4,32,128]{2,1,0:T(8,128)S(1)}, u32[]{:S(2)}, u32[]{:S(2)}) %collective-permute-start.5) | collective-permute-done | bytes 65568 | tf_op jit(solution)/shard_map/ppermute | solution.py:748
  27.6 29.2 %both_last.1 = (f32[4,32,128]{2,1,0:T(8,128)S(1)}, f32[2,64,128]{2,1,0:T(8,128)S(1)}, bf16[3072,128]{1,0:T(8,128)(2,1)S(1)}, bf16[3456,128]{1,0:T(8,128)(2,1)S(1...) custom-call(s32[1]{0:T(128)} %bitcast.core, ...), custom_call_target="tpu_custom_call" | custom-call | flops 8000000000 | bytes 1000000 | tf_op jit(solution)/shard_map/both_last/pallas_call | solution.py:603
  56.7 1.3 %collective-permute-start.7 = (f32[4,32,128]{2,1,0:T(8,128)S(1)}, f32[4,32,128]{2,1,0:T(8,128)S(1)}, u32[]{:S(2)}, u32[]{:S(2)}) collective-permute-start(f32[4,32,128]{2,1,0:T(8,128)S(1)} %get-tuple-element.67.refs_0_), channel_id=1, source_target_pairs={{0,6},{1,7},{2,0},{3,1},{4,2},{5,3},{6,4},{7,5},{8,14},{9,15},{10,... | collective-permute-start | bytes 196616 | tf_op jit(solution)/shard_map/ppermute | solution.py:748
  58.2 1.9 %collective-permute-start.9 = (f32[4,32,128]{2,1,0:T(8,128)S(1)}, f32[4,32,128]{2,1,0:T(8,128)S(1)}, u32[]{:S(2)}, u32[]{:S(2)}) collective-permute-start(f32[4,32,128]{2,1,0:T(8,128)S(1)} %get-tuple-element.67.refs_0_), channel_id=1, source_target_pairs={{0,2},{1,3},{2,4},{3,5},{4,6},{5,7},{6,0},{7,1},{8,10},{9,11},{10,... | collective-permute-start | bytes 196616 | tf_op jit(solution)/shard_map/ppermute | solution.py:748
  60.1 3.3 %weights_last.1.refs_9_ = f32[1920,128]{1,0:T(8,128)S(1)} custom-call(f32[2,64,128]{2,1,0:T(8,128)S(1)} %get-tuple-element.68.ext.refs_5_, bf16[3072,128]{1,0:T(8,128)(2,1)S(1)} %get-tuple-element.69.graw, bf16[3456,128]{1,0:T(8,128)(2,1)S(1)} %get-tuple-element.70.refs_0_, bf16[3328,128]{1,0:T(8,128)(2,1)S(1)} %get-tuple-element.71.refs_1_, ...), custom_call_target="tpu_custom_call" | custom-call | flops 3000000000 | bytes 1000000 | tf_op jit(solution)/shard_map/weights_last/pallas_call | solution.py:603
  63.4 1.3 %collective-permute-done.8.refs_2_ = f32[4,32,128]{2,1,0:T(8,128)S(1)} collective-permute-done((f32[4,32,128]{2,1,0:T(8,128)S(1)}, f32[4,32,128]{2,1,0:T(8,128)S(1)}, u32[]{:S(2)}, u32[]{:S(2)}) %collective-permute-start.8) | collective-permute-done | bytes 65568 | tf_op jit(solution)/shard_map/ppermute | solution.py:748
  64.8 10.1 %backward_first.1 = (f32[2,64,128]{2,1,0:T(8,128)S(1)}, bf16[1920,128]{1,0:T(8,128)(2,1)S(1)}, bf16[2176,128]{1,0:T(8,128)(2,1)S(1)}) custom-call(s32[1]{0:T(128)} %bitcast.core, s32[2]{0:T(128)S(1)} %copy-done, f32[4,32,128]{2,1,0:T(8,128)S(1)} %get-tuple-element.67.refs_0_, f32[4,32,128]{2,1,0:T(8,128)S(1)} %collective-permute-done.7.refs_1_, ...), custom_call_target="tpu_custom_call" | custom-call | flops 8000000000 | bytes 1000000 | tf_op jit(solution)/shard_map/backward_first/pallas_call | solution.py:603
  75.0 2.0 %collective-permute-done.11 = bf16[1920,128]{1,0:T(8,128)(2,1)} collective-permute-done((bf16[1920,128]{1,0:T(8,128)(2,1)S(1)}, bf16[1920,128]{1,0:T(8,128)(2,1)}, u32[]{:S(2)}, u32[]{:S(2)}) %collective-permute-start.11) | collective-permute-done | bytes 491552 | tf_op jit(solution)/shard_map/ppermute | solution.py:743
  78.7 1.6 %collective-permute-start.12 = (bf16[240,128]{1,0:T(8,128)(2,1)S(1)}, bf16[240,128]{1,0:T(8,128)(2,1)S(1)}, u32[]{:S(2)}, u32[]{:S(2)}) collective-permute-start(bf16[240,128]{1,0:T(8,128)(2,1)S(1)} %get-tuple-element.106), channel_id=1, source_target_pairs={{0,8},{8,0},{16,24},{24,16},{1,9},{9,1},{17,25},{25,17},{2,10},{10... | collective-permute-start | bytes 184328 | tf_op jit(solution)/shard_map/ppermute | solution.py:743
  80.3 1.8 %collective-permute-start.13 = (bf16[240,128]{1,0:T(8,128)(2,1)S(1)}, bf16[240,128]{1,0:T(8,128)(2,1)S(1)}, u32[]{:S(2)}, u32[]{:S(2)}) collective-permute-start(bf16[240,128]{1,0:T(8,128)(2,1)S(1)} %get-tuple-element.108), channel_id=1, source_target_pairs={{0,16},{8,24},{16,0},{24,8},{1,17},{9,25},{17,1},{25,9},{2,18},{10... | collective-permute-start | bytes 184328 | tf_op jit(solution)/shard_map/ppermute | solution.py:743
  83.0 1.7 %collective-permute-done.13 = bf16[240,128]{1,0:T(8,128)(2,1)S(1)} collective-permute-done((bf16[240,128]{1,0:T(8,128)(2,1)S(1)}, bf16[240,128]{1,0:T(8,128)(2,1)S(1)}, u32[]{:S(2)}, u32[]{:S(2)}) %collective-permute-start.13) | collective-permute-done | bytes 61472 | tf_op jit(solution)/shard_map/ppermute | solution.py:743
  84.7 2.4 %collective-permute-done.14 = bf16[240,128]{1,0:T(8,128)(2,1)S(1)} collective-permute-done((bf16[240,128]{1,0:T(8,128)(2,1)S(1)}, bf16[240,128]{1,0:T(8,128)(2,1)S(1)}, u32[]{:S(2)}, u32[]{:S(2)}) %collective-permute-start.14) | collective-permute-done | bytes 61472 | tf_op jit(solution)/shard_map/ppermute | solution.py:743
  88.2 2.1 %collective-permute-start.16 = (bf16[240,128]{1,0:T(8,128)(2,1)S(1)}, bf16[240,128]{1,0:T(8,128)(2,1)S(1)}, u32[]{:S(2)}, u32[]{:S(2)}) collective-permute-start(bf16[240,128]{1,0:T(8,128)(2,1)S(1)} %fusion.2), channel_id=1, source_target_pairs={{0,4},{1,5},{2,6},{3,7},{4,0},{5,1},{6,2},{7,3},{8,12},{9,13},{10,... | collective-permute-start | bytes 184328 | tf_op jit(solution)/shard_map/ppermute | solution.py:743
  90.3 2.1 %collective-permute-start.17 = (bf16[240,128]{1,0:T(8,128)(2,1)S(1)}, bf16[240,128]{1,0:T(8,128)(2,1)S(1)}, u32[]{:S(2)}, u32[]{:S(2)}) collective-permute-start(bf16[240,128]{1,0:T(8,128)(2,1)S(1)} %fusion.2), channel_id=1, source_target_pairs={{0,6},{1,7},{2,4},{3,5},{4,2},{5,3},{6,0},{7,1},{8,14},{9,15},{10,... | collective-permute-start | bytes 184328 | tf_op jit(solution)/shard_map/ppermute | solution.py:743
  92.5 2.9 %finish.1 = f32[4,32,128]{2,1,0:T(8,128)S(1)} custom-call(s32[1]{0:T(128)} %bitcast.core, s32[2]{0:T(128)S(1)} %copy-done, f32[4,32,128]{2,1,0:T(8,128)S(1)} %get-tuple-element.67.refs_0_, f32[4,32,128]{2,1,0:T(8,128)S(1)} %collective-permute-done.7.refs_1_, f32[4,32,128]{2,1,0:T(8,128)S(1)} %collective-permute-done.8.refs_2_, ...), custom_call_target="tpu_custom_call" | custom-call | flops 1000000000 | bytes 1000000 | tf_op jit(solution)/shard_map/finish/pallas_call | solution.py:603
  97.6 2.4 %collective-permute-start.20 = (bf16[240,128]{1,0:T(8,128)(2,1)S(1)}, bf16[240,128]{1,0:T(8,128)(2,1)S(1)}, u32[]{:S(2)}, u32[]{:S(2)}) collective-permute-start(bf16[240,128]{1,0:T(8,128)(2,1)S(1)} %get-tuple-element.105), channel_id=1, source_target_pairs={{0,24},{8,16},{16,8},{24,0},{1,25},{9,17},{17,9},{25,1},{2,26},{10... | collective-permute-start | bytes 184328 | tf_op jit(solution)/shard_map/ppermute | solution.py:743
  100.7 1.6 %collective-permute-done.19 = bf16[240,128]{1,0:T(8,128)(2,1)S(1)} collective-permute-done((bf16[240,128]{1,0:T(8,128)(2,1)S(1)}, bf16[240,128]{1,0:T(8,128)(2,1)S(1)}, u32[]{:S(2)}, u32[]{:S(2)}) %collective-permute-start.19) | collective-permute-done | bytes 61472 | tf_op jit(solution)/shard_map/ppermute | solution.py:743
  104.4 1.4 %unpack.1 = (f32[9,2,64]{2,1,0:T(2,128)}, f32[64]{0:T(128)}, f32[5,9,64,64]{3,2,1,0:T(8,128)}, f32[5,64]{1,0:T(8,128)}, f32[9,64,64]{2,1,0:T(8,128)}, /*index=5*/f32[64]{0:T(128)}) custom-call(s32[1]{0:T(128)} %bitcast.core, bf16[960,128]{1,0:T(8,128)(2,1)S(1)} %bitcast.31, bf16[960,128]{1,0:T(8,128)(2,1)S(1)} %collective-permute-done.21.other), custom_call_target="tpu_custom_call" | custom-call | flops 10000000 | bytes 2000000 | tf_op jit(solution)/shard_map/unpack/pallas_call | solution.py:723
  (42 shorter events, 10.7 us)
Async XLA Ops:
  0.6 8.1 %collective-permute-start = (f32[2,2,16,128]{3,2,1,0:T(8,128)}, f32[2,2,16,128]{3,2,1,0:T(8,128)S(1)}, u32[]{:S(2)}, u32[]{:S(2)}) collective-permute-start(f32[2,2,16,128]{3,2,1,0:T(8,128)} %refs_0_.1), channel_id=1, source_target_pairs={{0,1},{1,0},{2,3},{3,2},{4,5},{5,4},{6,7},{7,6},{8,9},{9,8},{10,11... | collective-permute-start | bytes 98312 | tf_op jit(solution)/shard_map/ppermute | solution.py:743
  1.2 7.5 %collective-permute-start.1 = (f32[2,2,16,128]{3,2,1,0:T(8,128)}, f32[2,2,16,128]{3,2,1,0:T(8,128)S(1)}, u32[]{:S(2)}, u32[]{:S(2)}) collective-permute-start(f32[2,2,16,128]{3,2,1,0:T(8,128)} %refs_0_.1), channel_id=1, source_target_pairs={{0,7},{1,2},{2,1},{3,4},{4,3},{5,6},{6,5},{7,0},{8,15},{9,10},{10,... | collective-permute-start | bytes 98312 | tf_op jit(solution)/shard_map/ppermute | solution.py:768
  5.9 4.1 %collective-permute-start.2 = (f32[2,2,16,128]{3,2,1,0:T(8,128)}, f32[2,2,16,128]{3,2,1,0:T(8,128)S(1)}, u32[]{:S(2)}, u32[]{:S(2)}) collective-permute-start(f32[2,2,16,128]{3,2,1,0:T(8,128)} %refs_0_.1), channel_id=1, source_target_pairs={{0,6},{1,3},{2,0},{3,5},{4,2},{5,7},{6,4},{7,1},{8,14},{9,11},{10,... | collective-permute-start | bytes 98312 | tf_op jit(solution)/shard_map/ppermute | solution.py:768
  6.3 3.7 %collective-permute-start.3 = (f32[2,2,16,128]{3,2,1,0:T(8,128)}, f32[2,2,16,128]{3,2,1,0:T(8,128)S(1)}, u32[]{:S(2)}, u32[]{:S(2)}) collective-permute-start(f32[2,2,16,128]{3,2,1,0:T(8,128)} %refs_1_.1), channel_id=1, source_target_pairs={{0,1},{1,0},{2,3},{3,2},{4,5},{5,4},{6,7},{7,6},{8,9},{9,8},{10,11... | collective-permute-start | bytes 98312 | tf_op jit(solution)/shard_map/ppermute | solution.py:743
  10.0 17.6 %copy-start = (s32[2]{0:T(128)S(1)}, s32[2]{0:T(128)}, u32[]{:S(2)}) copy-start(s32[2]{0:T(128)} %lengths.5) | copy-start | bytes 28
  18.8 4.6 %collective-permute-start.4 = (f32[4,32,128]{2,1,0:T(8,128)S(1)}, f32[4,32,128]{2,1,0:T(8,128)S(1)}, u32[]{:S(2)}, u32[]{:S(2)}) collective-permute-start(f32[4,32,128]{2,1,0:T(8,128)S(1)} %get-tuple-element.60.refs_0_), channel_id=1, source_target_pairs={{0,6},{1,7},{2,0},{3,1},{4,2},{5,3},{6,4},{7,5},{8,14},{9,15},{10,... | collective-permute-start | bytes 196616 | tf_op jit(solution)/shard_map/ppermute | solution.py:748
  21.1 6.5 %collective-permute-start.5 = (f32[4,32,128]{2,1,0:T(8,128)S(1)}, f32[4,32,128]{2,1,0:T(8,128)S(1)}, u32[]{:S(2)}, u32[]{:S(2)}) collective-permute-start(f32[4,32,128]{2,1,0:T(8,128)S(1)} %get-tuple-element.60.refs_0_), channel_id=1, source_target_pairs={{0,4},{1,5},{2,6},{3,7},{4,0},{5,1},{6,2},{7,3},{8,12},{9,13},{10,... | collective-permute-start | bytes 196616 | tf_op jit(solution)/shard_map/ppermute | solution.py:748
  21.1 6.5 %collective-permute-start.6 = (f32[4,32,128]{2,1,0:T(8,128)S(1)}, f32[4,32,128]{2,1,0:T(8,128)S(1)}, u32[]{:S(2)}, u32[]{:S(2)}) collective-permute-start(f32[4,32,128]{2,1,0:T(8,128)S(1)} %get-tuple-element.60.refs_0_), channel_id=1, source_target_pairs={{0,2},{1,3},{2,4},{3,5},{4,6},{5,7},{6,0},{7,1},{8,10},{9,11},{10,... | collective-permute-start | bytes 196616 | tf_op jit(solution)/shard_map/ppermute | solution.py:748
  56.7 6.7 %collective-permute-start.7 = (f32[4,32,128]{2,1,0:T(8,128)S(1)}, f32[4,32,128]{2,1,0:T(8,128)S(1)}, u32[]{:S(2)}, u32[]{:S(2)}) collective-permute-start(f32[4,32,128]{2,1,0:T(8,128)S(1)} %get-tuple-element.67.refs_0_), channel_id=1, source_target_pairs={{0,6},{1,7},{2,0},{3,1},{4,2},{5,3},{6,4},{7,5},{8,14},{9,15},{10,... | collective-permute-start | bytes 196616 | tf_op jit(solution)/shard_map/ppermute | solution.py:748
  58.0 6.7 %collective-permute-start.8 = (f32[4,32,128]{2,1,0:T(8,128)S(1)}, f32[4,32,128]{2,1,0:T(8,128)S(1)}, u32[]{:S(2)}, u32[]{:S(2)}) collective-permute-start(f32[4,32,128]{2,1,0:T(8,128)S(1)} %get-tuple-element.67.refs_0_), channel_id=1, source_target_pairs={{0,4},{1,5},{2,6},{3,7},{4,0},{5,1},{6,2},{7,3},{8,12},{9,13},{10,... | collective-permute-start | bytes 196616 | tf_op jit(solution)/shard_map/ppermute | solution.py:748
  58.2 6.6 %collective-permute-start.9 = (f32[4,32,128]{2,1,0:T(8,128)S(1)}, f32[4,32,128]{2,1,0:T(8,128)S(1)}, u32[]{:S(2)}, u32[]{:S(2)}) collective-permute-start(f32[4,32,128]{2,1,0:T(8,128)S(1)} %get-tuple-element.67.refs_0_), channel_id=1, source_target_pairs={{0,2},{1,3},{2,4},{3,5},{4,6},{5,7},{6,0},{7,1},{8,10},{9,11},{10,... | collective-permute-start | bytes 196616 | tf_op jit(solution)/shard_map/ppermute | solution.py:748
  74.9 2.1 %collective-permute-start.11 = (bf16[1920,128]{1,0:T(8,128)(2,1)S(1)}, bf16[1920,128]{1,0:T(8,128)(2,1)}, u32[]{:S(2)}, u32[]{:S(2)}) collective-permute-start(bf16[1920,128]{1,0:T(8,128)(2,1)S(1)} %get-tuple-element.97), channel_id=1, source_target_pairs={{0,1},{1,0},{2,3},{3,2},{4,5},{5,4},{6,7},{7,6},{8,9},{9,8},{10,11... | collective-permute-start | bytes 1474568 | tf_op jit(solution)/shard_map/ppermute | solution.py:743
  78.0 0.7 copy-start.1
  78.7 4.3 %collective-permute-start.12 = (bf16[240,128]{1,0:T(8,128)(2,1)S(1)}, bf16[240,128]{1,0:T(8,128)(2,1)S(1)}, u32[]{:S(2)}, u32[]{:S(2)}) collective-permute-start(bf16[240,128]{1,0:T(8,128)(2,1)S(1)} %get-tuple-element.106), channel_id=1, source_target_pairs={{0,8},{8,0},{16,24},{24,16},{1,9},{9,1},{17,25},{25,17},{2,10},{10... | collective-permute-start | bytes 184328 | tf_op jit(solution)/shard_map/ppermute | solution.py:743
  80.3 4.4 %collective-permute-start.13 = (bf16[240,128]{1,0:T(8,128)(2,1)S(1)}, bf16[240,128]{1,0:T(8,128)(2,1)S(1)}, u32[]{:S(2)}, u32[]{:S(2)}) collective-permute-start(bf16[240,128]{1,0:T(8,128)(2,1)S(1)} %get-tuple-element.108), channel_id=1, source_target_pairs={{0,16},{8,24},{16,0},{24,8},{1,17},{9,25},{17,1},{25,9},{2,18},{10... | collective-permute-start | bytes 184328 | tf_op jit(solution)/shard_map/ppermute | solution.py:743
  82.0 5.1 %collective-permute-start.14 = (bf16[240,128]{1,0:T(8,128)(2,1)S(1)}, bf16[240,128]{1,0:T(8,128)(2,1)S(1)}, u32[]{:S(2)}, u32[]{:S(2)}) collective-permute-start(bf16[240,128]{1,0:T(8,128)(2,1)S(1)} %get-tuple-element.107), channel_id=1, source_target_pairs={{0,24},{8,16},{16,8},{24,0},{1,25},{9,17},{17,9},{25,1},{2,26},{10... | collective-permute-start | bytes 184328 | tf_op jit(solution)/shard_map/ppermute | solution.py:743
  88.0 7.4 %collective-permute-start.15 = (bf16[240,128]{1,0:T(8,128)(2,1)S(1)}, bf16[240,128]{1,0:T(8,128)(2,1)S(1)}, u32[]{:S(2)}, u32[]{:S(2)}) collective-permute-start(bf16[240,128]{1,0:T(8,128)(2,1)S(1)} %fusion.2), channel_id=1, source_target_pairs={{0,2},{1,3},{2,0},{3,1},{4,6},{5,7},{6,4},{7,5},{8,10},{9,11},{10,... | collective-permute-start | bytes 184328 | tf_op jit(solution)/shard_map/ppermute | solution.py:743
  88.2 7.2 %collective-permute-start.16 = (bf16[240,128]{1,0:T(8,128)(2,1)S(1)}, bf16[240,128]{1,0:T(8,128)(2,1)S(1)}, u32[]{:S(2)}, u32[]{:S(2)}) collective-permute-start(bf16[240,128]{1,0:T(8,128)(2,1)S(1)} %fusion.2), channel_id=1, source_target_pairs={{0,4},{1,5},{2,6},{3,7},{4,0},{5,1},{6,2},{7,3},{8,12},{9,13},{10,... | collective-permute-start | bytes 184328 | tf_op jit(solution)/shard_map/ppermute | solution.py:743
  90.3 6.0 %collective-permute-start.17 = (bf16[240,128]{1,0:T(8,128)(2,1)S(1)}, bf16[240,128]{1,0:T(8,128)(2,1)S(1)}, u32[]{:S(2)}, u32[]{:S(2)}) collective-permute-start(bf16[240,128]{1,0:T(8,128)(2,1)S(1)} %fusion.2), channel_id=1, source_target_pairs={{0,6},{1,7},{2,4},{3,5},{4,2},{5,3},{6,0},{7,1},{8,14},{9,15},{10,... | collective-permute-start | bytes 184328 | tf_op jit(solution)/shard_map/ppermute | solution.py:743
  96.4 4.3 %collective-permute-start.18 = (bf16[240,128]{1,0:T(8,128)(2,1)S(1)}, bf16[240,128]{1,0:T(8,128)(2,1)S(1)}, u32[]{:S(2)}, u32[]{:S(2)}) collective-permute-start(bf16[240,128]{1,0:T(8,128)(2,1)S(1)} %get-tuple-element.105), channel_id=1, source_target_pairs={{0,8},{8,0},{16,24},{24,16},{1,9},{9,1},{17,25},{25,17},{2,10},{10... | collective-permute-start | bytes 184328 | tf_op jit(solution)/shard_map/ppermute | solution.py:743
  97.0 5.8 %collective-permute-start.10 = (f32[4,16,128]{2,1,0:T(8,128)S(1)}, f32[4,16,128]{2,1,0:T(8,128)S(1)}, u32[]{:S(2)}, u32[]{:S(2)}) collective-permute-start(f32[4,16,128]{2,1,0:T(8,128)S(1)} %get-tuple-element.112), channel_id=1, source_target_pairs={{0,1},{1,0},{2,3},{3,2},{4,5},{5,4},{6,7},{7,6},{8,9},{9,8},{10,11... | collective-permute-start | bytes 98312 | tf_op jit(solution)/shard_map/ppermute | solution.py:743
  97.0 5.3 %collective-permute-start.19 = (bf16[240,128]{1,0:T(8,128)(2,1)S(1)}, bf16[240,128]{1,0:T(8,128)(2,1)S(1)}, u32[]{:S(2)}, u32[]{:S(2)}) collective-permute-start(bf16[240,128]{1,0:T(8,128)(2,1)S(1)} %get-tuple-element.105), channel_id=1, source_target_pairs={{0,16},{8,24},{16,0},{24,8},{1,17},{9,25},{17,1},{25,9},{2,18},{10... | collective-permute-start | bytes 184328 | tf_op jit(solution)/shard_map/ppermute | solution.py:743
  97.6 5.1 %collective-permute-start.20 = (bf16[240,128]{1,0:T(8,128)(2,1)S(1)}, bf16[240,128]{1,0:T(8,128)(2,1)S(1)}, u32[]{:S(2)}, u32[]{:S(2)}) collective-permute-start(bf16[240,128]{1,0:T(8,128)(2,1)S(1)} %get-tuple-element.105), channel_id=1, source_target_pairs={{0,24},{8,16},{16,8},{24,0},{1,25},{9,17},{17,9},{25,1},{2,26},{10... | collective-permute-start | bytes 184328 | tf_op jit(solution)/shard_map/ppermute | solution.py:743
  102.8 1.6 %collective-permute-start.21 = (bf16[960,128]{1,0:T(8,128)(2,1)S(1)}, bf16[960,128]{1,0:T(8,128)(2,1)S(1)}, u32[]{:S(2)}, u32[]{:S(2)}) collective-permute-start(bf16[960,128]{1,0:T(8,128)(2,1)S(1)} %bitcast.30), channel_id=1, source_target_pairs={{0,1},{1,0},{2,3},{3,2},{4,5},{5,4},{6,7},{7,6},{8,9},{9,8},{10,11... | collective-permute-start | bytes 737288 | tf_op jit(solution)/shard_map/ppermute | solution.py:743
where the time goes:
time: 108 us; the launch traced here: 106 us
  Pallas kernels  58.1 us (54%)
  starting transfers between devices  24.2 us (22%)
  waiting for transfers between devices  19.3 us (18%)
  other arithmetic  1.95 us (2%)
  local copies, waits for them, and re-layouts  1.41 us (1%)
    pallas_call x5, Pallas kernels, call(): pl.pallas_call(kernel, in_specs=[SMEM] * len(smem) + [VMEM] * len(inputs)...  54.3 us
    ppermute x14, starting transfers between devices, swap(): return lax.ppermute(x, axis, [(i, i ^ offset) for i in range(count)])  12.5 us
    ppermute x14, waiting for transfers between devices, swap(): return lax.ppermute(x, axis, [(i, i ^ offset) for i in range(count)])  11 us
    ppermute x6, waiting for transfers between devices, from_group(): lax.ppermute(x, 'strip', [(i, (i - 2 * ahead) % count) for i in range(cou...  6.96 us
    ppermute x6, starting transfers between devices, from_group(): lax.ppermute(x, 'strip', [(i, (i - 2 * ahead) % count) for i in range(cou...  6.55 us
    ppermute x1, starting transfers between devices, margins(): lax.ppermute(velocity, 'strip', cross)  4.71 us
    pallas_call x1, Pallas kernels, run_prepare(): pl.pallas_call(prepare_kernel, in_specs=[SMEM] + [pl.BlockSpec(memory_spa...  2.36 us
  transfers between devices with their start and end apart: 22, of which 13 were waited for; matrix products, arithmetic and copies ran while one was open for 1% of the time, Pallas kernels for 8%

commit v1 on v0

v1 whole, which is shorter than its diff:
```python
import functools
import math

import jax
import jax.numpy as jnp
import numpy as np
from jax import lax
from jax.experimental import pallas as pl
from jax.experimental.pallas import tpu as pltpu
from jax.sharding import PartitionSpec as P

STEPS = 2
DT = 0.25
MARGIN = 16
MID = 8
RAW = 2
CH = 64
LAYERS = 6
N = 128
BUFFER = 30 * CH
bf16 = jnp.bfloat16
f32 = jnp.float32
NT = (((1,), (1,)), ((), ()))
VMEM_BYTES = 14 * 2**20


def reach(layer):
    return 12 - layer


def place(start, size):
    return slice(start, start + size) if isinstance(start, int) else pl.ds(pl.multiple_of(start, CH), size)


def feature_rows(count, layer, r, rows=1):
    return place(((layer - 1) * (count + 24) + r + 12) * CH, rows * CH)


def gradient_rows(count, layer, r, rows=1):
    return place(((layer - 1) * (count + 16) + r + 8) * CH, rows * CH)


def lanes(x, s):
    return x if s == 0 else pltpu.roll(x, (-s) % x.shape[1], 1)


def rows(x, s):
    return x if s == 0 else pltpu.roll(x, (-s) % x.shape[0], 0)


def poisson_tables(length):
    k = np.arange(length)
    angle = 2.0 * math.pi * ((k[:, None] * k[None, :]) % length) / length
    table = (np.cos(angle) + np.sin(angle)) / math.sqrt(length)
    eigen = 2.0 - 2.0 * np.cos(2.0 * math.pi * k / length)
    total = eigen[:, None] + eigen[None, :]
    total[0, 0] = 1.0
    weight = 1.0 / total
    weight[0, 0] = 0.0
    return np.stack([table, weight]).astype(np.float32)


def split(x):
    high = x.astype(bf16)
    return high, (x - high.astype(f32)).astype(bf16)


def times_right(x, right):
    high, low = split(x)
    return jnp.dot(jnp.concatenate([high, low, high], axis=1), right[...], preferred_element_type=f32)


def times_left(x, left):
    high, low = split(x)
    return jnp.dot(left[...], jnp.concatenate([high, high, low], axis=0), preferred_element_type=f32)


def project(fields, right, left, weight):
    count = len(fields)
    source = [u - lanes(u, -1) + (v - rows(v, -1)) for u, v in fields]
    x = times_right(jnp.concatenate(source, axis=0), right)
    x = jnp.concatenate([x[i * N : (i + 1) * N] for i in range(count)], axis=1)
    x = times_left(x, left) * jnp.concatenate([weight[...]] * count, axis=1)
    x = times_left(x, left)
    x = jnp.concatenate([x[:, i * N : (i + 1) * N] for i in range(count)], axis=0)
    x = times_right(x, right)
    out = []
    for i, (u, v) in enumerate(fields):
        p = -x[i * N : (i + 1) * N]
        out.append((u - (lanes(p, 1) - p), v - (rows(p, 1) - p)))
    return out


def local(x, count):
    return jnp.concatenate([x[N - MARGIN :], x[: count + MARGIN]], axis=0)


def fold(o):
    third = o.shape[0] // 3
    return lanes(o[:third], -1) + o[third : 2 * third] + lanes(o[2 * third :], 1)


def fold_rounded(o):
    third = o.shape[0] // 3
    left, right = lanes(o[:third].astype(bf16), -1), lanes(o[2 * third :].astype(bf16), 1)
    return left.astype(f32) + o[third : 2 * third] + right.astype(f32)


def conv_rows(window, kernel, low, high, emit, between=lambda: None):
    starts = list(range(low, high, 2))
    for k in range(0, len(starts), 2):
        group = starts[k : k + 2]
        o = jnp.dot(
            kernel[...],
            jnp.concatenate([window(r) for r in group], axis=1),
            preferred_element_type=f32,
        )
        half = o.shape[0] // 2
        for i, r in enumerate(group):
            part = o[:, i * N : (i + 1) * N]
            emit(r, part[:half])
            emit(r + 1, part[half:])
        between()


def first_window(us, vs, r):
    a = r - 1 + MARGIN
    return jnp.concatenate(
        [us[1, a : a + 4, :], vs[1, a : a + 4, :], jnp.zeros((8, N), f32)], axis=0
    ).astype(bf16)


def feature_window(feats, count, layer):
    return lambda r: feats[feature_rows(count, layer, r - 1, 4), :]


def gradient_window(grads, count, layer):
    return lambda r: grads[gradient_rows(count, layer, r - 1, 4), :]


def gelu_value(z):
    c = math.sqrt(2.0 / math.pi)
    zz = z * z
    h = 0.5 + 0.5 * jnp.tanh(z * (c + (c * 0.044715) * zz))
    return z * h, h, zz


def gelu_slope(f, h, zz):
    c = math.sqrt(2.0 / math.pi)
    return h + (f - f * h) * (2.0 * c + (6.0 * c * 0.044715) * zz)


def spread_columns(u, v, us, vs):
    for j in range(4):
        us[j] = lanes(u, j - 1)
        vs[j] = lanes(v, j - 1)


def network_forward(count, us, vs, w_first, w_hidden, bias, feats, slopes, raw, raw_done):
    for m in range(1, LAYERS + 1):

        def emit(r, o, m=m):
            value, h, zz = gelu_value(fold(o) + bias[m - 1])
            feats[feature_rows(count, m, r), :] = value.astype(bf16)
            if -m <= r < count + m:
                slopes[gradient_rows(count, m, r), :] = gelu_slope(value, h, zz).astype(bf16)

        low, high = -reach(m), count + reach(m)
        if m == 1:
            conv_rows(functools.partial(first_window, us, vs), w_first, low, high, emit)
        else:
            conv_rows(feature_window(feats, count, m - 1), w_hidden.at[m - 2], low, high, emit)

    def emit_raw(r, o):
        raw[(r + MID) * CH : (r + MID + 1) * CH, :] = fold(o) + bias[LAYERS]
        raw_done(r)

    conv_rows(
        feature_window(feats, count, LAYERS), w_hidden.at[LAYERS - 1], -RAW, count + RAW, emit_raw
    )


TARGETS = ((0.0, -0.5), (-0.5, 0.0), (0.0, -0.5), (-0.5, 0.0))


def moments(values):
    cols = [values[j] + values[4 + j] + (values[8 + j] + values[12 + j]) for j in range(4)]
    lines = [values[4 * i] + values[4 * i + 1] + (values[4 * i + 2] + values[4 * i + 3]) for i in range(4)]
    mean = (cols[0] + cols[1] + (cols[2] + cols[3])) * (1.0 / 16.0)
    mx = (1.5 * (cols[3] - cols[0]) + 0.5 * (cols[2] - cols[1])) * (1.0 / 20.0)
    my = (1.5 * (lines[3] - lines[0]) + 0.5 * (lines[2] - lines[1])) * (1.0 / 20.0)
    return mean, mx, my


def less(values, mean, mx, my):
    by_col = [mean + mx * (j - 1.5) for j in range(4)]
    by_line = [my * (i - 1.5) for i in range(4)]
    return [values[p] - (by_col[p % 4] + by_line[p // 4]) for p in range(16)]


def total_of(terms):
    while len(terms) > 1:
        terms = [a + b for a, b in zip(terms[::2], terms[1::2])] + terms[len(terms) // 2 * 2 :]
    return terms[0]


def patches(src, q):
    a = MARGIN - MID + 8 * q
    return [src[p % 4, a + p // 4 - 1 : a + p // 4 + 7, :] for p in range(16)]


def raw_rows(raw, k, q):
    return [raw[pl.ds(8 * q * CH + k * 16 + p, 8, stride=CH), :] for p in range(16)]


def eight(q):
    return slice(8 * q, 8 * q + 8) if isinstance(q, int) else pl.ds(pl.multiple_of(8 * q, 8), 8)


def interpolate(q, sources, raw, interp):
    for which, src in enumerate(sources):
        patch = patches(src, q)
        mean, mx, my = moments(patch)
        clear = less(patch, mean, mx, my)
        for k in (2 * which, 2 * which + 1):
            tx, ty = TARGETS[k]
            value = total_of([a * b for a, b in zip(raw_rows(raw, k, q), clear)])
            interp[k, 8 * q : 8 * q + 8, :] = value + (mean + (tx * mx if tx else ty * my))


def raw_gradient(count, q, sources, ginterp, graw32, grads):
    at = slice(8 * q, 8 * q + 8)
    for which, src in enumerate(sources):
        patch = patches(src, q)
        clear = less(patch, *moments(patch))
        for k in (2 * which, 2 * which + 1):
            g = ginterp[k, at, :]
            for p in range(16):
                graw32[pl.ds(k * 16 + p, 8, stride=CH), :] = clear[p] * g
    grads[gradient_rows(count, LAYERS + 1, 8 * q - MID, 8), :] = graw32[...].astype(bf16)


def spread_back(q, which, raw, ginterp, lines):
    k = 2 * which
    at = eight(q)
    g, h = ginterp[k, at, :], ginterp[k + 1, at, :]
    values = [a * g + b * h for a, b in zip(raw_rows(raw, k, q), raw_rows(raw, k + 1, q))]
    mean, mx, my = moments(values)
    values = less(values, mean - (g + h) * (1.0 / 16.0), mx + h * (0.5 / 20.0), my + g * (0.5 / 20.0))
    for i in range(4):
        lines[which, i, at, :] = total_of([lanes(values[4 * i + j], 1 - j) for j in range(4)])


def carriers(u, v):
    return (
        0.5 * (u + lanes(u, 1)),
        0.5 * (v + lanes(v, 1)),
        0.5 * (u + rows(u, 1)),
        0.5 * (v + rows(v, 1)),
    )


def middle(x, count):
    return x[MARGIN - MID : MARGIN + MID + count]


def provisional(count, u, v, interp):
    flux = [middle(x, count) * interp[k] for k, x in enumerate(carriers(u, v))]
    u, v = middle(u, count), middle(v, count)
    su = u - DT * (flux[0] - lanes(flux[0], -1) + (flux[1] - rows(flux[1], -1)))
    sv = v - DT * (flux[2] - lanes(flux[2], -1) + (flux[3] - rows(flux[3], -1)))
    return su[MID : MID + count], sv[MID : MID + count]


def flux_gradients(count, gu, gv):
    return [
        middle(x, count) * (-DT)
        for x in (gu - lanes(gu, 1), gu - rows(gu, 1), gv - lanes(gv, 1), gv - rows(gv, 1))
    ]


def interp_gradients(count, gu, gv, u, v, ginterp):
    for k, (g, x) in enumerate(zip(flux_gradients(count, gu, gv), carriers(u, v))):
        ginterp[k] = g * middle(x, count)


def velocity_gradients(count, gu, gv, interp, lines):
    half = [0.5 * g * interp[k] for k, g in enumerate(flux_gradients(count, gu, gv))]
    out = []
    for which, g in enumerate((gu, gv)):
        along, across = half[which], half[2 + which]
        x = middle(g, count) + (along + lanes(along, -1)) + (across + rows(across, -1))
        x = x[MID : MID + count]
        for i in range(4):
            x = x + lines[which, i, MID + 1 - i : MID + 1 - i + count, :]
        out.append(x)
    return out


def network_backward(count, w_hidden, slopes, grads, between=lambda: None):
    for m in range(LAYERS, 0, -1):

        def emit(r, o, m=m):
            at = gradient_rows(count, m, r)
            grads[at, :] = (fold_rounded(o) * slopes[at, :].astype(f32)).astype(bf16)

        conv_rows(gradient_window(grads, count, m + 1), w_hidden.at[m - 1], -m, count + m, emit, between)


def input_gradient(count, w_first, grads, gvel):
    window = gradient_window(grads, count, 1)
    starts = list(range(0, count, 2))
    for k in range(0, len(starts), 2):
        group = starts[k : k + 2]
        o = jnp.dot(
            w_first[...],
            jnp.concatenate([window(r) for r in group], axis=1),
            preferred_element_type=f32,
        )
        for i, r in enumerate(group):
            part = o[:, i * N : (i + 1) * N]
            both = lanes(part, -1)[0:4] + part[4:8] + lanes(part, 1)[8:12]
            gvel[0, r : r + 2, :] = both[0:2]
            gvel[1, r : r + 2, :] = both[2:4]


def folded(x):
    return x[: 3 * CH, : 3 * CH] + x[3 * CH :, CH:]


def weight_product(count, m, us, vs, feats, grads):
    starts = list(range(0, count, 2))
    left, total = [], None
    for r in starts:
        g = [grads[gradient_rows(count, m, r + k), :] for k in range(2)]
        left.append(jnp.concatenate([lanes(x, -e) for x in g for e in (-1, 0, 1)], axis=0))
        for x in g:
            x = x.astype(f32)
            total = x if total is None else total + x
    if isinstance(m, int) and m == 1:
        right = [first_window(us, vs, r) for r in starts]
    else:
        right = [feature_window(feats, count, m - 1)(r) for r in starts]
    out = lax.dot_general(
        jnp.concatenate(left, axis=1), jnp.concatenate(right, axis=1), NT, preferred_element_type=f32
    )
    return out, jnp.sum(total, axis=1, keepdims=True)


def weight_gradients(count, us, vs, feats, grads, put, columns, loop):
    lane = lax.broadcasted_iota(jnp.int32, (CH, N), 1)

    def pair_of(pair):
        lower, a = weight_product(count, 2 + 2 * pair, us, vs, feats, grads)
        upper, b = weight_product(count, 3 + 2 * pair, us, vs, feats, grads)
        x = jnp.where(lane == 33 + 2 * pair, a, columns[...])
        columns[...] = jnp.where(lane == 34 + 2 * pair, b, x)
        wide = jnp.concatenate([folded(lower), folded(upper)], axis=1)
        for q in range(3):
            put(3 * pair + q, wide[:, q * N : (q + 1) * N])

    columns[...] = jnp.zeros((CH, N), f32)
    if loop:
        lax.fori_loop(0, 3, lambda pair, _: (pair_of(pair), 0)[1], 0)
    else:
        for pair in range(2, -1, -1):
            pair_of(pair)
    first, total = weight_product(count, 1, us, vs, feats, grads)
    rest = jnp.where(lane == 32, total, columns[...])
    first = jnp.concatenate([first[: 3 * CH], first[3 * CH :], jnp.zeros((3 * CH, N - 32), f32)], axis=1)
    put(9, first + jnp.concatenate([rest, jnp.zeros((2 * CH, N), f32)], axis=0))


def prepare_kernel(core, group, lengths, *refs):
    own, f_first, f_hidden, b_first, b_hidden, bias, right, left, weight, flags = refs[9:19]
    sems = refs[28]
    copies = [pltpu.make_async_copy(refs[i], refs[19 + i], sems.at[i]) for i in range(9)]
    for copy in copies:
        copy.start()
    upper = core[0] == 0
    for i in range(STEPS):
        flags[i] = jnp.full((8, N), jnp.where(lengths[core[0]] > i, 1.0, 0.0), f32)
    flags[STEPS] = jnp.full((8, N), jnp.where(upper, 1.0, 0.0), f32)
    for bit in range(flags.shape[0] - STEPS - 1):
        flags[STEPS + 1 + bit] = jnp.full((8, N), jnp.where((group[0] >> bit) & 1 == 1, 1.0, 0.0), f32)
    for copy in copies:
        copy.wait()
    vel, cot, first, first_bias, middle, middle_bias, last, last_bias, tables = refs[19:28]
    own[0] = jnp.where(upper, vel[0], vel[1])
    own[1] = jnp.where(upper, cot[0], cot[1])
    zero = jnp.zeros((CH, CH), bf16)
    for m in range(LAYERS):
        tap = (lambda a, e: last[3 * a + e]) if m == LAYERS - 1 else (lambda a, e: middle[m, 3 * a + e])
        for two in range(2):
            for e in range(3):
                at = slice((two * 3 + e) * CH, (two * 3 + e + 1) * CH)
                taps = [tap(q - two, e) if 0 <= q - two < 3 else zero for q in range(4)]
                f_hidden[m, at, :] = jnp.concatenate(taps, axis=1)
                taps = [tap(2 - q + two, 2 - e) if 0 <= q - two < 3 else zero for q in range(4)]
                b_hidden[m, at, :] = jnp.concatenate(
                    [jnp.concatenate(taps[:2], axis=0).T, jnp.concatenate(taps[2:], axis=0).T], axis=1
                )
    lines = jnp.zeros((1, CH), f32)
    for two in range(2):
        for e in range(3):
            taps = [lines] * 16
            for a in range(3):
                for ch in range(2):
                    taps[4 * ch + a + two] = first[3 * a + e, ch : ch + 1, :].astype(f32)
            at = slice((two * 3 + e) * CH, (two * 3 + e + 1) * CH)
            f_first[at, :] = jnp.concatenate(taps, axis=0).T.astype(bf16)
    taps = []
    for e in range(3):
        for ch in range(2):
            for two in range(2):
                line = [
                    first[3 * (2 - q + two) + 2 - e, ch : ch + 1, :].astype(f32) if 0 <= q - two < 3 else lines
                    for q in range(4)
                ]
                taps.append(jnp.concatenate(line, axis=1))
    taps.append(jnp.zeros((4, 4 * CH), f32))
    b_first[...] = jnp.concatenate(taps, axis=0).astype(bf16)
    for m in range(LAYERS + 1):
        if 0 < m < LAYERS:
            line = middle_bias[m - 1 : m, :]
        else:
            line = (first_bias if m == 0 else last_bias)[...].reshape(1, CH)
        bias[m] = jnp.broadcast_to(line, (N, CH)).T
    high, low = split(tables[0])
    right[...] = jnp.concatenate([high, high, low], axis=0)
    left[...] = jnp.concatenate([high, low, high], axis=1)
    weight[...] = tables[1]


def chosen(flag, x, y):
    flag = flag[0:1, :] > 0.5
    return jnp.where(jnp.broadcast_to(flag, x.shape), x, y)


def assemble_kernel(flags, own, partner, cross, same, cot_partner, ext, cot):
    upper = flags[STEPS]

    def pair(mine, other, i):
        other = chosen(upper, other[0, i], other[1, i])
        return [chosen(upper, mine[i], other), chosen(upper, other, mine[i])]

    for i in range(2):
        above = chosen(upper, cross[0, i], same[1, i])[-MARGIN:]
        below = chosen(upper, same[0, i], cross[1, i])[:MARGIN]
        ext[i] = jnp.concatenate([above, *pair(own[0], partner, i), below], axis=0)
        cot[i] = jnp.concatenate(pair(own[1], cot_partner, i), axis=0)


def network_kernel(count, vel, extra, w_first, w_hidden, bias, block, interp, raw, feats, slopes, us, vs):
    u, v = vel[0], vel[1]
    spread_columns(u, v, us, vs)

    def raw_done(r):
        at = r + 1 + MID
        if at % 8 == 0:
            interpolate(at // 8 - 1, (us, vs), raw, interp)
        elif r + 1 == count + RAW:
            interpolate(at // 8, (us, vs), raw, interp)

    network_forward(count, us, vs, w_first, w_hidden, bias, feats, slopes, raw, raw_done)
    su, sv = provisional(count, u, v, interp)
    block[0] = su
    block[1] = sv
    block[2] = extra[0]
    block[3] = extra[1]


def joined(gathered, i):
    return jnp.concatenate([g[i] for g in gathered], axis=0)


def project_kernel(count, blocks, steps, flags, *refs):
    gathered, refs = refs[:blocks], refs[blocks:]
    vel, right, left, weight, gstar, own, *ext = refs
    su, sv, cu, cv = [joined(gathered, i) for i in range(4)]
    mv, mg = [flags[step][0:1, :] for step in steps]
    news, grads = project([(su, sv), (mg * cu, mg * cv)], right, left, weight)
    for i in range(2):
        x = vel[i] + mv * (local(news[i], count) - vel[i])
        for ref in ext:
            ref[i] = x
        own[i] = x[MARGIN : MARGIN + count]
        gstar[i] = local(grads[i], count)
        own[2 + i] = (1.0 - mg) * gathered[0][2 + i]


def back_kernel(count, ext, gstar, b_first, b_hidden, slopes, *refs):
    if len(refs) == 8:
        raw, grads, gvel, lines, us, vs, graw32, ginterp = refs
    else:
        raw, lines = None, None
        grads, gvel, us, vs, graw32, ginterp = refs
    u, v = ext[0], ext[1]
    spread_columns(u, v, us, vs)
    interp_gradients(count, gstar[0], gstar[1], u, v, ginterp)
    chunks = (count + 2 * MID) // 8
    for q in range(chunks):
        raw_gradient(count, q, (us, vs), ginterp, graw32, grads)
    tasks = []
    if raw is not None:
        tasks = [functools.partial(spread_back, q, w, raw, ginterp, lines) for q in range(chunks) for w in range(2)]
    turn = [0]

    def between():
        turn[0] += 1
        if tasks and turn[0] % 4 == 0:
            tasks.pop(0)()

    network_backward(count, b_hidden, slopes, grads, between)
    for task in tasks:
        task()
    input_gradient(count, b_first, grads, gvel)


def finish_kernel(count, front, base, ext, gstar, interp, gvel, *refs):
    raw, out, lines, ginterp = refs if len(refs) == 4 else (None, refs[1], refs[0], None)
    gu, gv = gstar[0], gstar[1]
    if raw is not None:
        interp_gradients(count, gu, gv, ext[0], ext[1], ginterp)

        def step(q, _):
            for which in range(2):
                spread_back(q, which, raw, ginterp, lines)
            return 0

        lax.fori_loop(0, (count + 2 * MID) // 8, step, 0)
    change = velocity_gradients(count, gu, gv, interp, lines)
    for i in range(2):
        out[i] = front[i]
        out[2 + i] = base[2 + i] + change[i] + gvel[i]


def weights_kernel(count, ext, feats, grads, buffer, columns, us, vs):
    spread_columns(ext[0], ext[1], us, vs)

    def put(block, value):
        buffer[place(block * 3 * CH, 3 * CH), :] = value

    weight_gradients(count, us, vs, feats, grads, put, columns, True)


def total_weights_kernel(count, flags, previous, ext, feats, grads, keep, send, columns, us, vs, total):
    spread_columns(ext[0], ext[1], us, vs)
    half = keep.shape[0]

    def put(block, value):
        at = slice(block * 3 * CH, (block + 1) * 3 * CH)
        total[at, :] = value + previous[at, :]

    if 2 * half > BUFFER:
        total[BUFFER:, :] = jnp.zeros((2 * half - BUFFER, N), f32)
    weight_gradients(count, us, vs, feats, grads, put, columns, False)
    for low in range(0, half, 3 * CH):
        high = min(low + 3 * CH, half)
        a, b = total[low:high, :], total[half + low : half + high, :]
        keep[low:high, :] = chosen(flags[STEPS], a, b).astype(bf16)
        send[low:high, :] = chosen(flags[STEPS], b, a).astype(bf16)


def exchanged(flags, blocks):
    for bit in range(len(blocks).bit_length() - 1):
        flag = flags[STEPS + 1 + bit]
        blocks = [chosen(flag, blocks[i ^ (1 << bit)], x) for i, x in enumerate(blocks)]
    return blocks


def halves_kernel(flags, keep, received, *out):
    rows_each = out[0].shape[0]
    blocks = []
    for i in range(len(out)):
        at = slice(i * rows_each, (i + 1) * rows_each)
        blocks.append(keep[at, :].astype(f32) + received[at, :].astype(f32))
    for ref, x in zip(out, exchanged(flags, blocks)):
        ref[...] = x.astype(bf16)


def arrange_kernel(flags, *refs):
    *blocks, out = refs
    rows_each = blocks[0].shape[0]
    for i, x in enumerate(exchanged(flags, [x[...].astype(f32) for x in blocks])):
        out[i * rows_each : (i + 1) * rows_each, :] = x.astype(bf16)


def unpack_kernel(flags, mine, other, first, first_bias, middle, middle_bias, last, last_bias):
    half = mine.shape[0]

    def block(b):
        lines = []
        for low, high, a, c in ((0, half, mine, other), (half, 2 * half, other, mine)):
            start, stop = max(b * 3 * CH, low), min((b + 1) * 3 * CH, high)
            if start < stop:
                at = slice(start - low, stop - low)
                lines.append(chosen(flags[STEPS], a[at, :].astype(f32), c[at, :].astype(f32)))
        return lines[0] if len(lines) == 1 else jnp.concatenate(lines, axis=0)

    for pair in range(3):
        wide = jnp.concatenate([block(3 * pair + q) for q in range(3)], axis=1)
        for side in range(2):
            m = 2 * pair + side
            for a in range(3):
                at = (3 * side + a) * CH
                part = wide[:, at : at + CH]
                for e in range(3):
                    value = part[e * CH : (e + 1) * CH]
                    if m < LAYERS - 1:
                        middle[m, 3 * a + e] = value
                    else:
                        last[3 * a + e] = value
    rest = block(9)
    turned = [rest[e * CH : (e + 1) * CH].T for e in range(3)]
    for a in range(3):
        for e in range(3):
            for ch in range(2):
                low, high = 4 * ch + a, 16 + 4 * ch + a + 1
                first[3 * a + e, ch : ch + 1, :] = turned[e][low : low + 1] + turned[e][high : high + 1]
    turned = turned[0]
    first_bias[...] = turned[32]
    middle_bias[...] = turned[33 : 33 + LAYERS - 1]
    last_bias[...] = turned[32 + LAYERS]


VMEM = pl.BlockSpec(memory_space=pltpu.VMEM)
SMEM = pl.BlockSpec(memory_space=pltpu.SMEM)
PARAMS = pltpu.CompilerParams(vmem_limit_bytes=VMEM_BYTES)


def array(dtype, *shape):
    return jax.ShapeDtypeStruct(shape, dtype)


def cost(flops, moved):
    return pl.CostEstimate(flops=flops, bytes_accessed=moved, transcendentals=0)


def field(count, *lead):
    return pltpu.VMEM(lead + (count, N), f32)


def feature_array(count):
    return array(bf16, LAYERS * (count + 24) * CH, N)


def gradient_array(count, slots):
    return array(bf16, slots * (count + 16) * CH, N)


def call(kernel, name, flops, inputs, out, scratch=()):
    return pl.pallas_call(
        kernel,
        in_specs=[VMEM] * len(inputs),
        out_specs=jax.tree.map(lambda _: VMEM, out),
        out_shape=out,
        scratch_shapes=list(scratch),
        compiler_params=PARAMS,
        cost_estimate=cost(flops, 10**6),
        name=name,
    )(*inputs)


def run_prepare(core, group, lengths, vel, cot, params, bits):
    rc = vel.shape[2]
    out = [
        array(f32, 2, 2, rc, N),
        array(bf16, 6 * CH, 16),
        array(bf16, LAYERS, 6 * CH, 4 * CH),
        array(bf16, 16, 4 * CH),
        array(bf16, LAYERS, 6 * CH, 4 * CH),
        array(f32, LAYERS + 1, CH, N),
        array(bf16, 3 * N, N),
        array(bf16, N, 3 * N),
        array(f32, N, N),
        array(f32, STEPS + 1 + bits, 8, N),
    ]
    inputs = [vel, cot, *params, jnp.asarray(poisson_tables(N))]
    inputs = [pltpu.with_memory_space_constraint(x, pltpu.HBM) for x in inputs]
    return pl.pallas_call(
        prepare_kernel,
        in_specs=[SMEM] * 3 + [pl.BlockSpec(memory_space=pltpu.HBM)] * len(inputs),
        out_specs=[VMEM] * len(out),
        out_shape=out,
        scratch_shapes=[pltpu.VMEM(x.shape, x.dtype) for x in inputs]
        + [pltpu.SemaphoreType.DMA((len(inputs),))],
        compiler_params=PARAMS,
        cost_estimate=cost(10**9, 10**6),
        name="prepare",
    )(core, group, lengths, *inputs)


def run_assemble(count, flags, fields):
    out = [array(f32, 2, count + 2 * MARGIN, N), array(f32, 2, count, N)]
    return call(assemble_kernel, "assemble", 10**6, [flags, *fields], out)


def run_network(count, vel, extra, weights):
    local_rows, mid = count + 2 * MARGIN, count + 2 * MID
    out = [array(f32, 4, count, N), array(f32, 4, mid, N), array(f32, mid * CH, N)]
    out += [feature_array(count), gradient_array(count, LAYERS)]
    scratch = [field(local_rows, 4), field(local_rows, 4)]
    return call(functools.partial(network_kernel, count), "network", 4 * 10**9, [vel, extra, *weights], out, scratch)


def run_project(count, steps, flags, gathered, vel, tables, last=False):
    local_rows = count + 2 * MARGIN
    out = [array(f32, 2, local_rows, N), array(f32, 4, count, N)]
    if not last:
        out.append(array(f32, 2, local_rows, N))
    kernel = functools.partial(project_kernel, count, len(gathered), steps)
    return call(kernel, "project", 10**9, [flags, *gathered, vel, *tables], out)


def run_back(count, ext, gstar, b_first, b_hidden, slopes, raw=None):
    local_rows, mid = count + 2 * MARGIN, count + 2 * MID
    inputs = [ext, gstar, b_first, b_hidden, slopes]
    out = [gradient_array(count, LAYERS + 1), array(f32, 2, count, N)]
    if raw is not None:
        inputs.append(raw)
        out.append(array(f32, 2, 4, mid, N))
    scratch = [field(local_rows, 4), field(local_rows, 4), field(8 * CH), field(mid, 4)]
    return call(functools.partial(back_kernel, count), "back", 4 * 10**9, inputs, out, scratch)


def run_finish(count, front, base, ext, gstar, interp, gvel, raw=None, lines=None):
    mid = count + 2 * MID
    inputs = [front, base, ext, gstar, interp, gvel, lines if raw is None else raw]
    scratch = [] if raw is None else [field(mid, 2, 4), field(mid, 4)]
    return call(functools.partial(finish_kernel, count), "finish", 10**9, inputs, array(f32, 4, count, N), scratch)


def run_weights(count, ext, feats, grads):
    scratch = [field(CH)] + [field(count + 2 * MARGIN, 4)] * 2
    kernel = functools.partial(weights_kernel, count)
    return call(kernel, "weights", 3 * 10**9, [ext, feats, grads], array(f32, BUFFER, N), scratch)


def run_total_weights(count, half, flags, previous, ext, feats, grads):
    scratch = [field(CH)] + [field(count + 2 * MARGIN, 4)] * 2 + [field(2 * half)]
    inputs = [flags, previous, ext, feats, grads]
    kernel = functools.partial(total_weights_kernel, count)
    return call(kernel, "total_weights", 3 * 10**9, inputs, [array(bf16, half, N)] * 2, scratch)


def run_halves(flags, keep, received, parts):
    out = [array(bf16, keep.shape[0] // parts, N)] * parts
    return call(halves_kernel, "halves", 10**6, [flags, keep, received], out)


def run_arrange(flags, blocks):
    out = array(bf16, len(blocks) * blocks[0].shape[0], N)
    return call(arrange_kernel, "arrange", 10**6, [flags, *blocks], out)


def run_unpack(flags, mine, other):
    out = [
        array(f32, 9, 2, CH),
        array(f32, CH),
        array(f32, LAYERS - 1, 9, CH, CH),
        array(f32, LAYERS - 1, CH),
        array(f32, 9, CH, CH),
        array(f32, CH),
    ]
    return call(unpack_kernel, "unpack", 10**7, [flags, mine, other], out)


def swap(x, axis, offset):
    count = lax.axis_size(axis)
    return lax.ppermute(x, axis, [(i, i ^ offset) for i in range(count)])


def from_group(x, ahead):
    count = lax.axis_size("strip")
    return lax.ppermute(x, "strip", [(i, (i - 2 * ahead) % count) for i in range(count)])


def gather_groups(x):
    return [x] + [from_group(x, k) for k in range(1, lax.axis_size("strip") // 2)]


def margins(velocity, partner, core):
    count = lax.axis_size("strip")
    if velocity.shape[2] < MARGIN:
        upper = core[0] == 0
        pair = jnp.where(
            upper,
            jnp.concatenate([velocity[0], partner[0]], axis=1),
            jnp.concatenate([partner[1], velocity[1]], axis=1),
        )
        above, below = from_group(pair[:, -MARGIN:], -1), from_group(pair[:, :MARGIN], 1)
        return jnp.stack([above, below]), jnp.stack([below, above])
    cross = [(i, (i - 1) % count if i % 2 == 0 else (i + 1) % count) for i in range(count)]
    same = [(i, (i - 2) % count if i % 2 == 0 else (i + 2) % count) for i in range(count)]
    return lax.ppermute(velocity, "strip", cross), lax.ppermute(velocity, "strip", same)


def sum_everywhere(keep, send, flags):
    parts = lax.axis_size("traj")
    groups = lax.axis_size("strip") // 2
    blocks = run_halves(flags, keep, swap(send, "strip", 1), parts)
    total = blocks[0].astype(f32)
    for k in range(1, parts):
        total = total + swap(blocks[k], "traj", k).astype(f32)
    x = total.astype(bf16)
    total = x.astype(f32)
    for k in range(1, groups):
        total = total + swap(x, "strip", 2 * k).astype(f32)
    x = total.astype(bf16)
    x = run_arrange(flags, [x] + [swap(x, "traj", k) for k in range(1, parts)])
    return x, swap(x, "strip", 1)


def per_device(
    velocity, lengths, cotangent, first_kernel, first_bias, middle_kernels, middle_biases, last_kernel, last_bias
):
    rc = velocity.shape[2]
    count = 2 * rc
    index = lax.axis_index("strip") & 1
    core = index[None]
    pick = lambda y, i: lax.dynamic_index_in_dim(y, i, 0, False)

    partner = swap(velocity, "strip", 1)
    cross, same = margins(velocity, partner, core)
    cot_partner = swap(cotangent, "strip", 1)
    first_kernel = first_kernel.transpose(0, 2, 1)
    params = (first_kernel, first_bias, middle_kernels, middle_biases, last_kernel, last_bias)
    parts = lax.axis_size("traj")
    half = -(-BUFFER // (2 * parts * 16)) * parts * 16
    group = lax.axis_index("traj")[None]
    own, w_first, w_hidden, b_first, b_hidden, bias, *tables, flags = run_prepare(
        core, group, lengths, velocity, cotangent, params, parts.bit_length() - 1
    )
    weights = (w_first, w_hidden, bias)

    v0, cot = run_assemble(count, flags, (own, partner, cross, same, cot_partner))
    block, interp0, raw0, feats0, slopes0 = run_network(count, v0, cot, weights)
    gathered = gather_groups(block)
    gstar1, base, v1 = run_project(count, (0, 1), flags, gathered, v0, tables)
    block, interp1, raw1, feats1, slopes1 = run_network(count, v1, cot, weights)
    grads1, gvel, lines = run_back(count, v1, gstar1, b_first, b_hidden, slopes1, raw1)
    block = run_finish(count, block, base, v1, gstar1, interp1, gvel, lines=lines)
    gathered = gather_groups(block)
    buffer = run_weights(count, v1, feats1, grads1)
    gstar0, base = run_project(count, (1, 0), flags, gathered, v1, tables, last=True)
    grads0, gvel = run_back(count, v0, gstar0, b_first, b_hidden, slopes0)
    keep, send = run_total_weights(count, half, flags, buffer, v0, feats0, grads0)
    out = run_finish(count, base, base, v0, gstar0, interp0, gvel, raw=raw0)

    strips = out.reshape(4, 2, rc, N).transpose(1, 0, 2, 3)
    mine, other = pick(strips, index)[None], swap(pick(strips, 1 - index), "strip", 1)[None]
    out = jnp.where(
        index == 0, jnp.concatenate([mine, other], axis=0), jnp.concatenate([other, mine], axis=0)
    )
    mine, other = sum_everywhere(keep, send, flags)
    first, *rest = run_unpack(flags, mine, other)
    return (out[:, :2], out[:, 2:], first.transpose(0, 2, 1), *rest)


def solution(mesh):
    band = P("traj", None, "strip", None)
    return jax.shard_map(
        per_device,
        mesh=mesh,
        in_specs=(band, P("traj"), band) + (P(),) * 6,
        out_specs=(band, band) + (P(),) * 6,
        check_vma=False,
    )
```

time: 108 us -> 88.6 us (0.82); the launches traced: 106 us -> 88.4 us
  Pallas kernels: 58.1 us -> 44.2 us
  other arithmetic: 1.95 us -> 0.09 us
  starting transfers between devices: 24.2 us -> 22.9 us
    pallas_call x7 -> x15, Pallas kernels: 58.1 us -> 44.2 us  [the longest x14 41.2 us: call(): pl.pallas_call(kernel, in_specs=[VMEM] * len(inputs), out_specs=jax.tree....]
    ppermute x1, waiting for transfers between devices: 1.28 us -> 0.09 us  [margins(): lax.ppermute(velocity, 'strip', same)]
  transfers between devices with their start and end apart: 22 -> 22, of which waited for: 13 -> 14; matrix products, arithmetic and copies ran while one was open for 1% -> 1% of each run, Pallas kernels for 8% -> 10%
where the time goes in v1:
time: 88.6 us; the launch traced here: 88.4 us
  Pallas kernels  44.2 us (50%)
  starting transfers between devices  22.9 us (26%)
  waiting for transfers between devices  19.1 us (22%)
  local copies, waits for them, and re-layouts  1.29 us (1%)
    pallas_call x14, Pallas kernels, call(): pl.pallas_call(kernel, in_specs=[VMEM] * len(inputs), out_specs=jax.tree....  41.2 us
    ppermute x14, starting transfers between devices, swap(): return lax.ppermute(x, axis, [(i, i ^ offset) for i in range(count)])  12.2 us
    ppermute x14, waiting for transfers between devices, swap(): return lax.ppermute(x, axis, [(i, i ^ offset) for i in range(count)])  11.4 us
    ppermute x6, waiting for transfers between devices, from_group(): lax.ppermute(x, 'strip', [(i, (i - 2 * ahead) % count) for i in range(cou...  7.67 us
    ppermute x6, starting transfers between devices, from_group(): lax.ppermute(x, 'strip', [(i, (i - 2 * ahead) % count) for i in range(cou...  5.56 us
    ppermute x1, starting transfers between devices, margins(): lax.ppermute(velocity, 'strip', cross)  4.71 us
    pallas_call x1, Pallas kernels, run_prepare(): pl.pallas_call(prepare_kernel, in_specs=[SMEM] * 3 + [pl.BlockSpec(memory...  2.9 us
  transfers between devices with their start and end apart: 22, of which 14 were waited for; matrix products, arithmetic and copies ran while one was open for 1% of the time, Pallas kernels for 10%

profile of v1, /device:TPU:0, one launch (start us, length us, event | category | flops | bytes accessed | tf_op | source)
XLA Modules:
  0.0 88.4 jit_solution(7775258701423616233)
XLA Ops:
  1.2 4.7 %collective-permute-start.1 = (f32[2,2,16,128]{3,2,1,0:T(8,128)}, f32[2,2,16,128]{3,2,1,0:T(8,128)S(1)}, u32[]{:S(2)}, u32[]{:S(2)}) collective-permute-start(f32[2,2,16,128]{3,2,1,0:T(8,128)} %refs_0_.1), channel_id=1, source_target_pairs={{0,7},{1,2},{2,1},{3,4},{4,3},{5,6},{6,5},{7,0},{8,15},{9,10},{10,... | collective-permute-start | bytes 98312 | tf_op jit(solution)/shard_map/ppermute | solution.py:796
  7.0 2.9 %prepare.1 = (f32[2,2,16,128]{3,2,1,0:T(8,128)S(1)}, bf16[384,16]{1,0:T(8,128)(2,1)S(1)}, bf16[6,384,256]{2,1,0:T(8,128)(2,1)S(1)}, bf16[16,256]{1,0:T(8,128)(2,...) custom-call(s32[1]{0:T(128)} %bitcast.core, ...), custom_call_target="tpu_custom_call" | custom-call | flops 1000000000 | bytes 1000000 | tf_op jit(solution)/shard_map/prepare/pallas_call | solution.py:681
  10.0 8.9 %network.2 = (f32[4,32,128]{2,1,0:T(8,128)S(1)}, f32[4,48,128]{2,1,0:T(8,128)S(1)}, f32[3072,128]{1,0:T(8,128)S(1)}, bf16[21504,128]{1,0:T(8,128)(2,1)S(1)}, bf16[18432,128]{1,0:T(8,128)(2,1)S(1)}) custom-call(f32[2,64,128]{2,1,0:T(8,128)S(1)} %get-tuple-element.54.vel.refs_4_.ext, f32[2,32,128]{2,1,0:T(8,128)S(1)} %get-tuple-element.55.extra, ...), custom_call_target="tpu_custom_call" | custom-call | flops 4000000000 | bytes 1000000 | tf_op jit(solution)/shard_map/network/pallas_call | solution.py:653
  18.9 2.3 %collective-permute-start.4 = (f32[4,32,128]{2,1,0:T(8,128)S(1)}, f32[4,32,128]{2,1,0:T(8,128)S(1)}, u32[]{:S(2)}, u32[]{:S(2)}) collective-permute-start(f32[4,32,128]{2,1,0:T(8,128)S(1)} %get-tuple-element.59.refs_0_), channel_id=1, source_target_pairs={{0,6},{1,7},{2,0},{3,1},{4,2},{5,3},{6,4},{7,5},{8,14},{9,15},{10,... | collective-permute-start | bytes 196616 | tf_op jit(solution)/shard_map/ppermute | solution.py:776
  21.9 1.8 %collective-permute-done.4.refs_1_ = f32[4,32,128]{2,1,0:T(8,128)S(1)} collective-permute-done((f32[4,32,128]{2,1,0:T(8,128)S(1)}, f32[4,32,128]{2,1,0:T(8,128)S(1)}, u32[]{:S(2)}, u32[]{:S(2)}) %collective-permute-start.4) | collective-permute-done | bytes 65568 | tf_op jit(solution)/shard_map/ppermute | solution.py:776
  23.7 4.9 %collective-permute-done.5.refs_2_ = f32[4,32,128]{2,1,0:T(8,128)S(1)} collective-permute-done((f32[4,32,128]{2,1,0:T(8,128)S(1)}, f32[4,32,128]{2,1,0:T(8,128)S(1)}, u32[]{:S(2)}, u32[]{:S(2)}) %collective-permute-start.5) | collective-permute-done | bytes 65568 | tf_op jit(solution)/shard_map/ppermute | solution.py:776
  29.5 8.7 %network.3 = (f32[4,32,128]{2,1,0:T(8,128)S(1)}, f32[4,48,128]{2,1,0:T(8,128)S(1)}, f32[3072,128]{1,0:T(8,128)S(1)}, bf16[21504,128]{1,0:T(8,128)(2,1)S(1)}, bf16[18432,128]{1,0:T(8,128)(2,1)S(1)}) custom-call(f32[2,64,128]{2,1,0:T(8,128)S(1)} %get-tuple-element.63.vel.ext.refs_4_, f32[2,32,128]{2,1,0:T(8,128)S(1)} %get-tuple-element.55.extra, ...), custom_call_target="tpu_custom_call" | custom-call | flops 4000000000 | bytes 1000000 | tf_op jit(solution)/shard_map/network/pallas_call | solution.py:653
  38.2 5.9 %back.2 = (bf16[21504,128]{1,0:T(8,128)(2,1)S(1)}, f32[2,32,128]{2,1,0:T(8,128)S(1)}, f32[2,4,48,128]{3,2,1,0:T(8,128)S(1)}) custom-call(f32[2,64,128]{2,1,0:T(8,128)S(1)} %get-tuple-element.63.vel.ext.refs_4_, f32[2,64,128]{2,1,0:T(8,128)S(1)} %get-tuple-element.66.gstar, bf16[16,256]{1,0:T(8,128)(2,1)S(1)} %get-tuple-element.68.b_first, ...), custom_call_target="tpu_custom_call" | custom-call | flops 4000000000 | bytes 1000000 | tf_op jit(solution)/shard_map/back/pallas_call | solution.py:653
  45.5 1.3 %collective-permute-start.9 = (f32[4,32,128]{2,1,0:T(8,128)S(1)}, f32[4,32,128]{2,1,0:T(8,128)S(1)}, u32[]{:S(2)}, u32[]{:S(2)}) collective-permute-start(f32[4,32,128]{2,1,0:T(8,128)S(1)} %finish.2.refs_0_), channel_id=1, source_target_pairs={{0,2},{1,3},{2,4},{3,5},{4,6},{5,7},{6,0},{7,1},{8,10},{9,11},{10,... | collective-permute-start | bytes 196616 | tf_op jit(solution)/shard_map/ppermute | solution.py:776
  46.8 4.4 %weights.1.previous = f32[1920,128]{1,0:T(8,128)S(1)} custom-call(f32[2,64,128]{2,1,0:T(8,128)S(1)} %get-tuple-element.63.vel.ext.refs_4_, bf16[21504,128]{1,0:T(8,128)(2,1)S(1)} %get-tuple-element.80.feats, bf16[21504,128]{1,0:T(8,128)(2,1)S(1)} %get-tuple-element.81.grads), custom_call_target="tpu_custom_call" | custom-call | flops 3000000000 | bytes 1000000 | tf_op jit(solution)/shard_map/weights/pallas_call | solution.py:653
  53.2 4.8 %back.3 = (bf16[21504,128]{1,0:T(8,128)(2,1)S(1)}, f32[2,32,128]{2,1,0:T(8,128)S(1)}) custom-call(f32[2,64,128]{2,1,0:T(8,128)S(1)} %get-tuple-element.54.vel.refs_4_.ext, f32[2,64,128]{2,1,0:T(8,128)S(1)} %get-tuple-element.75.gstar, bf16[16,256]{1,0:T(8,128)(2,1)S(1)} %get-tuple-element.68.b_first, bf16[6,384,256]{2,1,0:T(8,128)(2,1)S(1)} %get-tuple-element.69.b_hidden, ...), custom_call_target="tpu_custom_call" | custom-call | flops 4000000000 | bytes 1000000 | tf_op jit(solution)/shard_map/back/pallas_call | solution.py:653
  58.0 3.3 %total_weights.1 = (bf16[960,128]{1,0:T(8,128)(2,1)S(1)}, bf16[960,128]{1,0:T(8,128)(2,1)S(1)}) custom-call(f32[5,8,128]{2,1,0:T(8,128)S(1)} %get-tuple-element.52.flags, f32[1920,128]{1,0:T(8,128)S(1)} %weights.1.previous, f32[2,64,128]{2,1,0:T(8,128)S(1)} %get-tuple-element.54.vel.refs_4_.ext, bf16[21504,128]{1,0:T(8,128)(2,1)S(1)} %get-tuple-element.82.feats, ...), custom_call_target="tpu_custom_call" | custom-call | flops 3000000000 | bytes 1000000 | tf_op jit(solution)/shard_map/total_weights/pallas_call | solution.py:653
  61.3 1.5 %collective-permute-done.11.received = bf16[960,128]{1,0:T(8,128)(2,1)S(1)} collective-permute-done((bf16[960,128]{1,0:T(8,128)(2,1)S(1)}, bf16[960,128]{1,0:T(8,128)(2,1)S(1)}, u32[]{:S(2)}, u32[]{:S(2)}) %collective-permute-start.11) | collective-permute-done | bytes 245792 | tf_op jit(solution)/shard_map/ppermute | solution.py:771
  62.9 2.5 %collective-permute-start.14 = (bf16[240,128]{1,0:T(8,128)(2,1)S(1)}, bf16[240,128]{1,0:T(8,128)(2,1)S(1)}, u32[]{:S(2)}, u32[]{:S(2)}) collective-permute-start(bf16[240,128]{1,0:T(8,128)(2,1)S(1)} %get-tuple-element.89), channel_id=1, source_target_pairs={{0,24},{8,16},{16,8},{24,0},{1,25},{9,17},{17,9},{25,1},{2,26},{10... | collective-permute-start | bytes 184328 | tf_op jit(solution)/shard_map/ppermute | solution.py:771
  66.5 1.7 %collective-permute-done.14 = bf16[240,128]{1,0:T(8,128)(2,1)S(1)} collective-permute-done((bf16[240,128]{1,0:T(8,128)(2,1)S(1)}, bf16[240,128]{1,0:T(8,128)(2,1)S(1)}, u32[]{:S(2)}, u32[]{:S(2)}) %collective-permute-start.14) | collective-permute-done | bytes 61472 | tf_op jit(solution)/shard_map/ppermute | solution.py:771
  68.1 1.5 %collective-permute-done.13 = bf16[240,128]{1,0:T(8,128)(2,1)S(1)} collective-permute-done((bf16[240,128]{1,0:T(8,128)(2,1)S(1)}, bf16[240,128]{1,0:T(8,128)(2,1)S(1)}, u32[]{:S(2)}, u32[]{:S(2)}) %collective-permute-start.13) | collective-permute-done | bytes 61472 | tf_op jit(solution)/shard_map/ppermute | solution.py:771
  70.2 1.6 %collective-permute-start.17 = (bf16[240,128]{1,0:T(8,128)(2,1)S(1)}, bf16[240,128]{1,0:T(8,128)(2,1)S(1)}, u32[]{:S(2)}, u32[]{:S(2)}) collective-permute-start(bf16[240,128]{1,0:T(8,128)(2,1)S(1)} %add_convert_fusion.1), channel_id=1, source_target_pairs={{0,6},{1,7},{2,4},{3,5},{4,2},{5,3},{6,0},{7,1},{8,14},{9,15},{10,... | collective-permute-start | bytes 184328 | tf_op jit(solution)/shard_map/ppermute | solution.py:771
  71.9 2.8 %collective-permute-start.15 = (bf16[240,128]{1,0:T(8,128)(2,1)S(1)}, bf16[240,128]{1,0:T(8,128)(2,1)S(1)}, u32[]{:S(2)}, u32[]{:S(2)}) collective-permute-start(bf16[240,128]{1,0:T(8,128)(2,1)S(1)} %add_convert_fusion.1), channel_id=1, source_target_pairs={{0,2},{1,3},{2,0},{3,1},{4,6},{5,7},{6,4},{7,5},{8,10},{9,11},{10,... | collective-permute-start | bytes 184328 | tf_op jit(solution)/shard_map/ppermute | solution.py:771
  74.7 1.7 %finish.3 = f32[4,32,128]{2,1,0:T(8,128)S(1)} custom-call(f32[4,32,128]{2,1,0:T(8,128)S(1)} %get-tuple-element.74.front.base, f32[4,32,128]{2,1,0:T(8,128)S(1)} %get-tuple-element.74.front.base, f32[2,64,128]{2,1,0:T(8,128)S(1)} %get-tuple-element.54.vel.refs_4_.ext, f32[2,64,128]{2,1,0:T(8,128)S(1)} %get-tuple-element.75.gstar, ...), custom_call_target="tpu_custom_call" | custom-call | flops 1000000000 | bytes 1000000 | tf_op jit(solution)/shard_map/finish/pallas_call | solution.py:653
  76.4 1.3 %collective-permute-done.16 = bf16[240,128]{1,0:T(8,128)(2,1)S(1)} collective-permute-done((bf16[240,128]{1,0:T(8,128)(2,1)S(1)}, bf16[240,128]{1,0:T(8,128)(2,1)S(1)}, u32[]{:S(2)}, u32[]{:S(2)}) %collective-permute-start.16) | collective-permute-done | bytes 61472 | tf_op jit(solution)/shard_map/ppermute | solution.py:771
  77.8 1.4 %collective-permute-start.18 = (bf16[240,128]{1,0:T(8,128)(2,1)S(1)}, bf16[240,128]{1,0:T(8,128)(2,1)S(1)}, u32[]{:S(2)}, u32[]{:S(2)}) collective-permute-start(bf16[240,128]{1,0:T(8,128)(2,1)S(1)} %add_convert_fusion.refs_0_), channel_id=1, source_target_pairs={{0,8},{8,0},{16,24},{24,16},{1,9},{9,1},{17,25},{25,17},{2,10},{10... | collective-permute-start | bytes 184328 | tf_op jit(solution)/shard_map/ppermute | solution.py:771
  82.1 1.9 %collective-permute-done.19.refs_2_ = bf16[240,128]{1,0:T(8,128)(2,1)S(1)} collective-permute-done((bf16[240,128]{1,0:T(8,128)(2,1)S(1)}, bf16[240,128]{1,0:T(8,128)(2,1)S(1)}, u32[]{:S(2)}, u32[]{:S(2)}) %collective-permute-start.19) | collective-permute-done | bytes 61472 | tf_op jit(solution)/shard_map/ppermute | solution.py:771
  84.0 1.3 %collective-permute-done.20.refs_3_ = bf16[240,128]{1,0:T(8,128)(2,1)S(1)} collective-permute-done((bf16[240,128]{1,0:T(8,128)(2,1)S(1)}, bf16[240,128]{1,0:T(8,128)(2,1)S(1)}, u32[]{:S(2)}, u32[]{:S(2)}) %collective-permute-start.20) | collective-permute-done | bytes 61472 | tf_op jit(solution)/shard_map/ppermute | solution.py:771
  87.0 1.4 %unpack.1 = (f32[9,2,64]{2,1,0:T(2,128)}, f32[64]{0:T(128)}, f32[5,9,64,64]{3,2,1,0:T(8,128)}, f32[5,64]{1,0:T(8,128)}, f32[9,64,64]{2,1,0:T(8,128)}, /*index=5*/f32[64]{0:T(128)}) custom-call(f32[5,8,128]{2,1,0:T(8,128)S(1)} %get-tuple-element.52.flags, bf16[960,128]{1,0:T(8,128)(2,1)S(1)} %arrange.1.mine, bf16[960,128]{1,0:T(8,128)(2,1)S(1)} %collective-permute-done.21.other), custom_call_target="tpu_custom_call" | custom-call | flops 10000000 | bytes 1000000 | tf_op jit(solution)/shard_map/unpack/pallas_call | solution.py:653
  (42 shorter events, 13.1 us)
Async XLA Ops:
  0.6 9.3 %collective-permute-start = (f32[2,2,16,128]{3,2,1,0:T(8,128)}, f32[2,2,16,128]{3,2,1,0:T(8,128)S(1)}, u32[]{:S(2)}, u32[]{:S(2)}) collective-permute-start(f32[2,2,16,128]{3,2,1,0:T(8,128)} %refs_0_.1), channel_id=1, source_target_pairs={{0,1},{1,0},{2,3},{3,2},{4,5},{5,4},{6,7},{7,6},{8,9},{9,8},{10,11... | collective-permute-start | bytes 98312 | tf_op jit(solution)/shard_map/ppermute | solution.py:771
  1.2 8.7 %collective-permute-start.1 = (f32[2,2,16,128]{3,2,1,0:T(8,128)}, f32[2,2,16,128]{3,2,1,0:T(8,128)S(1)}, u32[]{:S(2)}, u32[]{:S(2)}) collective-permute-start(f32[2,2,16,128]{3,2,1,0:T(8,128)} %refs_0_.1), channel_id=1, source_target_pairs={{0,7},{1,2},{2,1},{3,4},{4,3},{5,6},{6,5},{7,0},{8,15},{9,10},{10,... | collective-permute-start | bytes 98312 | tf_op jit(solution)/shard_map/ppermute | solution.py:796
  5.9 4.1 %collective-permute-start.2 = (f32[2,2,16,128]{3,2,1,0:T(8,128)}, f32[2,2,16,128]{3,2,1,0:T(8,128)S(1)}, u32[]{:S(2)}, u32[]{:S(2)}) collective-permute-start(f32[2,2,16,128]{3,2,1,0:T(8,128)} %refs_0_.1), channel_id=1, source_target_pairs={{0,6},{1,3},{2,0},{3,5},{4,2},{5,7},{6,4},{7,1},{8,14},{9,11},{10,... | collective-permute-start | bytes 98312 | tf_op jit(solution)/shard_map/ppermute | solution.py:796
  6.3 3.7 %collective-permute-start.3 = (f32[2,2,16,128]{3,2,1,0:T(8,128)}, f32[2,2,16,128]{3,2,1,0:T(8,128)S(1)}, u32[]{:S(2)}, u32[]{:S(2)}) collective-permute-start(f32[2,2,16,128]{3,2,1,0:T(8,128)} %refs_1_.1), channel_id=1, source_target_pairs={{0,1},{1,0},{2,3},{3,2},{4,5},{5,4},{6,7},{7,6},{8,9},{9,8},{10,11... | collective-permute-start | bytes 98312 | tf_op jit(solution)/shard_map/ppermute | solution.py:771
  6.3 0.7 copy-start
  18.9 4.8 %collective-permute-start.4 = (f32[4,32,128]{2,1,0:T(8,128)S(1)}, f32[4,32,128]{2,1,0:T(8,128)S(1)}, u32[]{:S(2)}, u32[]{:S(2)}) collective-permute-start(f32[4,32,128]{2,1,0:T(8,128)S(1)} %get-tuple-element.59.refs_0_), channel_id=1, source_target_pairs={{0,6},{1,7},{2,0},{3,1},{4,2},{5,3},{6,4},{7,5},{8,14},{9,15},{10,... | collective-permute-start | bytes 196616 | tf_op jit(solution)/shard_map/ppermute | solution.py:776
  21.2 7.4 %collective-permute-start.5 = (f32[4,32,128]{2,1,0:T(8,128)S(1)}, f32[4,32,128]{2,1,0:T(8,128)S(1)}, u32[]{:S(2)}, u32[]{:S(2)}) collective-permute-start(f32[4,32,128]{2,1,0:T(8,128)S(1)} %get-tuple-element.59.refs_0_), channel_id=1, source_target_pairs={{0,4},{1,5},{2,6},{3,7},{4,0},{5,1},{6,2},{7,3},{8,12},{9,13},{10,... | collective-permute-start | bytes 196616 | tf_op jit(solution)/shard_map/ppermute | solution.py:776
  21.9 6.7 %collective-permute-start.6 = (f32[4,32,128]{2,1,0:T(8,128)S(1)}, f32[4,32,128]{2,1,0:T(8,128)S(1)}, u32[]{:S(2)}, u32[]{:S(2)}) collective-permute-start(f32[4,32,128]{2,1,0:T(8,128)S(1)} %get-tuple-element.59.refs_0_), channel_id=1, source_target_pairs={{0,2},{1,3},{2,4},{3,5},{4,6},{5,7},{6,0},{7,1},{8,10},{9,11},{10,... | collective-permute-start | bytes 196616 | tf_op jit(solution)/shard_map/ppermute | solution.py:776
  44.3 7.0 %collective-permute-start.7 = (f32[4,32,128]{2,1,0:T(8,128)S(1)}, f32[4,32,128]{2,1,0:T(8,128)S(1)}, u32[]{:S(2)}, u32[]{:S(2)}) collective-permute-start(f32[4,32,128]{2,1,0:T(8,128)S(1)} %finish.2.refs_0_), channel_id=1, source_target_pairs={{0,6},{1,7},{2,0},{3,1},{4,2},{5,3},{6,4},{7,5},{8,14},{9,15},{10,... | collective-permute-start | bytes 196616 | tf_op jit(solution)/shard_map/ppermute | solution.py:776
  44.4 7.9 %collective-permute-start.8 = (f32[4,32,128]{2,1,0:T(8,128)S(1)}, f32[4,32,128]{2,1,0:T(8,128)S(1)}, u32[]{:S(2)}, u32[]{:S(2)}) collective-permute-start(f32[4,32,128]{2,1,0:T(8,128)S(1)} %finish.2.refs_0_), channel_id=1, source_target_pairs={{0,4},{1,5},{2,6},{3,7},{4,0},{5,1},{6,2},{7,3},{8,12},{9,13},{10,... | collective-permute-start | bytes 196616 | tf_op jit(solution)/shard_map/ppermute | solution.py:776
  45.5 6.8 %collective-permute-start.9 = (f32[4,32,128]{2,1,0:T(8,128)S(1)}, f32[4,32,128]{2,1,0:T(8,128)S(1)}, u32[]{:S(2)}, u32[]{:S(2)}) collective-permute-start(f32[4,32,128]{2,1,0:T(8,128)S(1)} %finish.2.refs_0_), channel_id=1, source_target_pairs={{0,2},{1,3},{2,4},{3,5},{4,6},{5,7},{6,0},{7,1},{8,10},{9,11},{10,... | collective-permute-start | bytes 196616 | tf_op jit(solution)/shard_map/ppermute | solution.py:776
  61.2 1.6 %collective-permute-start.11 = (bf16[960,128]{1,0:T(8,128)(2,1)S(1)}, bf16[960,128]{1,0:T(8,128)(2,1)S(1)}, u32[]{:S(2)}, u32[]{:S(2)}) collective-permute-start(bf16[960,128]{1,0:T(8,128)(2,1)S(1)} %get-tuple-element.85), channel_id=1, source_target_pairs={{0,1},{1,0},{2,3},{3,2},{4,5},{5,4},{6,7},{7,6},{8,9},{9,8},{10,11... | collective-permute-start | bytes 737288 | tf_op jit(solution)/shard_map/ppermute | solution.py:771
  62.9 5.2 %collective-permute-start.14 = (bf16[240,128]{1,0:T(8,128)(2,1)S(1)}, bf16[240,128]{1,0:T(8,128)(2,1)S(1)}, u32[]{:S(2)}, u32[]{:S(2)}) collective-permute-start(bf16[240,128]{1,0:T(8,128)(2,1)S(1)} %get-tuple-element.89), channel_id=1, source_target_pairs={{0,24},{8,16},{16,8},{24,0},{1,25},{9,17},{17,9},{25,1},{2,26},{10... | collective-permute-start | bytes 184328 | tf_op jit(solution)/shard_map/ppermute | solution.py:771
  65.5 4.2 %collective-permute-start.13 = (bf16[240,128]{1,0:T(8,128)(2,1)S(1)}, bf16[240,128]{1,0:T(8,128)(2,1)S(1)}, u32[]{:S(2)}, u32[]{:S(2)}) collective-permute-start(bf16[240,128]{1,0:T(8,128)(2,1)S(1)} %get-tuple-element.88), channel_id=1, source_target_pairs={{0,16},{8,24},{16,0},{24,8},{1,17},{9,25},{17,1},{25,9},{2,18},{10... | collective-permute-start | bytes 184328 | tf_op jit(solution)/shard_map/ppermute | solution.py:771
  66.0 4.2 %collective-permute-start.12 = (bf16[240,128]{1,0:T(8,128)(2,1)S(1)}, bf16[240,128]{1,0:T(8,128)(2,1)S(1)}, u32[]{:S(2)}, u32[]{:S(2)}) collective-permute-start(bf16[240,128]{1,0:T(8,128)(2,1)S(1)} %get-tuple-element.87), channel_id=1, source_target_pairs={{0,8},{8,0},{16,24},{24,16},{1,9},{9,1},{17,25},{25,17},{2,10},{10... | collective-permute-start | bytes 184328 | tf_op jit(solution)/shard_map/ppermute | solution.py:771
  70.2 6.2 %collective-permute-start.17 = (bf16[240,128]{1,0:T(8,128)(2,1)S(1)}, bf16[240,128]{1,0:T(8,128)(2,1)S(1)}, u32[]{:S(2)}, u32[]{:S(2)}) collective-permute-start(bf16[240,128]{1,0:T(8,128)(2,1)S(1)} %add_convert_fusion.1), channel_id=1, source_target_pairs={{0,6},{1,7},{2,4},{3,5},{4,2},{5,3},{6,0},{7,1},{8,14},{9,15},{10,... | collective-permute-start | bytes 184328 | tf_op jit(solution)/shard_map/ppermute | solution.py:771
  71.8 6.0 %collective-permute-start.16 = (bf16[240,128]{1,0:T(8,128)(2,1)S(1)}, bf16[240,128]{1,0:T(8,128)(2,1)S(1)}, u32[]{:S(2)}, u32[]{:S(2)}) collective-permute-start(bf16[240,128]{1,0:T(8,128)(2,1)S(1)} %add_convert_fusion.1), channel_id=1, source_target_pairs={{0,4},{1,5},{2,6},{3,7},{4,0},{5,1},{6,2},{7,3},{8,12},{9,13},{10,... | collective-permute-start | bytes 184328 | tf_op jit(solution)/shard_map/ppermute | solution.py:771
  71.9 5.9 %collective-permute-start.15 = (bf16[240,128]{1,0:T(8,128)(2,1)S(1)}, bf16[240,128]{1,0:T(8,128)(2,1)S(1)}, u32[]{:S(2)}, u32[]{:S(2)}) collective-permute-start(bf16[240,128]{1,0:T(8,128)(2,1)S(1)} %add_convert_fusion.1), channel_id=1, source_target_pairs={{0,2},{1,3},{2,0},{3,1},{4,6},{5,7},{6,4},{7,5},{8,10},{9,11},{10,... | collective-permute-start | bytes 184328 | tf_op jit(solution)/shard_map/ppermute | solution.py:771
  77.8 4.3 %collective-permute-start.18 = (bf16[240,128]{1,0:T(8,128)(2,1)S(1)}, bf16[240,128]{1,0:T(8,128)(2,1)S(1)}, u32[]{:S(2)}, u32[]{:S(2)}) collective-permute-start(bf16[240,128]{1,0:T(8,128)(2,1)S(1)} %add_convert_fusion.refs_0_), channel_id=1, source_target_pairs={{0,8},{8,0},{16,24},{24,16},{1,9},{9,1},{17,25},{25,17},{2,10},{10... | collective-permute-start | bytes 184328 | tf_op jit(solution)/shard_map/ppermute | solution.py:771
  79.2 4.8 %collective-permute-start.19 = (bf16[240,128]{1,0:T(8,128)(2,1)S(1)}, bf16[240,128]{1,0:T(8,128)(2,1)S(1)}, u32[]{:S(2)}, u32[]{:S(2)}) collective-permute-start(bf16[240,128]{1,0:T(8,128)(2,1)S(1)} %add_convert_fusion.refs_0_), channel_id=1, source_target_pairs={{0,16},{8,24},{16,0},{24,8},{1,17},{9,25},{17,1},{25,9},{2,18},{10... | collective-permute-start | bytes 184328 | tf_op jit(solution)/shard_map/ppermute | solution.py:771
  80.2 5.1 %collective-permute-start.20 = (bf16[240,128]{1,0:T(8,128)(2,1)S(1)}, bf16[240,128]{1,0:T(8,128)(2,1)S(1)}, u32[]{:S(2)}, u32[]{:S(2)}) collective-permute-start(bf16[240,128]{1,0:T(8,128)(2,1)S(1)} %add_convert_fusion.refs_0_), channel_id=1, source_target_pairs={{0,24},{8,16},{16,8},{24,0},{1,25},{9,17},{17,9},{25,1},{2,26},{10... | collective-permute-start | bytes 184328 | tf_op jit(solution)/shard_map/ppermute | solution.py:771
  81.4 4.1 %collective-permute-start.10 = (f32[4,16,128]{2,1,0:T(8,128)S(1)}, f32[4,16,128]{2,1,0:T(8,128)S(1)}, u32[]{:S(2)}, u32[]{:S(2)}) collective-permute-start(f32[4,16,128]{2,1,0:T(8,128)S(1)} %get-tuple-element.99), channel_id=1, source_target_pairs={{0,1},{1,0},{2,3},{3,2},{4,5},{5,4},{6,7},{7,6},{8,9},{9,8},{10,11... | collective-permute-start | bytes 98312 | tf_op jit(solution)/shard_map/ppermute | solution.py:771
  85.4 1.6 %collective-permute-start.21 = (bf16[960,128]{1,0:T(8,128)(2,1)S(1)}, bf16[960,128]{1,0:T(8,128)(2,1)S(1)}, u32[]{:S(2)}, u32[]{:S(2)}) collective-permute-start(bf16[960,128]{1,0:T(8,128)(2,1)S(1)} %arrange.1.mine), channel_id=1, source_target_pairs={{0,1},{1,0},{2,3},{3,2},{4,5},{5,4},{6,7},{7,6},{8,9},{9,8},{10,11... | collective-permute-start | bytes 737288 | tf_op jit(solution)/shard_map/ppermute | solution.py:771

commit v2 on v1

--- a/solution.py
+++ b/solution.py
@@ -13,6 +13,7 @@
 DT = 0.25
 MARGIN = 16
 MID = 8
+LAG = 3
 RAW = 2
 CH = 64
 LAYERS = 6
@@ -48,7 +49,14 @@
     return x if s == 0 else pltpu.roll(x, (-s) % x.shape[0], 0)
 
 
-def poisson_tables(length):
+TARGETS = ((0.0, -0.5), (-0.5, 0.0), (0.0, -0.5), (-0.5, 0.0))
+POINTS = np.arange(16)
+PX, PY = POINTS % 4 - 1.5, POINTS // 4 - 1.5
+TAKEN = 5.0 + 4.0 * (PX[:, None] * PX[None, :] + PY[:, None] * PY[None, :])
+PUT = [5.0 + 4.0 * (tx * PX + ty * PY) for tx, ty in TARGETS]
+
+
+def constant_tables(length):
     k = np.arange(length)
     angle = 2.0 * math.pi * ((k[:, None] * k[None, :]) % length) / length
     table = (np.cos(angle) + np.sin(angle)) / math.sqrt(length)
@@ -57,7 +65,16 @@
     total[0, 0] = 1.0
     weight = 1.0 / total
     weight[0, 0] = 0.0
-    return np.stack([table, weight]).astype(np.float32)
+    small = np.zeros((length, length))
+    for part in range(2):
+        for which in range(2):
+            cols = slice(32 * which + 16 * part, 32 * which + 16 * part + 16)
+            small[16 * which : 16 * which + 16, cols] = TAKEN
+            small[32 + 2 * which, cols] = PUT[2 * which]
+            small[33 + 2 * which, cols] = PUT[2 * which + 1]
+        for i in range(8):
+            small[64 + i, 64 * part + 8 * i : 64 * part + 8 * i + 8] = 1.0
+    return np.stack([table, weight, small]).astype(np.float32)
 
 
 def split(x):
@@ -123,11 +140,9 @@
         between()
 
 
-def first_window(us, vs, r):
-    a = r - 1 + MARGIN
-    return jnp.concatenate(
-        [us[1, a : a + 4, :], vs[1, a : a + 4, :], jnp.zeros((8, N), f32)], axis=0
-    ).astype(bf16)
+def first_window(fields, r):
+    a = 4 * (r - 1 + MARGIN)
+    return jnp.concatenate([fields[0, a : a + 16, :], fields[1, a : a + 16, :]], axis=0).astype(bf16)
 
 
 def feature_window(feats, count, layer):
@@ -150,105 +165,138 @@
     return h + (f - f * h) * (2.0 * c + (6.0 * c * 0.044715) * zz)
 
 
-def spread_columns(u, v, us, vs):
-    for j in range(4):
-        us[j] = lanes(u, j - 1)
-        vs[j] = lanes(v, j - 1)
-
-
-def network_forward(count, us, vs, w_first, w_hidden, bias, feats, slopes, raw, raw_done):
+def network_forward(count, fields, w_first, w_hidden, bias, feats, slopes, raw, raw_done):
     for m in range(1, LAYERS + 1):
 
         def emit(r, o, m=m):
-            value, h, zz = gelu_value(fold(o) + bias[m - 1])
+            value, h, zz = gelu_value((o if m == 1 else fold(o)) + bias[m - 1])
             feats[feature_rows(count, m, r), :] = value.astype(bf16)
             if -m <= r < count + m:
                 slopes[gradient_rows(count, m, r), :] = gelu_slope(value, h, zz).astype(bf16)
 
         low, high = -reach(m), count + reach(m)
         if m == 1:
-            conv_rows(functools.partial(first_window, us, vs), w_first, low, high, emit)
+            conv_rows(functools.partial(first_window, fields), w_first, low, high, emit)
         else:
             conv_rows(feature_window(feats, count, m - 1), w_hidden.at[m - 2], low, high, emit)
 
     def emit_raw(r, o):
-        raw[(r + MID) * CH : (r + MID + 1) * CH, :] = fold(o) + bias[LAYERS]
-        raw_done(r)
+        value = fold(o) + bias[LAYERS]
+        raw[(r + MID) * CH : (r + MID + 1) * CH, :] = value
+        raw_done(r, value)
 
     conv_rows(
         feature_window(feats, count, LAYERS), w_hidden.at[LAYERS - 1], -RAW, count + RAW, emit_raw
     )
 
 
-TARGETS = ((0.0, -0.5), (-0.5, 0.0), (0.0, -0.5), (-0.5, 0.0))
-
-
-def moments(values):
-    cols = [values[j] + values[4 + j] + (values[8 + j] + values[12 + j]) for j in range(4)]
-    lines = [values[4 * i] + values[4 * i + 1] + (values[4 * i + 2] + values[4 * i + 3]) for i in range(4)]
-    mean = (cols[0] + cols[1] + (cols[2] + cols[3])) * (1.0 / 16.0)
-    mx = (1.5 * (cols[3] - cols[0]) + 0.5 * (cols[2] - cols[1])) * (1.0 / 20.0)
-    my = (1.5 * (lines[3] - lines[0]) + 0.5 * (lines[2] - lines[1])) * (1.0 / 20.0)
-    return mean, mx, my
-
-
-def less(values, mean, mx, my):
-    by_col = [mean + mx * (j - 1.5) for j in range(4)]
-    by_line = [my * (i - 1.5) for i in range(4)]
-    return [values[p] - (by_col[p % 4] + by_line[p // 4]) for p in range(16)]
-
-
-def total_of(terms):
-    while len(terms) > 1:
-        terms = [a + b for a, b in zip(terms[::2], terms[1::2])] + terms[len(terms) // 2 * 2 :]
-    return terms[0]
-
-
-def patches(src, q):
-    a = MARGIN - MID + 8 * q
-    return [src[p % 4, a + p // 4 - 1 : a + p // 4 + 7, :] for p in range(16)]
-
-
-def raw_rows(raw, k, q):
-    return [raw[pl.ds(8 * q * CH + k * 16 + p, 8, stride=CH), :] for p in range(16)]
-
-
-def eight(q):
-    return slice(8 * q, 8 * q + 8) if isinstance(q, int) else pl.ds(pl.multiple_of(8 * q, 8), 8)
-
-
-def interpolate(q, sources, raw, interp):
-    for which, src in enumerate(sources):
-        patch = patches(src, q)
-        mean, mx, my = moments(patch)
-        clear = less(patch, mean, mx, my)
-        for k in (2 * which, 2 * which + 1):
-            tx, ty = TARGETS[k]
-            value = total_of([a * b for a, b in zip(raw_rows(raw, k, q), clear)])
-            interp[k, 8 * q : 8 * q + 8, :] = value + (mean + (tx * mx if tx else ty * my))
-
-
-def raw_gradient(count, q, sources, ginterp, graw32, grads):
-    at = slice(8 * q, 8 * q + 8)
-    for which, src in enumerate(sources):
-        patch = patches(src, q)
-        clear = less(patch, *moments(patch))
-        for k in (2 * which, 2 * which + 1):
-            g = ginterp[k, at, :]
-            for p in range(16):
-                graw32[pl.ds(k * 16 + p, 8, stride=CH), :] = clear[p] * g
-    grads[gradient_rows(count, LAYERS + 1, 8 * q - MID, 8), :] = graw32[...].astype(bf16)
-
-
-def spread_back(q, which, raw, ginterp, lines):
-    k = 2 * which
-    at = eight(q)
-    g, h = ginterp[k, at, :], ginterp[k + 1, at, :]
-    values = [a * g + b * h for a, b in zip(raw_rows(raw, k, q), raw_rows(raw, k + 1, q))]
-    mean, mx, my = moments(values)
-    values = less(values, mean - (g + h) * (1.0 / 16.0), mx + h * (0.5 / 20.0), my + g * (0.5 / 20.0))
-    for i in range(4):
-        lines[which, i, at, :] = total_of([lanes(values[4 * i + j], 1 - j) for j in range(4)])
+def interleave(vel, fields):
+    for which in range(2):
+        x = vel[which]
+        for j in range(4):
+            fields[which, pl.ds(j, x.shape[0], stride=4), :] = lanes(x, j - 1)
+
+
+def mixed(pairs, mix):
+    cols = []
+    for u, v in pairs:
+        cols.append(jnp.concatenate([*split(u), *split(v)], axis=0))
+    o = jnp.dot(mix[...], jnp.concatenate(cols, axis=1), preferred_element_type=f32)
+    return [o[:, i * N : (i + 1) * N] * (1.0 / 80.0) for i in range(len(pairs))]
+
+
+def clear_patches(count, fields, mix, clear, put):
+    for r in range(-MID, count + MID, 2):
+        pairs = []
+        for k in range(2):
+            a = 4 * (r + k - 1 + MARGIN)
+            pairs.append((fields[0, a : a + 16, :], fields[1, a : a + 16, :]))
+        parts = mixed(pairs, mix)
+        for k, ((u, v), o) in enumerate(zip(pairs, parts)):
+            a = 32 * (r + k + MID)
+            clear[a : a + 16, :] = u - o[0:16]
+            clear[a + 16 : a + 32, :] = v - o[16:32]
+        a = 4 * (r + MID)
+        put[a : a + 8, :] = jnp.concatenate([parts[0][32:36], parts[1][32:36]], axis=0)
+
+
+def point_sums(r, value, clear):
+    a = 32 * (r + MID)
+    out = []
+    for k in range(4):
+        b = a + 16 * (k // 2)
+        x = value[16 * k : 16 * k + 16] * clear[b : b + 16, :]
+        out.append(x[:8] + x[8:])
+    return out
+
+
+def interpolate(r, sums, adder, put, interp):
+    cols = []
+    for i in range(0, len(sums), 2):
+        high, low = split(jnp.concatenate(sums[i] + sums[i + 1], axis=0))
+        cols.append(jnp.concatenate([high, low], axis=0))
+    o = jnp.dot(adder[...], jnp.concatenate(cols, axis=1), preferred_element_type=f32)
+    for i in range(len(cols)):
+        a = 4 * (r + 2 * i + MID)
+        interp[a : a + 8, :] = o[0:8, i * N : (i + 1) * N] + put[a : a + 8, :]
+
+
+def by_kind(interp, k, mid):
+    return interp[pl.ds(k, mid, stride=4), :]
+
+
+def raw_gradient(count, clear, ginterp, grads):
+    for r in range(-MID, count + MID):
+        a = 32 * (r + MID)
+        parts = []
+        for k in range(4):
+            b = a + 16 * (k // 2)
+            parts.append(clear[b : b + 16, :] * ginterp[k, r + MID : r + MID + 1, :])
+        grads[gradient_rows(count, LAYERS + 1, r), :] = jnp.concatenate(parts, axis=0).astype(bf16)
+
+
+def put_columns():
+    point = lax.broadcasted_iota(jnp.int32, (16, N), 0)
+    px, py = (point & 3).astype(f32) - 1.5, (point >> 2).astype(f32) - 1.5
+    return [(1.0 / 16.0) + (tx / 20.0) * px + (ty / 20.0) * py for tx, ty in TARGETS]
+
+
+def spread_back(r, at, columns, mix, raw, ginterp, spread):
+    pairs, gs = [], []
+    for k in range(2):
+        z = raw[at((r + k + MID) * CH, CH), :]
+        g = [ginterp[i, at(r + k + MID, 1), :] for i in range(4)]
+        x = [z[16 * i : 16 * i + 16] * g[i] for i in range(4)]
+        pairs.append((x[0] + x[1], x[2] + x[3]))
+        gs.append(g)
+    parts = mixed(pairs, mix)
+    for which in range(2):
+        out = []
+        for pair, o, g in zip(pairs, parts, gs):
+            back = columns[2 * which] * g[2 * which] + columns[2 * which + 1] * g[2 * which + 1]
+            out.append(pair[which] - o[16 * which : 16 * which + 16] + back)
+        for i in range(4):
+            spread[which, i, at(4 * (r + MID), 8), :] = jnp.concatenate(
+                [x[4 * i : 4 * i + 4] for x in out], axis=0
+            )
+
+
+def gathered_back(count, spread, lines):
+    out = []
+    for which in range(2):
+        for r in range(0, count, 2):
+            total = None
+            for i in range(4):
+                a = 4 * (r + 1 - i + MID)
+                x = spread[which, i, a : a + 8, :]
+                total = x if total is None else total + x
+            lines[which, 4 * r : 4 * r + 8, :] = total
+        total = None
+        for j in range(4):
+            x = lanes(lines[which, pl.ds(j, count, stride=4), :], 1 - j)
+            total = x if total is None else total + x
+        out.append(total)
+    return out
 
 
 def carriers(u, v):
@@ -265,7 +313,8 @@
 
 
 def provisional(count, u, v, interp):
-    flux = [middle(x, count) * interp[k] for k, x in enumerate(carriers(u, v))]
+    mid = count + 2 * MID
+    flux = [middle(x, count) * by_kind(interp, k, mid) for k, x in enumerate(carriers(u, v))]
     u, v = middle(u, count), middle(v, count)
     su = u - DT * (flux[0] - lanes(flux[0], -1) + (flux[1] - rows(flux[1], -1)))
     sv = v - DT * (flux[2] - lanes(flux[2], -1) + (flux[3] - rows(flux[3], -1)))
@@ -284,16 +333,15 @@
         ginterp[k] = g * middle(x, count)
 
 
-def velocity_gradients(count, gu, gv, interp, lines):
-    half = [0.5 * g * interp[k] for k, g in enumerate(flux_gradients(count, gu, gv))]
+def velocity_gradients(count, gu, gv, interp, spread, lines):
+    mid = count + 2 * MID
+    half = [0.5 * g * by_kind(interp, k, mid) for k, g in enumerate(flux_gradients(count, gu, gv))]
+    shares = gathered_back(count, spread, lines)
     out = []
     for which, g in enumerate((gu, gv)):
         along, across = half[which], half[2 + which]
         x = middle(g, count) + (along + lanes(along, -1)) + (across + rows(across, -1))
-        x = x[MID : MID + count]
-        for i in range(4):
-            x = x + lines[which, i, MID + 1 - i : MID + 1 - i + count, :]
-        out.append(x)
+        out.append(x[MID : MID + count] + shares[which])
     return out
 
 
@@ -328,17 +376,18 @@
     return x[: 3 * CH, : 3 * CH] + x[3 * CH :, CH:]
 
 
-def weight_product(count, m, us, vs, feats, grads):
+def weight_product(count, m, fields, feats, grads):
     starts = list(range(0, count, 2))
+    shifts = (0,) if isinstance(m, int) and m == 1 else (-1, 0, 1)
     left, total = [], None
     for r in starts:
         g = [grads[gradient_rows(count, m, r + k), :] for k in range(2)]
-        left.append(jnp.concatenate([lanes(x, -e) for x in g for e in (-1, 0, 1)], axis=0))
+        left.append(jnp.concatenate([lanes(x, -e) for x in g for e in shifts], axis=0))
         for x in g:
             x = x.astype(f32)
             total = x if total is None else total + x
     if isinstance(m, int) and m == 1:
-        right = [first_window(us, vs, r) for r in starts]
+        right = [first_window(fields, r) for r in starts]
     else:
         right = [feature_window(feats, count, m - 1)(r) for r in starts]
     out = lax.dot_general(
@@ -347,12 +396,12 @@
     return out, jnp.sum(total, axis=1, keepdims=True)
 
 
-def weight_gradients(count, us, vs, feats, grads, put, columns, loop):
+def weight_gradients(count, fields, feats, grads, put, columns, loop):
     lane = lax.broadcasted_iota(jnp.int32, (CH, N), 1)
 
     def pair_of(pair):
-        lower, a = weight_product(count, 2 + 2 * pair, us, vs, feats, grads)
-        upper, b = weight_product(count, 3 + 2 * pair, us, vs, feats, grads)
+        lower, a = weight_product(count, 2 + 2 * pair, fields, feats, grads)
+        upper, b = weight_product(count, 3 + 2 * pair, fields, feats, grads)
         x = jnp.where(lane == 33 + 2 * pair, a, columns[...])
         columns[...] = jnp.where(lane == 34 + 2 * pair, b, x)
         wide = jnp.concatenate([folded(lower), folded(upper)], axis=1)
@@ -365,50 +414,81 @@
     else:
         for pair in range(2, -1, -1):
             pair_of(pair)
-    first, total = weight_product(count, 1, us, vs, feats, grads)
+    first, total = weight_product(count, 1, fields, feats, grads)
     rest = jnp.where(lane == 32, total, columns[...])
-    first = jnp.concatenate([first[: 3 * CH], first[3 * CH :], jnp.zeros((3 * CH, N - 32), f32)], axis=1)
-    put(9, first + jnp.concatenate([rest, jnp.zeros((2 * CH, N), f32)], axis=0))
-
-
-def prepare_kernel(core, group, lengths, *refs):
-    own, f_first, f_hidden, b_first, b_hidden, bias, right, left, weight, flags = refs[9:19]
-    sems = refs[28]
-    copies = [pltpu.make_async_copy(refs[i], refs[19 + i], sems.at[i]) for i in range(9)]
+    first = jnp.concatenate([first, jnp.zeros((2 * CH, N - 32), f32)], axis=1)
+    put(9, jnp.concatenate([first[:CH] + rest, first[CH:], jnp.zeros((CH, N), f32)], axis=0))
+
+
+def fetch(sources, targets, sems):
+    copies = [pltpu.make_async_copy(a, b, sems.at[i]) for i, (a, b) in enumerate(zip(sources, targets))]
     for copy in copies:
         copy.start()
-    upper = core[0] == 0
-    for i in range(STEPS):
-        flags[i] = jnp.full((8, N), jnp.where(lengths[core[0]] > i, 1.0, 0.0), f32)
-    flags[STEPS] = jnp.full((8, N), jnp.where(upper, 1.0, 0.0), f32)
-    for bit in range(flags.shape[0] - STEPS - 1):
-        flags[STEPS + 1 + bit] = jnp.full((8, N), jnp.where((group[0] >> bit) & 1 == 1, 1.0, 0.0), f32)
+    return copies
+
+
+def tap_of(middle, last, m):
+    return (lambda a, e: last[3 * a + e]) if m == LAYERS - 1 else (lambda a, e: middle[m, 3 * a + e])
+
+
+def prepare_kernel(*refs):
+    own, f_first, f_hidden, bias, mix, adder, flags = refs[10:17]
+    vel, cot, first, first_bias, middle, middle_bias, last, last_bias, tables, lengths = refs[17:27]
+    copies = fetch(refs[:10], refs[17:27], refs[27])
+    core = lax.axis_index("strip") & 1
+    group = lax.axis_index("traj")
     for copy in copies:
         copy.wait()
-    vel, cot, first, first_bias, middle, middle_bias, last, last_bias, tables = refs[19:28]
-    own[0] = jnp.where(upper, vel[0], vel[1])
-    own[1] = jnp.where(upper, cot[0], cot[1])
+    for i in range(STEPS):
+        flags[i] = jnp.full((8, N), jnp.where(lengths[core] > i, 1.0, 0.0), f32)
+    flags[STEPS] = jnp.full((8, N), jnp.where(core == 0, 1.0, 0.0), f32)
+    for bit in range(flags.shape[0] - STEPS - 1):
+        flags[STEPS + 1 + bit] = jnp.full((8, N), jnp.where((group >> bit) & 1 == 1, 1.0, 0.0), f32)
+    own[0] = jnp.where(core == 0, vel[0], vel[1])
+    own[1] = jnp.where(core == 0, cot[0], cot[1])
     zero = jnp.zeros((CH, CH), bf16)
     for m in range(LAYERS):
-        tap = (lambda a, e: last[3 * a + e]) if m == LAYERS - 1 else (lambda a, e: middle[m, 3 * a + e])
+        tap = tap_of(middle, last, m)
         for two in range(2):
             for e in range(3):
-                at = slice((two * 3 + e) * CH, (two * 3 + e + 1) * CH)
                 taps = [tap(q - two, e) if 0 <= q - two < 3 else zero for q in range(4)]
-                f_hidden[m, at, :] = jnp.concatenate(taps, axis=1)
+                f_hidden[m, (two * 3 + e) * CH : (two * 3 + e + 1) * CH, :] = jnp.concatenate(taps, axis=1)
+    for two in range(2):
+        lines = []
+        for ch in range(2):
+            for i in range(4):
+                for j in range(4):
+                    if 0 <= i - two < 3 and j < 3:
+                        lines.append(first[3 * (i - two) + j, ch : ch + 1, :].astype(f32))
+                    else:
+                        lines.append(jnp.zeros((1, CH), f32))
+        f_first[two * CH : (two + 1) * CH, :] = jnp.concatenate(lines, axis=0).T.astype(bf16)
+    for m in range(LAYERS + 1):
+        if 0 < m < LAYERS:
+            line = middle_bias[m - 1 : m, :]
+        else:
+            line = (first_bias if m == 0 else last_bias)[...].reshape(1, CH)
+        bias[m] = jnp.broadcast_to(line, (N, CH)).T
+    mix[...] = tables[2, 0:48, 0:64].astype(bf16)
+    adder[...] = tables[2, 64:80, :].astype(bf16)
+
+
+def prepare_back_kernel(*refs):
+    b_first, b_hidden, right, left, weight = refs[5:10]
+    first, middle, last, tables = refs[10:14]
+    copies = fetch(refs[:4], refs[10:14], refs[14])
+    for copy in copies:
+        copy.wait()
+    zero = jnp.zeros((CH, CH), bf16)
+    for m in range(LAYERS):
+        tap = tap_of(middle, last, m)
+        for two in range(2):
+            for e in range(3):
                 taps = [tap(2 - q + two, 2 - e) if 0 <= q - two < 3 else zero for q in range(4)]
-                b_hidden[m, at, :] = jnp.concatenate(
+                b_hidden[m, (two * 3 + e) * CH : (two * 3 + e + 1) * CH, :] = jnp.concatenate(
                     [jnp.concatenate(taps[:2], axis=0).T, jnp.concatenate(taps[2:], axis=0).T], axis=1
                 )
     lines = jnp.zeros((1, CH), f32)
-    for two in range(2):
-        for e in range(3):
-            taps = [lines] * 16
-            for a in range(3):
-                for ch in range(2):
-                    taps[4 * ch + a + two] = first[3 * a + e, ch : ch + 1, :].astype(f32)
-            at = slice((two * 3 + e) * CH, (two * 3 + e + 1) * CH)
-            f_first[at, :] = jnp.concatenate(taps, axis=0).T.astype(bf16)
     taps = []
     for e in range(3):
         for ch in range(2):
@@ -420,12 +500,6 @@
                 taps.append(jnp.concatenate(line, axis=1))
     taps.append(jnp.zeros((4, 4 * CH), f32))
     b_first[...] = jnp.concatenate(taps, axis=0).astype(bf16)
-    for m in range(LAYERS + 1):
-        if 0 < m < LAYERS:
-            line = middle_bias[m - 1 : m, :]
-        else:
-            line = (first_bias if m == 0 else last_bias)[...].reshape(1, CH)
-        bias[m] = jnp.broadcast_to(line, (N, CH)).T
     high, low = split(tables[0])
     right[...] = jnp.concatenate([high, high, low], axis=0)
     left[...] = jnp.concatenate([high, low, high], axis=1)
@@ -451,19 +525,23 @@
         cot[i] = jnp.concatenate(pair(own[1], cot_partner, i), axis=0)
 
 
-def network_kernel(count, vel, extra, w_first, w_hidden, bias, block, interp, raw, feats, slopes, us, vs):
-    u, v = vel[0], vel[1]
-    spread_columns(u, v, us, vs)
-
-    def raw_done(r):
-        at = r + 1 + MID
-        if at % 8 == 0:
-            interpolate(at // 8 - 1, (us, vs), raw, interp)
-        elif r + 1 == count + RAW:
-            interpolate(at // 8, (us, vs), raw, interp)
-
-    network_forward(count, us, vs, w_first, w_hidden, bias, feats, slopes, raw, raw_done)
-    su, sv = provisional(count, u, v, interp)
+def network_kernel(
+    count, vel, extra, w_first, w_hidden, bias, mix, adder, block, interp, raw, clear, fields, feats, slopes, put
+):
+    interleave(vel, fields)
+    clear_patches(count, fields, mix, clear, put)
+    sums = []
+
+    def raw_done(r, value):
+        sums.append(point_sums(r, value, clear))
+        if len(sums) == 4 * LAG + 4:
+            interpolate(r + 1 - len(sums), sums[:4], adder, put, interp)
+            del sums[:4]
+
+    network_forward(count, fields, w_first, w_hidden, bias, feats, slopes, raw, raw_done)
+    for i in range(0, len(sums), 4):
+        interpolate(count + RAW - len(sums) + i, sums[i : i + 4], adder, put, interp)
+    su, sv = provisional(count, vel[0], vel[1], interp)
     block[0] = su
     block[1] = sv
     block[2] = extra[0]
@@ -489,26 +567,27 @@
         own[2 + i] = (1.0 - mg) * gathered[0][2 + i]
 
 
-def back_kernel(count, ext, gstar, b_first, b_hidden, slopes, *refs):
-    if len(refs) == 8:
-        raw, grads, gvel, lines, us, vs, graw32, ginterp = refs
+def static(start, size):
+    return slice(start, start + size)
+
+
+def back_kernel(count, ext, gstar, clear, b_first, b_hidden, slopes, *refs):
+    if len(refs) == 6:
+        mix, raw, grads, gvel, spread, ginterp = refs
     else:
-        raw, lines = None, None
-        grads, gvel, us, vs, graw32, ginterp = refs
-    u, v = ext[0], ext[1]
-    spread_columns(u, v, us, vs)
-    interp_gradients(count, gstar[0], gstar[1], u, v, ginterp)
-    chunks = (count + 2 * MID) // 8
-    for q in range(chunks):
-        raw_gradient(count, q, (us, vs), ginterp, graw32, grads)
+        grads, gvel, ginterp = refs
+    interp_gradients(count, gstar[0], gstar[1], ext[0], ext[1], ginterp)
+    raw_gradient(count, clear, ginterp, grads)
     tasks = []
-    if raw is not None:
-        tasks = [functools.partial(spread_back, q, w, raw, ginterp, lines) for q in range(chunks) for w in range(2)]
+    if len(refs) == 6:
+        columns = put_columns()
+        for r in range(-RAW, count + RAW, 2):
+            tasks.append(functools.partial(spread_back, r, static, columns, mix, raw, ginterp, spread))
     turn = [0]
 
     def between():
         turn[0] += 1
-        if tasks and turn[0] % 4 == 0:
+        if tasks and turn[0] % 3 == 0:
             tasks.pop(0)()
 
     network_backward(count, b_hidden, slopes, grads, between)
@@ -518,34 +597,37 @@
 
 
 def finish_kernel(count, front, base, ext, gstar, interp, gvel, *refs):
-    raw, out, lines, ginterp = refs if len(refs) == 4 else (None, refs[1], refs[0], None)
     gu, gv = gstar[0], gstar[1]
-    if raw is not None:
+    if len(refs) == 3:
+        spread, out, lines = refs
+    else:
+        mix, raw, out, lines, spread, ginterp = refs
         interp_gradients(count, gu, gv, ext[0], ext[1], ginterp)
-
-        def step(q, _):
-            for which in range(2):
-                spread_back(q, which, raw, ginterp, lines)
+        columns = put_columns()
+
+        def at(start, size):
+            return pl.ds(pl.multiple_of(start, size), size) if size > 1 else pl.ds(start, size)
+
+        def step(i, _):
+            for k in range(2):
+                spread_back(4 * i + 2 * k - RAW, at, columns, mix, raw, ginterp, spread)
             return 0
 
-        lax.fori_loop(0, (count + 2 * MID) // 8, step, 0)
-    change = velocity_gradients(count, gu, gv, interp, lines)
+        lax.fori_loop(0, (count + 2 * RAW) // 4, step, 0)
+    change = velocity_gradients(count, gu, gv, interp, spread, lines)
     for i in range(2):
         out[i] = front[i]
         out[2 + i] = base[2 + i] + change[i] + gvel[i]
 
 
-def weights_kernel(count, ext, feats, grads, buffer, columns, us, vs):
-    spread_columns(ext[0], ext[1], us, vs)
-
+def weights_kernel(count, fields, feats, grads, buffer, columns):
     def put(block, value):
         buffer[place(block * 3 * CH, 3 * CH), :] = value
 
-    weight_gradients(count, us, vs, feats, grads, put, columns, True)
-
-
-def total_weights_kernel(count, flags, previous, ext, feats, grads, keep, send, columns, us, vs, total):
-    spread_columns(ext[0], ext[1], us, vs)
+    weight_gradients(count, fields, feats, grads, put, columns, True)
+
+
+def total_weights_kernel(count, flags, previous, fields, feats, grads, keep, send, columns, total):
     half = keep.shape[0]
 
     def put(block, value):
@@ -554,7 +636,7 @@
 
     if 2 * half > BUFFER:
         total[BUFFER:, :] = jnp.zeros((2 * half - BUFFER, N), f32)
-    weight_gradients(count, us, vs, feats, grads, put, columns, False)
+    weight_gradients(count, fields, feats, grads, put, columns, False)
     for low in range(0, half, 3 * CH):
         high = min(low + 3 * CH, half)
         a, b = total[low:high, :], total[half + low : half + high, :]
@@ -612,12 +694,12 @@
                     else:
                         last[3 * a + e] = value
     rest = block(9)
-    turned = [rest[e * CH : (e + 1) * CH].T for e in range(3)]
+    turned = [rest[two * CH : (two + 1) * CH].T for two in range(2)]
     for a in range(3):
         for e in range(3):
             for ch in range(2):
-                low, high = 4 * ch + a, 16 + 4 * ch + a + 1
-                first[3 * a + e, ch : ch + 1, :] = turned[e][low : low + 1] + turned[e][high : high + 1]
+                low, high = 16 * ch + 4 * a + e, 16 * ch + 4 * (a + 1) + e
+                first[3 * a + e, ch : ch + 1, :] = turned[0][low : low + 1] + turned[1][high : high + 1]
     turned = turned[0]
     first_bias[...] = turned[32]
     middle_bias[...] = turned[33 : 33 + LAYERS - 1]
@@ -662,33 +744,49 @@
     )(*inputs)
 
 
-def run_prepare(core, group, lengths, vel, cot, params, bits):
-    rc = vel.shape[2]
+def run_prepare(lengths, vel, cot, params, bits):
     out = [
-        array(f32, 2, 2, rc, N),
-        array(bf16, 6 * CH, 16),
+        array(f32, 2, 2, vel.shape[2], N),
+        array(bf16, 2 * CH, 32),
         array(bf16, LAYERS, 6 * CH, 4 * CH),
+        array(f32, LAYERS + 1, CH, N),
+        array(bf16, 48, 64),
+        array(bf16, 16, N),
+        array(f32, STEPS + 1 + bits, 8, N),
+    ]
+    inputs = [vel, cot, *params, jnp.asarray(constant_tables(N)), lengths]
+    scratch = [pltpu.VMEM(x.shape, x.dtype) for x in inputs[:-1]] + [pltpu.SMEM(lengths.shape, lengths.dtype)]
+    return call_from_hbm(prepare_kernel, "prepare", inputs, out, scratch)
+
+
+def run_prepare_back(params, after):
+    first, _, middle, _, last, _ = params
+    out = [
         array(bf16, 16, 4 * CH),
         array(bf16, LAYERS, 6 * CH, 4 * CH),
-        array(f32, LAYERS + 1, CH, N),
         array(bf16, 3 * N, N),
         array(bf16, N, 3 * N),
         array(f32, N, N),
-        array(f32, STEPS + 1 + bits, 8, N),
     ]
-    inputs = [vel, cot, *params, jnp.asarray(poisson_tables(N))]
+    inputs = [first, middle, last, jnp.asarray(constant_tables(N))]
+    scratch = [pltpu.VMEM(x.shape, x.dtype) for x in inputs]
+    b_first, b_hidden, *tables = call_from_hbm(prepare_back_kernel, "prepare_back", inputs, out, scratch, after)
+    return b_first, b_hidden, tables
+
+
+def call_from_hbm(kernel, name, inputs, out, scratch, *after):
+    hbm = pl.BlockSpec(memory_space=pltpu.HBM)
     inputs = [pltpu.with_memory_space_constraint(x, pltpu.HBM) for x in inputs]
     return pl.pallas_call(
-        prepare_kernel,
-        in_specs=[SMEM] * 3 + [pl.BlockSpec(memory_space=pltpu.HBM)] * len(inputs),
+        kernel,
+        in_specs=[hbm] * len(inputs) + [VMEM] * len(after),
         out_specs=[VMEM] * len(out),
         out_shape=out,
-        scratch_shapes=[pltpu.VMEM(x.shape, x.dtype) for x in inputs]
-        + [pltpu.SemaphoreType.DMA((len(inputs),))],
+        scratch_shapes=scratch + [pltpu.SemaphoreType.DMA((len(inputs),))],
         compiler_params=PARAMS,
         cost_estimate=cost(10**9, 10**6),
-        name="prepare",
-    )(core, group, lengths, *inputs)
+        name=name,
+    )(*inputs, *after)
 
 
 def run_assemble(count, flags, fields):
@@ -698,9 +796,10 @@
 
 def run_network(count, vel, extra, weights):
     local_rows, mid = count + 2 * MARGIN, count + 2 * MID
-    out = [array(f32, 4, count, N), array(f32, 4, mid, N), array(f32, mid * CH, N)]
+    out = [array(f32, 4, count, N), array(f32, 4 * mid, N), array(f32, mid * CH, N), array(f32, mid * 32, N)]
+    out += [array(f32, 2, 4 * local_rows, N)]
     out += [feature_array(count), gradient_array(count, LAYERS)]
-    scratch = [field(local_rows, 4), field(local_rows, 4)]
+    scratch = [field(4 * mid)]
     return call(functools.partial(network_kernel, count), "network", 4 * 10**9, [vel, extra, *weights], out, scratch)
 
 
@@ -713,33 +812,33 @@
     return call(kernel, "project", 10**9, [flags, *gathered, vel, *tables], out)
 
 
-def run_back(count, ext, gstar, b_first, b_hidden, slopes, raw=None):
-    local_rows, mid = count + 2 * MARGIN, count + 2 * MID
-    inputs = [ext, gstar, b_first, b_hidden, slopes]
+def run_back(count, ext, gstar, clear, b_first, b_hidden, slopes, *more):
+    mid = count + 2 * MID
+    inputs = [ext, gstar, clear, b_first, b_hidden, slopes, *more]
     out = [gradient_array(count, LAYERS + 1), array(f32, 2, count, N)]
-    if raw is not None:
-        inputs.append(raw)
-        out.append(array(f32, 2, 4, mid, N))
-    scratch = [field(local_rows, 4), field(local_rows, 4), field(8 * CH), field(mid, 4)]
-    return call(functools.partial(back_kernel, count), "back", 4 * 10**9, inputs, out, scratch)
-
-
-def run_finish(count, front, base, ext, gstar, interp, gvel, raw=None, lines=None):
+    if more:
+        out.append(array(f32, 2, 4, 4 * mid, N))
+    return call(functools.partial(back_kernel, count), "back", 4 * 10**9, inputs, out, [field(mid, 4)])
+
+
+def run_finish(count, front, base, ext, gstar, interp, gvel, *more):
     mid = count + 2 * MID
-    inputs = [front, base, ext, gstar, interp, gvel, lines if raw is None else raw]
-    scratch = [] if raw is None else [field(mid, 2, 4), field(mid, 4)]
+    inputs = [front, base, ext, gstar, interp, gvel, *more]
+    scratch = [field(4 * count, 2)]
+    if len(more) > 1:
+        scratch += [field(4 * mid, 2, 4), field(mid, 4)]
     return call(functools.partial(finish_kernel, count), "finish", 10**9, inputs, array(f32, 4, count, N), scratch)
 
 
-def run_weights(count, ext, feats, grads):
-    scratch = [field(CH)] + [field(count + 2 * MARGIN, 4)] * 2
+def run_weights(count, fields, feats, grads):
+    scratch = [field(CH)]
     kernel = functools.partial(weights_kernel, count)
-    return call(kernel, "weights", 3 * 10**9, [ext, feats, grads], array(f32, BUFFER, N), scratch)
-
-
-def run_total_weights(count, half, flags, previous, ext, feats, grads):
-    scratch = [field(CH)] + [field(count + 2 * MARGIN, 4)] * 2 + [field(2 * half)]
-    inputs = [flags, previous, ext, feats, grads]
+    return call(kernel, "weights", 3 * 10**9, [fields, feats, grads], array(f32, BUFFER, N), scratch)
+
+
+def run_total_weights(count, half, flags, previous, fields, feats, grads):
+    scratch = [field(CH), field(2 * half)]
+    inputs = [flags, previous, fields, feats, grads]
     kernel = functools.partial(total_weights_kernel, count)
     return call(kernel, "total_weights", 3 * 10**9, inputs, [array(bf16, half, N)] * 2, scratch)
 
@@ -828,25 +927,25 @@
     params = (first_kernel, first_bias, middle_kernels, middle_biases, last_kernel, last_bias)
     parts = lax.axis_size("traj")
     half = -(-BUFFER // (2 * parts * 16)) * parts * 16
-    group = lax.axis_index("traj")[None]
-    own, w_first, w_hidden, b_first, b_hidden, bias, *tables, flags = run_prepare(
-        core, group, lengths, velocity, cotangent, params, parts.bit_length() - 1
+    own, w_first, w_hidden, bias, mix, adder, flags = run_prepare(
+        lengths, velocity, cotangent, params, parts.bit_length() - 1
     )
-    weights = (w_first, w_hidden, bias)
+    weights = (w_first, w_hidden, bias, mix, adder)
 
     v0, cot = run_assemble(count, flags, (own, partner, cross, same, cot_partner))
-    block, interp0, raw0, feats0, slopes0 = run_network(count, v0, cot, weights)
+    block, interp0, raw0, clear0, fields0, feats0, slopes0 = run_network(count, v0, cot, weights)
     gathered = gather_groups(block)
+    b_first, b_hidden, tables = run_prepare_back(params, interp0)
     gstar1, base, v1 = run_project(count, (0, 1), flags, gathered, v0, tables)
-    block, interp1, raw1, feats1, slopes1 = run_network(count, v1, cot, weights)
-    grads1, gvel, lines = run_back(count, v1, gstar1, b_first, b_hidden, slopes1, raw1)
-    block = run_finish(count, block, base, v1, gstar1, interp1, gvel, lines=lines)
+    block, interp1, raw1, clear1, fields1, feats1, slopes1 = run_network(count, v1, cot, weights)
+    grads1, gvel, spread = run_back(count, v1, gstar1, clear1, b_first, b_hidden, slopes1, mix, raw1)
+    block = run_finish(count, block, base, v1, gstar1, interp1, gvel, spread)
     gathered = gather_groups(block)
-    buffer = run_weights(count, v1, feats1, grads1)
+    buffer = run_weights(count, fields1, feats1, grads1)
     gstar0, base = run_project(count, (1, 0), flags, gathered, v1, tables, last=True)
-    grads0, gvel = run_back(count, v0, gstar0, b_first, b_hidden, slopes0)
-    keep, send = run_total_weights(count, half, flags, buffer, v0, feats0, grads0)
-    out = run_finish(count, base, base, v0, gstar0, interp0, gvel, raw=raw0)
+    grads0, gvel = run_back(count, v0, gstar0, clear0, b_first, b_hidden, slopes0)
+    keep, send = run_total_weights(count, half, flags, buffer, fields0, feats0, grads0)
+    out = run_finish(count, base, base, v0, gstar0, interp0, gvel, mix, raw0)
 
     strips = out.reshape(4, 2, rc, N).transpose(1, 0, 2, 3)
     mine, other = pick(strips, index)[None], swap(pick(strips, 1 - index), "strip", 1)[None]

time: 88.6 us -> 83.5 us (0.942)
  Pallas kernels: 44.2 us -> 40.1 us
  waiting for transfers between devices: 19.1 us -> 17.6 us
  starting transfers between devices: 22.9 us -> 24 us
    pallas_call x14, Pallas kernels: 41.2 us -> 36.4 us  [call(): pl.pallas_call(kernel, in_specs=[VMEM] * len(inputs), out_specs=jax.tree....]
    ppermute x6, waiting for transfers between devices: 7.67 us -> 4.34 us  [from_group(): lax.ppermute(x, 'strip', [(i, (i - 2 * ahead) % count) for i in range(cou...]
    ppermute x1, waiting for transfers between devices: 0.09 us -> 1.82 us  [margins(): lax.ppermute(velocity, 'strip', same)]
    ppermute x6, starting transfers between devices: 5.56 us -> 6.66 us  [from_group(): lax.ppermute(x, 'strip', [(i, (i - 2 * ahead) % count) for i in range(cou...]
    pallas_call x1 -> x2, Pallas kernels: 2.9 us -> 3.69 us  [call_from_hbm(): pl.pallas_call(kernel, in_specs=[hbm] * len(inputs) + [VMEM] * len(after)...]
  transfers between devices with their start and end apart: 22 -> 22, of which waited for: 14 -> 13; matrix products, arithmetic and copies ran while one was open for 1% -> 1% of each run, Pallas kernels for 10% -> 11%
where the time goes in v2:
time: 83.5 us; the launch traced here: 83.3 us
  Pallas kernels  40.1 us (48%)
  starting transfers between devices  24 us (29%)
  waiting for transfers between devices  17.6 us (21%)
    pallas_call x14, Pallas kernels, call(): pl.pallas_call(kernel, in_specs=[VMEM] * len(inputs), out_specs=jax.tree....  36.4 us
    ppermute x14, starting transfers between devices, swap(): return lax.ppermute(x, axis, [(i, i ^ offset) for i in range(count)])  12.2 us
    ppermute x14, waiting for transfers between devices, swap(): return lax.ppermute(x, axis, [(i, i ^ offset) for i in range(count)])  11.5 us
    ppermute x6, starting transfers between devices, from_group(): lax.ppermute(x, 'strip', [(i, (i - 2 * ahead) % count) for i in range(cou...  6.66 us
    ppermute x1, starting transfers between devices, margins(): lax.ppermute(velocity, 'strip', cross)  4.71 us
    ppermute x6, waiting for transfers between devices, from_group(): lax.ppermute(x, 'strip', [(i, (i - 2 * ahead) % count) for i in range(cou...  4.34 us
    pallas_call x2, Pallas kernels, call_from_hbm(): pl.pallas_call(kernel, in_specs=[hbm] * len(inputs) + [VMEM] * len(after)...  3.69 us
    ppermute x1, waiting for transfers between devices, margins(): lax.ppermute(velocity, 'strip', same)  1.82 us
  transfers between devices with their start and end apart: 22, of which 13 were waited for; matrix products, arithmetic and copies ran while one was open for 1% of the time, Pallas kernels for 11%

profile of v2, /device:TPU:0, one launch (start us, length us, event | category | flops | bytes accessed | tf_op | source)
XLA Modules:
  0.0 83.3 jit_solution(11925788600203426401)
XLA Ops:
  1.2 4.7 %collective-permute-start.1 = (f32[2,2,16,128]{3,2,1,0:T(8,128)}, f32[2,2,16,128]{3,2,1,0:T(8,128)S(1)}, u32[]{:S(2)}, u32[]{:S(2)}) collective-permute-start(f32[2,2,16,128]{3,2,1,0:T(8,128)} %refs_0_.1), channel_id=1, source_target_pairs={{0,7},{1,2},{2,1},{3,4},{4,3},{5,6},{6,5},{7,0},{8,15},{9,10},{10,... | collective-permute-start | bytes 98312 | tf_op jit(solution)/shard_map/ppermute | solution.py:895
  6.3 1.8 %prepare.1 = (f32[2,2,16,128]{3,2,1,0:T(8,128)S(1)}, bf16[128,32]{1,0:T(8,128)(2,1)S(1)}, bf16[6,384,256]{2,1,0:T(8,128)(2,1)S(1)}, f32[7,64,128]{2,1,0:T(8,128)...) custom-call(f32[2,2,16,128]{3,2,1,0:T(8,128)} %refs_0_.1, ...), custom_call_target="tpu_custom_call" | custom-call | flops 1000000000 | bytes 1000000 | tf_op jit(solution)/shard_map/prepare/pallas_call | solution.py:780
  8.2 1.8 %collective-permute-done.2.same = f32[2,2,16,128]{3,2,1,0:T(8,128)S(1)} collective-permute-done((f32[2,2,16,128]{3,2,1,0:T(8,128)}, f32[2,2,16,128]{3,2,1,0:T(8,128)S(1)}, u32[]{:S(2)}, u32[]{:S(2)}) %collective-permute-start.2) | collective-permute-done | bytes 32800 | tf_op jit(solution)/shard_map/ppermute | solution.py:895
  10.0 7.9 %network.2 = (f32[4,32,128]{2,1,0:T(8,128)S(1)}, f32[192,128]{1,0:T(8,128)S(1)}, f32[3072,128]{1,0:T(8,128)S(1)}, f32[1536,128]{1,0:T(8,128)S(1)}, f32[2,256,128...) custom-call(f32[2,64,128]{2,1,0:T(8,128)S(1)} %get-tuple-element.60.vel.refs_4_.ext, ...), custom_call_target="tpu_custom_call" | custom-call | flops 4000000000 | bytes 1000000 | tf_op jit(solution)/shard_map/network/pallas_call | solution.py:735
  17.9 2.2 %collective-permute-start.4 = (f32[4,32,128]{2,1,0:T(8,128)S(1)}, f32[4,32,128]{2,1,0:T(8,128)S(1)}, u32[]{:S(2)}, u32[]{:S(2)}) collective-permute-start(f32[4,32,128]{2,1,0:T(8,128)S(1)} %get-tuple-element.67.refs_0_), channel_id=1, source_target_pairs={{0,6},{1,7},{2,0},{3,1},{4,2},{5,3},{6,4},{7,5},{8,14},{9,15},{10,... | collective-permute-start | bytes 196616 | tf_op jit(solution)/shard_map/ppermute | solution.py:875
  20.8 1.9 %prepare_back.1 = (bf16[16,256]{1,0:T(8,128)(2,1)S(1)}, bf16[6,384,256]{2,1,0:T(8,128)(2,1)S(1)}, bf16[384,128]{1,0:T(8,128)(2,1)S(1)}, bf16[128,384]{1,0:T(8,128)(2,1)S(1)}, f32[128,128]{1,0:T(8,128)S(1)}) custom-call(bf16[9,2,64]{2,1,0:T(2,128)(2,1)} %bitcast.12, bf16[5,9,64,64]{3,2,1,0:T(8,128)(2,1)} %refs_1_.3, bf16[9,64,64]{2,1,0:T(8,128)(2,1)} %refs_2_.1, ...), custom_call_target="tpu_custom_call" | custom-call | flops 1000000000 | bytes 1000000 | tf_op jit(solution)/shard_map/prepare_back/pallas_call | solution.py:780
  22.7 3.8 %collective-permute-done.5.refs_2_ = f32[4,32,128]{2,1,0:T(8,128)S(1)} collective-permute-done((f32[4,32,128]{2,1,0:T(8,128)S(1)}, f32[4,32,128]{2,1,0:T(8,128)S(1)}, u32[]{:S(2)}, u32[]{:S(2)}) %collective-permute-start.5) | collective-permute-done | bytes 65568 | tf_op jit(solution)/shard_map/ppermute | solution.py:875
  27.4 7.9 %network.3 = (f32[4,32,128]{2,1,0:T(8,128)S(1)}, f32[192,128]{1,0:T(8,128)S(1)}, f32[3072,128]{1,0:T(8,128)S(1)}, f32[1536,128]{1,0:T(8,128)S(1)}, f32[2,256,128...) custom-call(f32[2,64,128]{2,1,0:T(8,128)S(1)} %get-tuple-element.72.vel.ext.refs_4_, ...), custom_call_target="tpu_custom_call" | custom-call | flops 4000000000 | bytes 1000000 | tf_op jit(solution)/shard_map/network/pallas_call | solution.py:735
  35.3 4.4 %back.2 = (bf16[21504,128]{1,0:T(8,128)(2,1)S(1)}, f32[2,32,128]{2,1,0:T(8,128)S(1)}, f32[2,4,192,128]{3,2,1,0:T(8,128)S(1)}) custom-call(f32[2,64,128]{2,1,0:T(8,128)S(1)} %get-tuple-element.72.vel.ext.refs_4_, f32[2,64,128]{2,1,0:T(8,128)S(1)} %get-tuple-element.75.gstar, f32[1536,128]{1,0:T(8,128)S(1)} %get-tuple-element.77.clear, ...), custom_call_target="tpu_custom_call" | custom-call | flops 4000000000 | bytes 1000000 | tf_op jit(solution)/shard_map/back/pallas_call | solution.py:735
  39.8 1.9 %collective-permute-start.7 = (f32[4,32,128]{2,1,0:T(8,128)S(1)}, f32[4,32,128]{2,1,0:T(8,128)S(1)}, u32[]{:S(2)}, u32[]{:S(2)}) collective-permute-start(f32[4,32,128]{2,1,0:T(8,128)S(1)} %finish.2.refs_0_), channel_id=1, source_target_pairs={{0,6},{1,7},{2,0},{3,1},{4,2},{5,3},{6,4},{7,5},{8,14},{9,15},{10,... | collective-permute-start | bytes 196616 | tf_op jit(solution)/shard_map/ppermute | solution.py:875
  41.8 1.9 %collective-permute-start.9 = (f32[4,32,128]{2,1,0:T(8,128)S(1)}, f32[4,32,128]{2,1,0:T(8,128)S(1)}, u32[]{:S(2)}, u32[]{:S(2)}) collective-permute-start(f32[4,32,128]{2,1,0:T(8,128)S(1)} %finish.2.refs_0_), channel_id=1, source_target_pairs={{0,2},{1,3},{2,4},{3,5},{4,6},{5,7},{6,0},{7,1},{8,10},{9,11},{10,... | collective-permute-start | bytes 196616 | tf_op jit(solution)/shard_map/ppermute | solution.py:875
  43.6 4.0 %weights.1.previous = f32[1920,128]{1,0:T(8,128)S(1)} custom-call(f32[2,256,128]{2,1,0:T(8,128)S(1)} %get-tuple-element.90.fields, bf16[21504,128]{1,0:T(8,128)(2,1)S(1)} %get-tuple-element.91.feats, bf16[21504,128]{1,0:T(8,128)(2,1)S(1)} %get-tuple-element.92.grads), custom_call_target="tpu_custom_call" | custom-call | flops 3000000000 | bytes 1000000 | tf_op jit(solution)/shard_map/weights/pallas_call | solution.py:735
  49.1 4.0 %back.3 = (bf16[21504,128]{1,0:T(8,128)(2,1)S(1)}, f32[2,32,128]{2,1,0:T(8,128)S(1)}) custom-call(f32[2,64,128]{2,1,0:T(8,128)S(1)} %get-tuple-element.60.vel.refs_4_.ext, f32[2,64,128]{2,1,0:T(8,128)S(1)} %get-tuple-element.85.gstar, f32[1536,128]{1,0:T(8,128)S(1)} %get-tuple-element.86.clear, bf16[16,256]{1,0:T(8,128)(2,1)S(1)} %get-tuple-element.78.b_first, ...), custom_call_target="tpu_custom_call" | custom-call | flops 4000000000 | bytes 1000000 | tf_op jit(solution)/shard_map/back/pallas_call | solution.py:735
  53.1 3.1 %total_weights.1 = (bf16[960,128]{1,0:T(8,128)(2,1)S(1)}, bf16[960,128]{1,0:T(8,128)(2,1)S(1)}) custom-call(f32[5,8,128]{2,1,0:T(8,128)S(1)} %get-tuple-element.58.flags, f32[1920,128]{1,0:T(8,128)S(1)} %weights.1.previous, f32[2,256,128]{2,1,0:T(8,128)S(1)} %get-tuple-element.93.fields, bf16[21504,128]{1,0:T(8,128)(2,1)S(1)} %get-tuple-element.94.feats, ...), custom_call_target="tpu_custom_call" | custom-call | flops 3000000000 | bytes 1000000 | tf_op jit(solution)/shard_map/total_weights/pallas_call | solution.py:735
  56.2 1.5 %collective-permute-done.11.received = bf16[960,128]{1,0:T(8,128)(2,1)S(1)} collective-permute-done((bf16[960,128]{1,0:T(8,128)(2,1)S(1)}, bf16[960,128]{1,0:T(8,128)(2,1)S(1)}, u32[]{:S(2)}, u32[]{:S(2)}) %collective-permute-start.11) | collective-permute-done | bytes 245792 | tf_op jit(solution)/shard_map/ppermute | solution.py:870
  57.8 2.5 %collective-permute-start.14 = (bf16[240,128]{1,0:T(8,128)(2,1)S(1)}, bf16[240,128]{1,0:T(8,128)(2,1)S(1)}, u32[]{:S(2)}, u32[]{:S(2)}) collective-permute-start(bf16[240,128]{1,0:T(8,128)(2,1)S(1)} %get-tuple-element.101), channel_id=1, source_target_pairs={{0,24},{8,16},{16,8},{24,0},{1,25},{9,17},{17,9},{25,1},{2,26},{10... | collective-permute-start | bytes 184328 | tf_op jit(solution)/shard_map/ppermute | solution.py:870
  61.4 1.7 %collective-permute-done.14 = bf16[240,128]{1,0:T(8,128)(2,1)S(1)} collective-permute-done((bf16[240,128]{1,0:T(8,128)(2,1)S(1)}, bf16[240,128]{1,0:T(8,128)(2,1)S(1)}, u32[]{:S(2)}, u32[]{:S(2)}) %collective-permute-start.14) | collective-permute-done | bytes 61472 | tf_op jit(solution)/shard_map/ppermute | solution.py:870
  63.1 1.5 %collective-permute-done.13 = bf16[240,128]{1,0:T(8,128)(2,1)S(1)} collective-permute-done((bf16[240,128]{1,0:T(8,128)(2,1)S(1)}, bf16[240,128]{1,0:T(8,128)(2,1)S(1)}, u32[]{:S(2)}, u32[]{:S(2)}) %collective-permute-start.13) | collective-permute-done | bytes 61472 | tf_op jit(solution)/shard_map/ppermute | solution.py:870
  65.1 1.7 %collective-permute-start.17 = (bf16[240,128]{1,0:T(8,128)(2,1)S(1)}, bf16[240,128]{1,0:T(8,128)(2,1)S(1)}, u32[]{:S(2)}, u32[]{:S(2)}) collective-permute-start(bf16[240,128]{1,0:T(8,128)(2,1)S(1)} %add_convert_fusion.1), channel_id=1, source_target_pairs={{0,6},{1,7},{2,4},{3,5},{4,2},{5,3},{6,0},{7,1},{8,14},{9,15},{10,... | collective-permute-start | bytes 184328 | tf_op jit(solution)/shard_map/ppermute | solution.py:870
  67.8 1.8 %collective-permute-start.15 = (bf16[240,128]{1,0:T(8,128)(2,1)S(1)}, bf16[240,128]{1,0:T(8,128)(2,1)S(1)}, u32[]{:S(2)}, u32[]{:S(2)}) collective-permute-start(bf16[240,128]{1,0:T(8,128)(2,1)S(1)} %add_convert_fusion.1), channel_id=1, source_target_pairs={{0,2},{1,3},{2,0},{3,1},{4,6},{5,7},{6,4},{7,5},{8,10},{9,11},{10,... | collective-permute-start | bytes 184328 | tf_op jit(solution)/shard_map/ppermute | solution.py:870
  69.6 1.6 %finish.3 = f32[4,32,128]{2,1,0:T(8,128)S(1)} custom-call(f32[4,32,128]{2,1,0:T(8,128)S(1)} %get-tuple-element.84.front.base, f32[4,32,128]{2,1,0:T(8,128)S(1)} %get-tuple-element.84.front.base, f32[2,64,128]{2,1,0:T(8,128)S(1)} %get-tuple-element.60.vel.refs_4_.ext, f32[2,64,128]{2,1,0:T(8,128)S(1)} %get-tuple-element.85.gstar, ...), custom_call_target="tpu_custom_call" | custom-call | flops 1000000000 | bytes 1000000 | tf_op jit(solution)/shard_map/finish/pallas_call | solution.py:735
  72.7 1.9 %collective-permute-start.18 = (bf16[240,128]{1,0:T(8,128)(2,1)S(1)}, bf16[240,128]{1,0:T(8,128)(2,1)S(1)}, u32[]{:S(2)}, u32[]{:S(2)}) collective-permute-start(bf16[240,128]{1,0:T(8,128)(2,1)S(1)} %add_convert_fusion.refs_0_), channel_id=1, source_target_pairs={{0,8},{8,0},{16,24},{24,16},{1,9},{9,1},{17,25},{25,17},{2,10},{10... | collective-permute-start | bytes 184328 | tf_op jit(solution)/shard_map/ppermute | solution.py:870
  77.0 2.0 %collective-permute-done.19.refs_2_ = bf16[240,128]{1,0:T(8,128)(2,1)S(1)} collective-permute-done((bf16[240,128]{1,0:T(8,128)(2,1)S(1)}, bf16[240,128]{1,0:T(8,128)(2,1)S(1)}, u32[]{:S(2)}, u32[]{:S(2)}) %collective-permute-start.19) | collective-permute-done | bytes 61472 | tf_op jit(solution)/shard_map/ppermute | solution.py:870
  81.9 1.4 %unpack.1 = (f32[9,2,64]{2,1,0:T(2,128)}, f32[64]{0:T(128)}, f32[5,9,64,64]{3,2,1,0:T(8,128)}, f32[5,64]{1,0:T(8,128)}, f32[9,64,64]{2,1,0:T(8,128)}, /*index=5*/f32[64]{0:T(128)}) custom-call(f32[5,8,128]{2,1,0:T(8,128)S(1)} %get-tuple-element.58.flags, bf16[960,128]{1,0:T(8,128)(2,1)S(1)} %arrange.1.mine, bf16[960,128]{1,0:T(8,128)(2,1)S(1)} %collective-permute-done.21.other), custom_call_target="tpu_custom_call" | custom-call | flops 10000000 | bytes 1000000 | tf_op jit(solution)/shard_map/unpack/pallas_call | solution.py:735
  (41 shorter events, 13.6 us)
Async XLA Ops:
  0.6 7.5 %collective-permute-start = (f32[2,2,16,128]{3,2,1,0:T(8,128)}, f32[2,2,16,128]{3,2,1,0:T(8,128)S(1)}, u32[]{:S(2)}, u32[]{:S(2)}) collective-permute-start(f32[2,2,16,128]{3,2,1,0:T(8,128)} %refs_0_.1), channel_id=1, source_target_pairs={{0,1},{1,0},{2,3},{3,2},{4,5},{5,4},{6,7},{7,6},{8,9},{9,8},{10,11... | collective-permute-start | bytes 98312 | tf_op jit(solution)/shard_map/ppermute | solution.py:870
  1.2 7.0 %collective-permute-start.1 = (f32[2,2,16,128]{3,2,1,0:T(8,128)}, f32[2,2,16,128]{3,2,1,0:T(8,128)S(1)}, u32[]{:S(2)}, u32[]{:S(2)}) collective-permute-start(f32[2,2,16,128]{3,2,1,0:T(8,128)} %refs_0_.1), channel_id=1, source_target_pairs={{0,7},{1,2},{2,1},{3,4},{4,3},{5,6},{6,5},{7,0},{8,15},{9,10},{10,... | collective-permute-start | bytes 98312 | tf_op jit(solution)/shard_map/ppermute | solution.py:895
  5.9 4.1 %collective-permute-start.2 = (f32[2,2,16,128]{3,2,1,0:T(8,128)}, f32[2,2,16,128]{3,2,1,0:T(8,128)S(1)}, u32[]{:S(2)}, u32[]{:S(2)}) collective-permute-start(f32[2,2,16,128]{3,2,1,0:T(8,128)} %refs_0_.1), channel_id=1, source_target_pairs={{0,6},{1,3},{2,0},{3,5},{4,2},{5,7},{6,4},{7,1},{8,14},{9,11},{10,... | collective-permute-start | bytes 98312 | tf_op jit(solution)/shard_map/ppermute | solution.py:895
  6.3 3.7 %collective-permute-start.3 = (f32[2,2,16,128]{3,2,1,0:T(8,128)}, f32[2,2,16,128]{3,2,1,0:T(8,128)S(1)}, u32[]{:S(2)}, u32[]{:S(2)}) collective-permute-start(f32[2,2,16,128]{3,2,1,0:T(8,128)} %refs_1_.2), channel_id=1, source_target_pairs={{0,1},{1,0},{2,3},{3,2},{4,5},{5,4},{6,7},{7,6},{8,9},{9,8},{10,11... | collective-permute-start | bytes 98312 | tf_op jit(solution)/shard_map/ppermute | solution.py:870
  17.9 4.8 %collective-permute-start.4 = (f32[4,32,128]{2,1,0:T(8,128)S(1)}, f32[4,32,128]{2,1,0:T(8,128)S(1)}, u32[]{:S(2)}, u32[]{:S(2)}) collective-permute-start(f32[4,32,128]{2,1,0:T(8,128)S(1)} %get-tuple-element.67.refs_0_), channel_id=1, source_target_pairs={{0,6},{1,7},{2,0},{3,1},{4,2},{5,3},{6,4},{7,5},{8,14},{9,15},{10,... | collective-permute-start | bytes 196616 | tf_op jit(solution)/shard_map/ppermute | solution.py:875
  20.2 6.3 %collective-permute-start.5 = (f32[4,32,128]{2,1,0:T(8,128)S(1)}, f32[4,32,128]{2,1,0:T(8,128)S(1)}, u32[]{:S(2)}, u32[]{:S(2)}) collective-permute-start(f32[4,32,128]{2,1,0:T(8,128)S(1)} %get-tuple-element.67.refs_0_), channel_id=1, source_target_pairs={{0,4},{1,5},{2,6},{3,7},{4,0},{5,1},{6,2},{7,3},{8,12},{9,13},{10,... | collective-permute-start | bytes 196616 | tf_op jit(solution)/shard_map/ppermute | solution.py:875
  20.2 6.3 %collective-permute-start.6 = (f32[4,32,128]{2,1,0:T(8,128)S(1)}, f32[4,32,128]{2,1,0:T(8,128)S(1)}, u32[]{:S(2)}, u32[]{:S(2)}) collective-permute-start(f32[4,32,128]{2,1,0:T(8,128)S(1)} %get-tuple-element.67.refs_0_), channel_id=1, source_target_pairs={{0,2},{1,3},{2,4},{3,5},{4,6},{5,7},{6,0},{7,1},{8,10},{9,11},{10,... | collective-permute-start | bytes 196616 | tf_op jit(solution)/shard_map/ppermute | solution.py:875
  39.8 7.8 %collective-permute-start.7 = (f32[4,32,128]{2,1,0:T(8,128)S(1)}, f32[4,32,128]{2,1,0:T(8,128)S(1)}, u32[]{:S(2)}, u32[]{:S(2)}) collective-permute-start(f32[4,32,128]{2,1,0:T(8,128)S(1)} %finish.2.refs_0_), channel_id=1, source_target_pairs={{0,6},{1,7},{2,0},{3,1},{4,2},{5,3},{6,4},{7,5},{8,14},{9,15},{10,... | collective-permute-start | bytes 196616 | tf_op jit(solution)/shard_map/ppermute | solution.py:875
  41.7 6.4 %collective-permute-start.8 = (f32[4,32,128]{2,1,0:T(8,128)S(1)}, f32[4,32,128]{2,1,0:T(8,128)S(1)}, u32[]{:S(2)}, u32[]{:S(2)}) collective-permute-start(f32[4,32,128]{2,1,0:T(8,128)S(1)} %finish.2.refs_0_), channel_id=1, source_target_pairs={{0,4},{1,5},{2,6},{3,7},{4,0},{5,1},{6,2},{7,3},{8,12},{9,13},{10,... | collective-permute-start | bytes 196616 | tf_op jit(solution)/shard_map/ppermute | solution.py:875
  41.8 6.4 %collective-permute-start.9 = (f32[4,32,128]{2,1,0:T(8,128)S(1)}, f32[4,32,128]{2,1,0:T(8,128)S(1)}, u32[]{:S(2)}, u32[]{:S(2)}) collective-permute-start(f32[4,32,128]{2,1,0:T(8,128)S(1)} %finish.2.refs_0_), channel_id=1, source_target_pairs={{0,2},{1,3},{2,4},{3,5},{4,6},{5,7},{6,0},{7,1},{8,10},{9,11},{10,... | collective-permute-start | bytes 196616 | tf_op jit(solution)/shard_map/ppermute | solution.py:875
  56.2 1.6 %collective-permute-start.11 = (bf16[960,128]{1,0:T(8,128)(2,1)S(1)}, bf16[960,128]{1,0:T(8,128)(2,1)S(1)}, u32[]{:S(2)}, u32[]{:S(2)}) collective-permute-start(bf16[960,128]{1,0:T(8,128)(2,1)S(1)} %get-tuple-element.97), channel_id=1, source_target_pairs={{0,1},{1,0},{2,3},{3,2},{4,5},{5,4},{6,7},{7,6},{8,9},{9,8},{10,11... | collective-permute-start | bytes 737288 | tf_op jit(solution)/shard_map/ppermute | solution.py:870
  57.8 5.2 %collective-permute-start.14 = (bf16[240,128]{1,0:T(8,128)(2,1)S(1)}, bf16[240,128]{1,0:T(8,128)(2,1)S(1)}, u32[]{:S(2)}, u32[]{:S(2)}) collective-permute-start(bf16[240,128]{1,0:T(8,128)(2,1)S(1)} %get-tuple-element.101), channel_id=1, source_target_pairs={{0,24},{8,16},{16,8},{24,0},{1,25},{9,17},{17,9},{25,1},{2,26},{10... | collective-permute-start | bytes 184328 | tf_op jit(solution)/shard_map/ppermute | solution.py:870
  60.4 4.2 %collective-permute-start.13 = (bf16[240,128]{1,0:T(8,128)(2,1)S(1)}, bf16[240,128]{1,0:T(8,128)(2,1)S(1)}, u32[]{:S(2)}, u32[]{:S(2)}) collective-permute-start(bf16[240,128]{1,0:T(8,128)(2,1)S(1)} %get-tuple-element.100), channel_id=1, source_target_pairs={{0,16},{8,24},{16,0},{24,8},{1,17},{9,25},{17,1},{25,9},{2,18},{10... | collective-permute-start | bytes 184328 | tf_op jit(solution)/shard_map/ppermute | solution.py:870
  60.9 4.2 %collective-permute-start.12 = (bf16[240,128]{1,0:T(8,128)(2,1)S(1)}, bf16[240,128]{1,0:T(8,128)(2,1)S(1)}, u32[]{:S(2)}, u32[]{:S(2)}) collective-permute-start(bf16[240,128]{1,0:T(8,128)(2,1)S(1)} %get-tuple-element.99), channel_id=1, source_target_pairs={{0,8},{8,0},{16,24},{24,16},{1,9},{9,1},{17,25},{25,17},{2,10},{10... | collective-permute-start | bytes 184328 | tf_op jit(solution)/shard_map/ppermute | solution.py:870
  65.1 6.2 %collective-permute-start.17 = (bf16[240,128]{1,0:T(8,128)(2,1)S(1)}, bf16[240,128]{1,0:T(8,128)(2,1)S(1)}, u32[]{:S(2)}, u32[]{:S(2)}) collective-permute-start(bf16[240,128]{1,0:T(8,128)(2,1)S(1)} %add_convert_fusion.1), channel_id=1, source_target_pairs={{0,6},{1,7},{2,4},{3,5},{4,2},{5,3},{6,0},{7,1},{8,14},{9,15},{10,... | collective-permute-start | bytes 184328 | tf_op jit(solution)/shard_map/ppermute | solution.py:870
  66.8 5.9 %collective-permute-start.16 = (bf16[240,128]{1,0:T(8,128)(2,1)S(1)}, bf16[240,128]{1,0:T(8,128)(2,1)S(1)}, u32[]{:S(2)}, u32[]{:S(2)}) collective-permute-start(bf16[240,128]{1,0:T(8,128)(2,1)S(1)} %add_convert_fusion.1), channel_id=1, source_target_pairs={{0,4},{1,5},{2,6},{3,7},{4,0},{5,1},{6,2},{7,3},{8,12},{9,13},{10,... | collective-permute-start | bytes 184328 | tf_op jit(solution)/shard_map/ppermute | solution.py:870
  67.8 4.9 %collective-permute-start.15 = (bf16[240,128]{1,0:T(8,128)(2,1)S(1)}, bf16[240,128]{1,0:T(8,128)(2,1)S(1)}, u32[]{:S(2)}, u32[]{:S(2)}) collective-permute-start(bf16[240,128]{1,0:T(8,128)(2,1)S(1)} %add_convert_fusion.1), channel_id=1, source_target_pairs={{0,2},{1,3},{2,0},{3,1},{4,6},{5,7},{6,4},{7,5},{8,10},{9,11},{10,... | collective-permute-start | bytes 184328 | tf_op jit(solution)/shard_map/ppermute | solution.py:870
  72.7 4.3 %collective-permute-start.18 = (bf16[240,128]{1,0:T(8,128)(2,1)S(1)}, bf16[240,128]{1,0:T(8,128)(2,1)S(1)}, u32[]{:S(2)}, u32[]{:S(2)}) collective-permute-start(bf16[240,128]{1,0:T(8,128)(2,1)S(1)} %add_convert_fusion.refs_0_), channel_id=1, source_target_pairs={{0,8},{8,0},{16,24},{24,16},{1,9},{9,1},{17,25},{25,17},{2,10},{10... | collective-permute-start | bytes 184328 | tf_op jit(solution)/shard_map/ppermute | solution.py:870
  74.6 4.4 %collective-permute-start.19 = (bf16[240,128]{1,0:T(8,128)(2,1)S(1)}, bf16[240,128]{1,0:T(8,128)(2,1)S(1)}, u32[]{:S(2)}, u32[]{:S(2)}) collective-permute-start(bf16[240,128]{1,0:T(8,128)(2,1)S(1)} %add_convert_fusion.refs_0_), channel_id=1, source_target_pairs={{0,16},{8,24},{16,0},{24,8},{1,17},{9,25},{17,1},{25,9},{2,18},{10... | collective-permute-start | bytes 184328 | tf_op jit(solution)/shard_map/ppermute | solution.py:870
  75.1 5.1 %collective-permute-start.20 = (bf16[240,128]{1,0:T(8,128)(2,1)S(1)}, bf16[240,128]{1,0:T(8,128)(2,1)S(1)}, u32[]{:S(2)}, u32[]{:S(2)}) collective-permute-start(bf16[240,128]{1,0:T(8,128)(2,1)S(1)} %add_convert_fusion.refs_0_), channel_id=1, source_target_pairs={{0,24},{8,16},{16,8},{24,0},{1,25},{9,17},{17,9},{25,1},{2,26},{10... | collective-permute-start | bytes 184328 | tf_op jit(solution)/shard_map/ppermute | solution.py:870
  76.3 4.1 %collective-permute-start.10 = (f32[4,16,128]{2,1,0:T(8,128)S(1)}, f32[4,16,128]{2,1,0:T(8,128)S(1)}, u32[]{:S(2)}, u32[]{:S(2)}) collective-permute-start(f32[4,16,128]{2,1,0:T(8,128)S(1)} %get-tuple-element.111), channel_id=1, source_target_pairs={{0,1},{1,0},{2,3},{3,2},{4,5},{5,4},{6,7},{7,6},{8,9},{9,8},{10,11... | collective-permute-start | bytes 98312 | tf_op jit(solution)/shard_map/ppermute | solution.py:870
  80.3 1.6 %collective-permute-start.21 = (bf16[960,128]{1,0:T(8,128)(2,1)S(1)}, bf16[960,128]{1,0:T(8,128)(2,1)S(1)}, u32[]{:S(2)}, u32[]{:S(2)}) collective-permute-start(bf16[960,128]{1,0:T(8,128)(2,1)S(1)} %arrange.1.mine), channel_id=1, source_target_pairs={{0,1},{1,0},{2,3},{3,2},{4,5},{5,4},{6,7},{7,6},{8,9},{9,8},{10,11... | collective-permute-start | bytes 737288 | tf_op jit(solution)/shard_map/ppermute | solution.py:870

commit v3 on v2

--- a/solution.py
+++ b/solution.py
@@ -18,7 +18,7 @@
 CH = 64
 LAYERS = 6
 N = 128
-BUFFER = 30 * CH
+HALF = 15 * CH
 bf16 = jnp.bfloat16
 f32 = jnp.float32
 NT = (((1,), (1,)), ((), ()))
@@ -92,24 +92,24 @@
     return jnp.dot(left[...], jnp.concatenate([high, high, low], axis=0), preferred_element_type=f32)
 
 
-def project(fields, right, left, weight):
-    count = len(fields)
+def local(x, count):
+    return jnp.concatenate([x[N - MARGIN :], x[: count + MARGIN]], axis=0)
+
+
+def project(fields, count, right, left, weight):
+    number = len(fields)
     source = [u - lanes(u, -1) + (v - rows(v, -1)) for u, v in fields]
     x = times_right(jnp.concatenate(source, axis=0), right)
-    x = jnp.concatenate([x[i * N : (i + 1) * N] for i in range(count)], axis=1)
-    x = times_left(x, left) * jnp.concatenate([weight[...]] * count, axis=1)
-    x = times_left(x, left)
-    x = jnp.concatenate([x[:, i * N : (i + 1) * N] for i in range(count)], axis=0)
-    x = times_right(x, right)
+    x = jnp.concatenate([x[i * N : (i + 1) * N] for i in range(number)], axis=1)
+    x = times_left(x, left) * jnp.concatenate([weight[...]] * number, axis=1)
+    x = local(times_left(x, left), count)
+    size = x.shape[0]
+    x = times_right(jnp.concatenate([x[:, i * N : (i + 1) * N] for i in range(number)], axis=0), right)
     out = []
     for i, (u, v) in enumerate(fields):
-        p = -x[i * N : (i + 1) * N]
-        out.append((u - (lanes(p, 1) - p), v - (rows(p, 1) - p)))
+        p = -x[i * size : (i + 1) * size]
+        out.append((local(u, count) - (lanes(p, 1) - p), local(v, count) - (rows(p, 1) - p)))
     return out
-
-
-def local(x, count):
-    return jnp.concatenate([x[N - MARGIN :], x[: count + MARGIN]], axis=0)
 
 
 def fold(o):
@@ -165,13 +165,25 @@
     return h + (f - f * h) * (2.0 * c + (6.0 * c * 0.044715) * zz)
 
 
-def network_forward(count, fields, w_first, w_hidden, bias, feats, slopes, raw, raw_done):
+def network_forward(count, fields, w_first, w_hidden, bias, feats, slopes, raw, raw_done, kept):
+    tasks = []
+
+    def slope_later(r, at):
+        z, h = kept[0, at, :], kept[1, at, :]
+        slopes[gradient_rows(count, LAYERS, r), :] = gelu_slope(z * h, h, z * z).astype(bf16)
+
     for m in range(1, LAYERS + 1):
 
         def emit(r, o, m=m):
-            value, h, zz = gelu_value((o if m == 1 else fold(o)) + bias[m - 1])
+            z = (o if m == 1 else fold(o)) + bias[m - 1]
+            value, h, zz = gelu_value(z)
             feats[feature_rows(count, m, r), :] = value.astype(bf16)
-            if -m <= r < count + m:
+            if m == LAYERS:
+                at = slice((r + m) * CH, (r + m + 1) * CH)
+                kept[0, at, :] = z
+                kept[1, at, :] = h
+                tasks.append(functools.partial(slope_later, r, at))
+            elif -m <= r < count + m:
                 slopes[gradient_rows(count, m, r), :] = gelu_slope(value, h, zz).astype(bf16)
 
         low, high = -reach(m), count + reach(m)
@@ -185,9 +197,18 @@
         raw[(r + MID) * CH : (r + MID + 1) * CH, :] = value
         raw_done(r, value)
 
-    conv_rows(
-        feature_window(feats, count, LAYERS), w_hidden.at[LAYERS - 1], -RAW, count + RAW, emit_raw
-    )
+    groups = (count + 2 * RAW) // 4
+    share = -(-len(tasks) // groups)
+
+    def between():
+        for task in tasks[:share]:
+            task()
+        del tasks[:share]
+
+    window = feature_window(feats, count, LAYERS)
+    conv_rows(window, w_hidden.at[LAYERS - 1], -RAW, count + RAW, emit_raw, between)
+    for task in tasks:
+        task()
 
 
 def interleave(vel, fields):
@@ -345,18 +366,20 @@
     return out
 
 
-def network_backward(count, w_hidden, slopes, grads, between=lambda: None):
+def network_backward(count, w_hidden, slopes, grads, between=lambda: None, copy=None):
     for m in range(LAYERS, 0, -1):
 
         def emit(r, o, m=m):
             at = gradient_rows(count, m, r)
-            grads[at, :] = (fold_rounded(o) * slopes[at, :].astype(f32)).astype(bf16)
+            value = (fold_rounded(o) * slopes[at, :].astype(f32)).astype(bf16)
+            grads[at, :] = value
+            if m == 1 and copy is not None:
+                copy[(r + 1) * CH : (r + 2) * CH, :] = value
 
         conv_rows(gradient_window(grads, count, m + 1), w_hidden.at[m - 1], -m, count + m, emit, between)
 
 
-def input_gradient(count, w_first, grads, gvel):
-    window = gradient_window(grads, count, 1)
+def input_gradient(count, w_first, window, gvel):
     starts = list(range(0, count, 2))
     for k in range(0, len(starts), 2):
         group = starts[k : k + 2]
@@ -396,28 +419,26 @@
     return out, jnp.sum(total, axis=1, keepdims=True)
 
 
-def weight_gradients(count, fields, feats, grads, put, columns, loop):
+def weight_half(count, half, fields, feats, grads, put, extra):
     lane = lax.broadcasted_iota(jnp.int32, (CH, N), 1)
-
-    def pair_of(pair):
-        lower, a = weight_product(count, 2 + 2 * pair, fields, feats, grads)
-        upper, b = weight_product(count, 3 + 2 * pair, fields, feats, grads)
-        x = jnp.where(lane == 33 + 2 * pair, a, columns[...])
-        columns[...] = jnp.where(lane == 34 + 2 * pair, b, x)
-        wide = jnp.concatenate([folded(lower), folded(upper)], axis=1)
-        for q in range(3):
-            put(3 * pair + q, wide[:, q * N : (q + 1) * N])
-
-    columns[...] = jnp.zeros((CH, N), f32)
-    if loop:
-        lax.fori_loop(0, 3, lambda pair, _: (pair_of(pair), 0)[1], 0)
-    else:
-        for pair in range(2, -1, -1):
-            pair_of(pair)
-    first, total = weight_product(count, 1, fields, feats, grads)
-    rest = jnp.where(lane == 32, total, columns[...])
-    first = jnp.concatenate([first, jnp.zeros((2 * CH, N - 32), f32)], axis=1)
-    put(9, jnp.concatenate([first[:CH] + rest, first[CH:], jnp.zeros((CH, N), f32)], axis=0))
+    extra[...] = jnp.zeros((3 * CH, N), f32)
+
+    @pl.when(half == 1)
+    def _():
+        first, total = weight_product(count, 1, fields, feats, grads)
+        first = jnp.concatenate([first, jnp.zeros((2 * CH, N - 32), f32)], axis=1)
+        extra[:CH, :] = jnp.where(lane == 35, total, first[:CH])
+        extra[CH : 2 * CH, :] = first[CH:]
+
+    parts, columns = [], extra[:CH, :]
+    for i in range(3):
+        product, total = weight_product(count, 2 + 3 * half + i, fields, feats, grads)
+        parts.append(folded(product))
+        columns = jnp.where(lane == 32 + i, total, columns)
+    parts.append(jnp.concatenate([columns[:, :CH], extra[CH:, :CH]], axis=0))
+    wide = jnp.concatenate(parts, axis=1)
+    for q in range(5):
+        put(q, wide[:, q * N : (q + 1) * N])
 
 
 def fetch(sources, targets, sems):
@@ -526,7 +547,7 @@
 
 
 def network_kernel(
-    count, vel, extra, w_first, w_hidden, bias, mix, adder, block, interp, raw, clear, fields, feats, slopes, put
+    count, vel, extra, w_first, w_hidden, bias, mix, adder, block, interp, raw, clear, fields, feats, slopes, put, kept
 ):
     interleave(vel, fields)
     clear_patches(count, fields, mix, clear, put)
@@ -538,7 +559,7 @@
             interpolate(r + 1 - len(sums), sums[:4], adder, put, interp)
             del sums[:4]
 
-    network_forward(count, fields, w_first, w_hidden, bias, feats, slopes, raw, raw_done)
+    network_forward(count, fields, w_first, w_hidden, bias, feats, slopes, raw, raw_done, kept)
     for i in range(0, len(sums), 4):
         interpolate(count + RAW - len(sums) + i, sums[i : i + 4], adder, put, interp)
     su, sv = provisional(count, vel[0], vel[1], interp)
@@ -554,17 +575,21 @@
 
 def project_kernel(count, blocks, steps, flags, *refs):
     gathered, refs = refs[:blocks], refs[blocks:]
-    vel, right, left, weight, gstar, own, *ext = refs
-    su, sv, cu, cv = [joined(gathered, i) for i in range(4)]
-    mv, mg = [flags[step][0:1, :] for step in steps]
-    news, grads = project([(su, sv), (mg * cu, mg * cv)], right, left, weight)
+    forward, backward = steps
+    mg = flags[backward][0:1, :]
+    fields = [(mg * joined(gathered, 2), mg * joined(gathered, 3))]
+    if forward is None:
+        right, left, weight, gstar, own = refs
+    else:
+        vel, right, left, weight, gstar, own, ext = refs
+        fields.append((joined(gathered, 0), joined(gathered, 1)))
+        mv = flags[forward][0:1, :]
+    out = project(fields, count, right, left, weight)
     for i in range(2):
-        x = vel[i] + mv * (local(news[i], count) - vel[i])
-        for ref in ext:
-            ref[i] = x
-        own[i] = x[MARGIN : MARGIN + count]
-        gstar[i] = local(grads[i], count)
-        own[2 + i] = (1.0 - mg) * gathered[0][2 + i]
+        gstar[i] = out[0][i]
+        own[i] = (1.0 - mg) * gathered[0][2 + i]
+        if forward is not None:
+            ext[i] = vel[i] + mv * (out[1][i] - vel[i])
 
 
 def static(start, size):
@@ -575,7 +600,7 @@
     if len(refs) == 6:
         mix, raw, grads, gvel, spread, ginterp = refs
     else:
-        grads, gvel, ginterp = refs
+        grads, first, ginterp = refs
     interp_gradients(count, gstar[0], gstar[1], ext[0], ext[1], ginterp)
     raw_gradient(count, clear, ginterp, grads)
     tasks = []
@@ -590,58 +615,69 @@
         if tasks and turn[0] % 3 == 0:
             tasks.pop(0)()
 
-    network_backward(count, b_hidden, slopes, grads, between)
+    network_backward(count, b_hidden, slopes, grads, between, None if len(refs) == 6 else first)
     for task in tasks:
         task()
-    input_gradient(count, b_first, grads, gvel)
-
-
-def finish_kernel(count, front, base, ext, gstar, interp, gvel, *refs):
+    if len(refs) == 6:
+        input_gradient(count, b_first, gradient_window(grads, count, 1), gvel)
+
+
+def finish_kernel(count, front, base, gstar, interp, gvel, spread, out, lines):
+    change = velocity_gradients(count, gstar[0], gstar[1], interp, spread, lines)
+    for i in range(2):
+        out[i] = front[i]
+        out[2 + i] = base[i] + change[i] + gvel[i]
+
+
+def last_kernel(count, blocks, flags, *refs):
+    gathered, refs = refs[:blocks], refs[blocks:]
+    now, right, left, weight, base, ext, gstar, interp, first, b_first, mix, raw, out = refs[:13]
+    lines, spread, ginterp, gvel = refs[13:]
+    (news,) = project([(joined(gathered, 0), joined(gathered, 1))], count, right, left, weight)
+    own = slice(MARGIN, MARGIN + count)
+    mask = flags[STEPS - 1][0:1, :]
+    for i in range(2):
+        out[i] = now[i, own] + mask * (news[i][own] - now[i, own])
     gu, gv = gstar[0], gstar[1]
-    if len(refs) == 3:
-        spread, out, lines = refs
-    else:
-        mix, raw, out, lines, spread, ginterp = refs
-        interp_gradients(count, gu, gv, ext[0], ext[1], ginterp)
-        columns = put_columns()
-
-        def at(start, size):
-            return pl.ds(pl.multiple_of(start, size), size) if size > 1 else pl.ds(start, size)
-
-        def step(i, _):
-            for k in range(2):
-                spread_back(4 * i + 2 * k - RAW, at, columns, mix, raw, ginterp, spread)
-            return 0
-
-        lax.fori_loop(0, (count + 2 * RAW) // 4, step, 0)
+    input_gradient(count, b_first, lambda r: first[r * CH : (r + 4) * CH, :], gvel)
+    interp_gradients(count, gu, gv, ext[0], ext[1], ginterp)
+    columns = put_columns()
+
+    def at(start, size):
+        return pl.ds(pl.multiple_of(start, size), size) if size > 1 else pl.ds(start, size)
+
+    def step(i, _):
+        for k in range(2):
+            spread_back(4 * i + 2 * k - RAW, at, columns, mix, raw, ginterp, spread)
+        return 0
+
+    lax.fori_loop(0, (count + 2 * RAW) // 4, step, 0)
     change = velocity_gradients(count, gu, gv, interp, spread, lines)
     for i in range(2):
-        out[i] = front[i]
-        out[2 + i] = base[2 + i] + change[i] + gvel[i]
-
-
-def weights_kernel(count, fields, feats, grads, buffer, columns):
-    def put(block, value):
-        buffer[place(block * 3 * CH, 3 * CH), :] = value
-
-    weight_gradients(count, fields, feats, grads, put, columns, True)
-
-
-def total_weights_kernel(count, flags, previous, fields, feats, grads, keep, send, columns, total):
-    half = keep.shape[0]
-
-    def put(block, value):
-        at = slice(block * 3 * CH, (block + 1) * 3 * CH)
-        total[at, :] = value + previous[at, :]
-
-    if 2 * half > BUFFER:
-        total[BUFFER:, :] = jnp.zeros((2 * half - BUFFER, N), f32)
-    weight_gradients(count, fields, feats, grads, put, columns, False)
-    for low in range(0, half, 3 * CH):
-        high = min(low + 3 * CH, half)
-        a, b = total[low:high, :], total[half + low : half + high, :]
-        keep[low:high, :] = chosen(flags[STEPS], a, b).astype(bf16)
-        send[low:high, :] = chosen(flags[STEPS], b, a).astype(bf16)
+        out[2 + i] = base[i] + change[i] + gvel[i]
+
+
+def weights_kernel(count, fields, feats, grads, buffer, extra):
+    def both(half, _):
+        def put(q, value):
+            buffer[place(half * HALF + q * 3 * CH, 3 * CH), :] = value
+
+        weight_half(count, half, fields, feats, grads, put, extra)
+        return 0
+
+    lax.fori_loop(0, 2, both, 0)
+
+
+def half_kernel(count, side, previous, fields, feats, grads, out, extra):
+    half = (lax.axis_index("strip") & 1) ^ side
+
+    def put(q, value):
+        value = value + previous[place(half * HALF + q * 3 * CH, 3 * CH), :]
+        out[q * 3 * CH : (q + 1) * 3 * CH, :] = value.astype(bf16)
+
+    weight_half(count, half, fields, feats, grads, put, extra)
+    if out.shape[0] > HALF:
+        out[HALF:, :] = jnp.zeros((out.shape[0] - HALF, N), bf16)
 
 
 def exchanged(flags, blocks):
@@ -669,41 +705,34 @@
 
 
 def unpack_kernel(flags, mine, other, first, first_bias, middle, middle_bias, last, last_bias):
-    half = mine.shape[0]
-
-    def block(b):
-        lines = []
-        for low, high, a, c in ((0, half, mine, other), (half, 2 * half, other, mine)):
-            start, stop = max(b * 3 * CH, low), min((b + 1) * 3 * CH, high)
-            if start < stop:
-                at = slice(start - low, stop - low)
-                lines.append(chosen(flags[STEPS], a[at, :].astype(f32), c[at, :].astype(f32)))
-        return lines[0] if len(lines) == 1 else jnp.concatenate(lines, axis=0)
-
-    for pair in range(3):
-        wide = jnp.concatenate([block(3 * pair + q) for q in range(3)], axis=1)
-        for side in range(2):
-            m = 2 * pair + side
+    for half in range(2):
+        a, b = (mine, other) if half == 0 else (other, mine)
+        blocks = []
+        for q in range(5):
+            at = slice(q * 3 * CH, (q + 1) * 3 * CH)
+            blocks.append(chosen(flags[STEPS], a[at, :].astype(f32), b[at, :].astype(f32)))
+        wide = jnp.concatenate(blocks, axis=1)
+        turned = [blocks[4][two * CH : (two + 1) * CH].T[CH:] for two in range(2)]
+        for i in range(3):
+            m = 3 * half + i
             for a in range(3):
-                at = (3 * side + a) * CH
-                part = wide[:, at : at + CH]
+                part = wide[:, (3 * i + a) * CH : (3 * i + a + 1) * CH]
                 for e in range(3):
                     value = part[e * CH : (e + 1) * CH]
                     if m < LAYERS - 1:
                         middle[m, 3 * a + e] = value
                     else:
                         last[3 * a + e] = value
-    rest = block(9)
-    turned = [rest[two * CH : (two + 1) * CH].T for two in range(2)]
+            if m < LAYERS - 1:
+                middle_bias[m : m + 1, :] = turned[0][32 + i : 33 + i]
+            else:
+                last_bias[...] = turned[0][32 + i]
+    first_bias[...] = turned[0][35]
     for a in range(3):
         for e in range(3):
             for ch in range(2):
                 low, high = 16 * ch + 4 * a + e, 16 * ch + 4 * (a + 1) + e
                 first[3 * a + e, ch : ch + 1, :] = turned[0][low : low + 1] + turned[1][high : high + 1]
-    turned = turned[0]
-    first_bias[...] = turned[32]
-    middle_bias[...] = turned[33 : 33 + LAYERS - 1]
-    last_bias[...] = turned[32 + LAYERS]
 
 
 VMEM = pl.BlockSpec(memory_space=pltpu.VMEM)
@@ -799,48 +828,53 @@
     out = [array(f32, 4, count, N), array(f32, 4 * mid, N), array(f32, mid * CH, N), array(f32, mid * 32, N)]
     out += [array(f32, 2, 4 * local_rows, N)]
     out += [feature_array(count), gradient_array(count, LAYERS)]
-    scratch = [field(4 * mid)]
+    scratch = [field(4 * mid), field((count + 2 * LAYERS) * CH, 2)]
     return call(functools.partial(network_kernel, count), "network", 4 * 10**9, [vel, extra, *weights], out, scratch)
 
 
-def run_project(count, steps, flags, gathered, vel, tables, last=False):
+def run_project(count, steps, flags, gathered, tables, *vel):
     local_rows = count + 2 * MARGIN
-    out = [array(f32, 2, local_rows, N), array(f32, 4, count, N)]
-    if not last:
+    out = [array(f32, 2, local_rows, N), array(f32, 2, count, N)]
+    if vel:
         out.append(array(f32, 2, local_rows, N))
     kernel = functools.partial(project_kernel, count, len(gathered), steps)
-    return call(kernel, "project", 10**9, [flags, *gathered, vel, *tables], out)
+    return call(kernel, "project", 10**9, [flags, *gathered, *vel, *tables], out)
 
 
 def run_back(count, ext, gstar, clear, b_first, b_hidden, slopes, *more):
     mid = count + 2 * MID
     inputs = [ext, gstar, clear, b_first, b_hidden, slopes, *more]
-    out = [gradient_array(count, LAYERS + 1), array(f32, 2, count, N)]
+    out = [gradient_array(count, LAYERS + 1)]
     if more:
-        out.append(array(f32, 2, 4, 4 * mid, N))
+        out += [array(f32, 2, count, N), array(f32, 2, 4, 4 * mid, N)]
+    else:
+        out.append(array(bf16, (count + 2) * CH, N))
     return call(functools.partial(back_kernel, count), "back", 4 * 10**9, inputs, out, [field(mid, 4)])
 
 
-def run_finish(count, front, base, ext, gstar, interp, gvel, *more):
+def run_finish(count, *inputs):
+    kernel = functools.partial(finish_kernel, count)
+    return call(kernel, "finish", 10**9, inputs, array(f32, 4, count, N), [field(4 * count, 2)])
+
+
+def run_last(count, flags, gathered, *inputs):
     mid = count + 2 * MID
-    inputs = [front, base, ext, gstar, interp, gvel, *more]
-    scratch = [field(4 * count, 2)]
-    if len(more) > 1:
-        scratch += [field(4 * mid, 2, 4), field(mid, 4)]
-    return call(functools.partial(finish_kernel, count), "finish", 10**9, inputs, array(f32, 4, count, N), scratch)
+    scratch = [field(4 * count, 2), field(4 * mid, 2, 4), field(mid, 4), field(count, 2)]
+    kernel = functools.partial(last_kernel, count, len(gathered))
+    return call(kernel, "last", 10**9, [flags, *gathered, *inputs], array(f32, 4, count, N), scratch)
 
 
 def run_weights(count, fields, feats, grads):
-    scratch = [field(CH)]
     kernel = functools.partial(weights_kernel, count)
-    return call(kernel, "weights", 3 * 10**9, [fields, feats, grads], array(f32, BUFFER, N), scratch)
-
-
-def run_total_weights(count, half, flags, previous, fields, feats, grads):
-    scratch = [field(CH), field(2 * half)]
-    inputs = [flags, previous, fields, feats, grads]
-    kernel = functools.partial(total_weights_kernel, count)
-    return call(kernel, "total_weights", 3 * 10**9, inputs, [array(bf16, half, N)] * 2, scratch)
+    return call(kernel, "weights", 3 * 10**9, [fields, feats, grads], array(f32, 2 * HALF, N), [field(3 * CH)])
+
+
+def run_half(count, side, rows, previous, fields, feats, grads, *after):
+    inputs = [previous, fields, feats, grads, *after]
+    kernel = functools.partial(half_kernel, count, side)
+    if after:
+        kernel = lambda *refs: half_kernel(count, side, *refs[:4], *refs[5:])
+    return call(kernel, "half", 10**9, inputs, array(bf16, rows, N), [field(3 * CH)])
 
 
 def run_halves(flags, keep, received, parts):
@@ -895,10 +929,10 @@
     return lax.ppermute(velocity, "strip", cross), lax.ppermute(velocity, "strip", same)
 
 
-def sum_everywhere(keep, send, flags):
+def sum_everywhere(keep, received, flags):
     parts = lax.axis_size("traj")
     groups = lax.axis_size("strip") // 2
-    blocks = run_halves(flags, keep, swap(send, "strip", 1), parts)
+    blocks = run_halves(flags, keep, received, parts)
     total = blocks[0].astype(f32)
     for k in range(1, parts):
         total = total + swap(blocks[k], "traj", k).astype(f32)
@@ -926,7 +960,7 @@
     first_kernel = first_kernel.transpose(0, 2, 1)
     params = (first_kernel, first_bias, middle_kernels, middle_biases, last_kernel, last_bias)
     parts = lax.axis_size("traj")
-    half = -(-BUFFER // (2 * parts * 16)) * parts * 16
+    half_rows = -(-HALF // (parts * 16)) * parts * 16
     own, w_first, w_hidden, bias, mix, adder, flags = run_prepare(
         lengths, velocity, cotangent, params, parts.bit_length() - 1
     )
@@ -936,25 +970,29 @@
     block, interp0, raw0, clear0, fields0, feats0, slopes0 = run_network(count, v0, cot, weights)
     gathered = gather_groups(block)
     b_first, b_hidden, tables = run_prepare_back(params, interp0)
-    gstar1, base, v1 = run_project(count, (0, 1), flags, gathered, v0, tables)
+    gstar1, base, v1 = run_project(count, (0, 1), flags, gathered, tables, v0)
     block, interp1, raw1, clear1, fields1, feats1, slopes1 = run_network(count, v1, cot, weights)
     grads1, gvel, spread = run_back(count, v1, gstar1, clear1, b_first, b_hidden, slopes1, mix, raw1)
-    block = run_finish(count, block, base, v1, gstar1, interp1, gvel, spread)
+    block = run_finish(count, block, base, gstar1, interp1, gvel, spread)
     gathered = gather_groups(block)
     buffer = run_weights(count, fields1, feats1, grads1)
-    gstar0, base = run_project(count, (1, 0), flags, gathered, v1, tables, last=True)
-    grads0, gvel = run_back(count, v0, gstar0, clear0, b_first, b_hidden, slopes0)
-    keep, send = run_total_weights(count, half, flags, buffer, fields0, feats0, grads0)
-    out = run_finish(count, base, base, v0, gstar0, interp0, gvel, mix, raw0)
+    gstar0, base = run_project(count, (None, 0), flags, gathered, tables)
+    grads0, first = run_back(count, v0, gstar0, clear0, b_first, b_hidden, slopes0)
+    send = run_half(count, 1, half_rows, buffer, fields0, feats0, grads0)
+    received = swap(send, "strip", 1)
+    keep = run_half(count, 0, half_rows, buffer, fields0, feats0, grads0, send)
+    out = run_last(
+        count, flags, gathered, v1, *tables, base, v0, gstar0, interp0, first, b_first, mix, raw0
+    )
 
     strips = out.reshape(4, 2, rc, N).transpose(1, 0, 2, 3)
     mine, other = pick(strips, index)[None], swap(pick(strips, 1 - index), "strip", 1)[None]
     out = jnp.where(
         index == 0, jnp.concatenate([mine, other], axis=0), jnp.concatenate([other, mine], axis=0)
     )
-    mine, other = sum_everywhere(keep, send, flags)
-    first, *rest = run_unpack(flags, mine, other)
-    return (out[:, :2], out[:, 2:], first.transpose(0, 2, 1), *rest)
+    mine, other = sum_everywhere(keep, received, flags)
+    grad_first, *rest = run_unpack(flags, mine, other)
+    return (out[:, :2], out[:, 2:], grad_first.transpose(0, 2, 1), *rest)
 
 
 def solution(mesh):

time: 83.5 us -> 82.8 us (level)
  waiting for transfers between devices: 17.6 us -> 16.3 us
    ppermute x14, waiting for transfers between devices: 11.5 us -> 9.84 us  [swap(): return lax.ppermute(x, axis, [(i, i ^ offset) for i in range(count)])]
    pallas_call x14 -> x15, Pallas kernels: 36.4 us -> 37.1 us  [call(): pl.pallas_call(kernel, in_specs=[VMEM] * len(inputs), out_specs=jax.tree....]
  transfers between devices with their start and end apart: 22 -> 22, of which waited for: 13 -> 11; matrix products, arithmetic and copies ran while one was open for 1% -> 1% of each run, Pallas kernels for 11% -> 14%
where the time goes in v3:
time: 82.8 us; the launch traced here: 82.7 us
  Pallas kernels  40.8 us (49%)
  starting transfers between devices  24 us (29%)
  waiting for transfers between devices  16.3 us (20%)
  between operations  0.83 us (1%)
    pallas_call x15, Pallas kernels, call(): pl.pallas_call(kernel, in_specs=[VMEM] * len(inputs), out_specs=jax.tree....  37.1 us
    ppermute x14, starting transfers between devices, swap(): return lax.ppermute(x, axis, [(i, i ^ offset) for i in range(count)])  12.2 us
    ppermute x14, waiting for transfers between devices, swap(): return lax.ppermute(x, axis, [(i, i ^ offset) for i in range(count)])  9.84 us
    ppermute x6, starting transfers between devices, from_group(): lax.ppermute(x, 'strip', [(i, (i - 2 * ahead) % count) for i in range(cou...  6.66 us
    ppermute x1, starting transfers between devices, margins(): lax.ppermute(velocity, 'strip', cross)  4.71 us
    ppermute x6, waiting for transfers between devices, from_group(): lax.ppermute(x, 'strip', [(i, (i - 2 * ahead) % count) for i in range(cou...  4.64 us
    pallas_call x2, Pallas kernels, call_from_hbm(): pl.pallas_call(kernel, in_specs=[hbm] * len(inputs) + [VMEM] * len(after)...  3.69 us
    ppermute x1, waiting for transfers between devices, margins(): lax.ppermute(velocity, 'strip', same)  1.82 us
  transfers between devices with their start and end apart: 22, of which 11 were waited for; matrix products, arithmetic and copies ran while one was open for 1% of the time, Pallas kernels for 14%

profile of v3, /device:TPU:0, one launch (start us, length us, event | category | flops | bytes accessed | tf_op | source)
XLA Modules:
  0.0 82.7 jit_solution(6673107083612649447)
XLA Ops:
  1.2 4.7 %collective-permute-start.1 = (f32[2,2,16,128]{3,2,1,0:T(8,128)}, f32[2,2,16,128]{3,2,1,0:T(8,128)S(1)}, u32[]{:S(2)}, u32[]{:S(2)}) collective-permute-start(f32[2,2,16,128]{3,2,1,0:T(8,128)} %refs_0_.1), channel_id=1, source_target_pairs={{0,7},{1,2},{2,1},{3,4},{4,3},{5,6},{6,5},{7,0},{8,15},{9,10},{10,... | collective-permute-start | bytes 98312 | tf_op jit(solution)/shard_map/ppermute | solution.py:929
  6.3 1.8 %prepare.1 = (f32[2,2,16,128]{3,2,1,0:T(8,128)S(1)}, bf16[128,32]{1,0:T(8,128)(2,1)S(1)}, bf16[6,384,256]{2,1,0:T(8,128)(2,1)S(1)}, f32[7,64,128]{2,1,0:T(8,128)...) custom-call(f32[2,2,16,128]{3,2,1,0:T(8,128)} %refs_0_.1, ...), custom_call_target="tpu_custom_call" | custom-call | flops 1000000000 | bytes 1000000 | tf_op jit(solution)/shard_map/prepare/pallas_call | solution.py:809
  8.2 1.8 %collective-permute-done.2.same = f32[2,2,16,128]{3,2,1,0:T(8,128)S(1)} collective-permute-done((f32[2,2,16,128]{3,2,1,0:T(8,128)}, f32[2,2,16,128]{3,2,1,0:T(8,128)S(1)}, u32[]{:S(2)}, u32[]{:S(2)}) %collective-permute-start.2) | collective-permute-done | bytes 32800 | tf_op jit(solution)/shard_map/ppermute | solution.py:929
  10.0 7.9 %network.2 = (f32[4,32,128]{2,1,0:T(8,128)S(1)}, f32[192,128]{1,0:T(8,128)S(1)}, f32[3072,128]{1,0:T(8,128)S(1)}, f32[1536,128]{1,0:T(8,128)S(1)}, f32[2,256,128...) custom-call(f32[2,64,128]{2,1,0:T(8,128)S(1)} %get-tuple-element.58.vel.refs_4_.ext.refs_9_, ...), custom_call_target="tpu_custom_call" | custom-call | flops 4000000000 | bytes 1000000 | tf_op jit(solution)/shard_map/network/pallas_call | solution.py:764
  17.9 2.2 %collective-permute-start.4 = (f32[4,32,128]{2,1,0:T(8,128)S(1)}, f32[4,32,128]{2,1,0:T(8,128)S(1)}, u32[]{:S(2)}, u32[]{:S(2)}) collective-permute-start(f32[4,32,128]{2,1,0:T(8,128)S(1)} %get-tuple-element.65.refs_0_), channel_id=1, source_target_pairs={{0,6},{1,7},{2,0},{3,1},{4,2},{5,3},{6,4},{7,5},{8,14},{9,15},{10,... | collective-permute-start | bytes 196616 | tf_op jit(solution)/shard_map/ppermute | solution.py:909
  20.8 1.9 %prepare_back.1 = (bf16[16,256]{1,0:T(8,128)(2,1)S(1)}, bf16[6,384,256]{2,1,0:T(8,128)(2,1)S(1)}, bf16[384,128]{1,0:T(8,128)(2,1)S(1)}, bf16[128,384]{1,0:T(8,128)(2,1)S(1)}, f32[128,128]{1,0:T(8,128)S(1)}) custom-call(bf16[9,2,64]{2,1,0:T(2,128)(2,1)} %bitcast.12, bf16[5,9,64,64]{3,2,1,0:T(8,128)(2,1)} %refs_1_.3, bf16[9,64,64]{2,1,0:T(8,128)(2,1)} %refs_2_.1, ...), custom_call_target="tpu_custom_call" | custom-call | flops 1000000000 | bytes 1000000 | tf_op jit(solution)/shard_map/prepare_back/pallas_call | solution.py:809
  22.6 3.8 %collective-permute-done.5.refs_2_ = f32[4,32,128]{2,1,0:T(8,128)S(1)} collective-permute-done((f32[4,32,128]{2,1,0:T(8,128)S(1)}, f32[4,32,128]{2,1,0:T(8,128)S(1)}, u32[]{:S(2)}, u32[]{:S(2)}) %collective-permute-start.5) | collective-permute-done | bytes 65568 | tf_op jit(solution)/shard_map/ppermute | solution.py:909
  27.4 7.9 %network.3 = (f32[4,32,128]{2,1,0:T(8,128)S(1)}, f32[192,128]{1,0:T(8,128)S(1)}, f32[3072,128]{1,0:T(8,128)S(1)}, f32[1536,128]{1,0:T(8,128)S(1)}, f32[2,256,128...) custom-call(f32[2,64,128]{2,1,0:T(8,128)S(1)} %get-tuple-element.70.vel.ext.refs_4_, ...), custom_call_target="tpu_custom_call" | custom-call | flops 4000000000 | bytes 1000000 | tf_op jit(solution)/shard_map/network/pallas_call | solution.py:764
  35.2 4.4 %back.2 = (bf16[21504,128]{1,0:T(8,128)(2,1)S(1)}, f32[2,32,128]{2,1,0:T(8,128)S(1)}, f32[2,4,192,128]{3,2,1,0:T(8,128)S(1)}) custom-call(f32[2,64,128]{2,1,0:T(8,128)S(1)} %get-tuple-element.70.vel.ext.refs_4_, f32[2,64,128]{2,1,0:T(8,128)S(1)} %get-tuple-element.73.gstar, f32[1536,128]{1,0:T(8,128)S(1)} %get-tuple-element.75.clear, ...), custom_call_target="tpu_custom_call" | custom-call | flops 4000000000 | bytes 1000000 | tf_op jit(solution)/shard_map/back/pallas_call | solution.py:764
  39.8 1.9 %collective-permute-start.7 = (f32[4,32,128]{2,1,0:T(8,128)S(1)}, f32[4,32,128]{2,1,0:T(8,128)S(1)}, u32[]{:S(2)}, u32[]{:S(2)}) collective-permute-start(f32[4,32,128]{2,1,0:T(8,128)S(1)} %finish.1.refs_0_), channel_id=1, source_target_pairs={{0,6},{1,7},{2,0},{3,1},{4,2},{5,3},{6,4},{7,5},{8,14},{9,15},{10,... | collective-permute-start | bytes 196616 | tf_op jit(solution)/shard_map/ppermute | solution.py:909
  41.6 1.9 %collective-permute-start.9 = (f32[4,32,128]{2,1,0:T(8,128)S(1)}, f32[4,32,128]{2,1,0:T(8,128)S(1)}, u32[]{:S(2)}, u32[]{:S(2)}) collective-permute-start(f32[4,32,128]{2,1,0:T(8,128)S(1)} %finish.1.refs_0_), channel_id=1, source_target_pairs={{0,2},{1,3},{2,4},{3,5},{4,6},{5,7},{6,0},{7,1},{8,10},{9,11},{10,... | collective-permute-start | bytes 196616 | tf_op jit(solution)/shard_map/ppermute | solution.py:909
  43.5 3.7 %weights.1.previous.refs_0_ = f32[1920,128]{1,0:T(8,128)S(1)} custom-call(f32[2,256,128]{2,1,0:T(8,128)S(1)} %get-tuple-element.88.fields, bf16[21504,128]{1,0:T(8,128)(2,1)S(1)} %get-tuple-element.89.feats, bf16[21504,128]{1,0:T(8,128)(2,1)S(1)} %get-tuple-element.90.grads), custom_call_target="tpu_custom_call" | custom-call | flops 3000000000 | bytes 1000000 | tf_op jit(solution)/shard_map/weights/pallas_call | solution.py:764
  48.8 3.8 %back.3 = (bf16[21504,128]{1,0:T(8,128)(2,1)S(1)}, bf16[2176,128]{1,0:T(8,128)(2,1)S(1)}) custom-call(f32[2,64,128]{2,1,0:T(8,128)S(1)} %get-tuple-element.58.vel.refs_4_.ext.refs_9_, f32[2,64,128]{2,1,0:T(8,128)S(1)} %get-tuple-element.83.gstar.refs_10_, f32[1536,128]{1,0:T(8,128)S(1)} %get-tuple-element.84.clear, ...), custom_call_target="tpu_custom_call" | custom-call | flops 4000000000 | bytes 1000000 | tf_op jit(solution)/shard_map/back/pallas_call | solution.py:764
  52.6 2.0 %half.2.refs_4_ = bf16[960,128]{1,0:T(8,128)(2,1)S(1)} custom-call(f32[1920,128]{1,0:T(8,128)S(1)} %weights.1.previous.refs_0_, f32[2,256,128]{2,1,0:T(8,128)S(1)} %get-tuple-element.91.fields.refs_1_, bf16[21504,128]{1,0:T(8,128)(2,1)S(1)} %get-tuple-element.92.feats.refs_2_, bf16[21504,128]{1,0:T(8,128)(2,1)S(1)} %get-tuple-element.93.grads.refs_3_), custom_call_target="tpu_custom_call" | custom-call | flops 1000000000 | bytes 1000000 | tf_op jit(solution)/shard_map/half/pallas_call | solution.py:764
  54.7 1.7 %half.3.keep = bf16[960,128]{1,0:T(8,128)(2,1)S(1)} custom-call(f32[1920,128]{1,0:T(8,128)S(1)} %weights.1.previous.refs_0_, f32[2,256,128]{2,1,0:T(8,128)S(1)} %get-tuple-element.91.fields.refs_1_, bf16[21504,128]{1,0:T(8,128)(2,1)S(1)} %get-tuple-element.92.feats.refs_2_, bf16[21504,128]{1,0:T(8,128)(2,1)S(1)} %get-tuple-element.93.grads.refs_3_, ...), custom_call_target="tpu_custom_call" | custom-call | flops 1000000000 | bytes 1000000 | tf_op jit(solution)/shard_map/half/pallas_call | solution.py:764
  56.5 2.5 %collective-permute-start.14 = (bf16[240,128]{1,0:T(8,128)(2,1)S(1)}, bf16[240,128]{1,0:T(8,128)(2,1)S(1)}, u32[]{:S(2)}, u32[]{:S(2)}) collective-permute-start(bf16[240,128]{1,0:T(8,128)(2,1)S(1)} %get-tuple-element.97), channel_id=1, source_target_pairs={{0,24},{8,16},{16,8},{24,0},{1,25},{9,17},{17,9},{25,1},{2,26},{10... | collective-permute-start | bytes 184328 | tf_op jit(solution)/shard_map/ppermute | solution.py:904
  60.1 2.1 %collective-permute-done.14 = bf16[240,128]{1,0:T(8,128)(2,1)S(1)} collective-permute-done((bf16[240,128]{1,0:T(8,128)(2,1)S(1)}, bf16[240,128]{1,0:T(8,128)(2,1)S(1)}, u32[]{:S(2)}, u32[]{:S(2)}) %collective-permute-start.14) | collective-permute-done | bytes 61472 | tf_op jit(solution)/shard_map/ppermute | solution.py:904
  63.8 1.7 %collective-permute-start.17 = (bf16[240,128]{1,0:T(8,128)(2,1)S(1)}, bf16[240,128]{1,0:T(8,128)(2,1)S(1)}, u32[]{:S(2)}, u32[]{:S(2)}) collective-permute-start(bf16[240,128]{1,0:T(8,128)(2,1)S(1)} %add_convert_fusion.1), channel_id=1, source_target_pairs={{0,6},{1,7},{2,4},{3,5},{4,2},{5,3},{6,0},{7,1},{8,14},{9,15},{10,... | collective-permute-start | bytes 184328 | tf_op jit(solution)/shard_map/ppermute | solution.py:904
  66.1 2.1 %collective-permute-start.15 = (bf16[240,128]{1,0:T(8,128)(2,1)S(1)}, bf16[240,128]{1,0:T(8,128)(2,1)S(1)}, u32[]{:S(2)}, u32[]{:S(2)}) collective-permute-start(bf16[240,128]{1,0:T(8,128)(2,1)S(1)} %add_convert_fusion.1), channel_id=1, source_target_pairs={{0,2},{1,3},{2,0},{3,1},{4,6},{5,7},{6,4},{7,5},{8,10},{9,11},{10,... | collective-permute-start | bytes 184328 | tf_op jit(solution)/shard_map/ppermute | solution.py:904
  68.3 2.4 %last.1 = f32[4,32,128]{2,1,0:T(8,128)S(1)} custom-call(f32[5,8,128]{2,1,0:T(8,128)S(1)} %get-tuple-element.56.flags, f32[4,32,128]{2,1,0:T(8,128)S(1)} %finish.1.refs_0_, f32[4,32,128]{2,1,0:T(8,128)S(1)} %collective-permute-done.7.refs_1_, f32[4,32,128]{2,1,0:T(8,128)S(1)} %collective-permute-done.8.refs_2_, ...), custom_call_target="tpu_custom_call" | custom-call | flops 1000000000 | bytes 1000000 | tf_op jit(solution)/shard_map/last/pallas_call | solution.py:764
  70.6 1.6 %collective-permute-done.16 = bf16[240,128]{1,0:T(8,128)(2,1)S(1)} collective-permute-done((bf16[240,128]{1,0:T(8,128)(2,1)S(1)}, bf16[240,128]{1,0:T(8,128)(2,1)S(1)}, u32[]{:S(2)}, u32[]{:S(2)}) %collective-permute-start.16) | collective-permute-done | bytes 61472 | tf_op jit(solution)/shard_map/ppermute | solution.py:904
  74.4 1.4 %collective-permute-start.20 = (bf16[240,128]{1,0:T(8,128)(2,1)S(1)}, bf16[240,128]{1,0:T(8,128)(2,1)S(1)}, u32[]{:S(2)}, u32[]{:S(2)}) collective-permute-start(bf16[240,128]{1,0:T(8,128)(2,1)S(1)} %add_convert_fusion.refs_0_), channel_id=1, source_target_pairs={{0,24},{8,16},{16,8},{24,0},{1,25},{9,17},{17,9},{25,1},{2,26},{10... | collective-permute-start | bytes 184328 | tf_op jit(solution)/shard_map/ppermute | solution.py:904
  76.6 1.9 %collective-permute-done.19.refs_2_ = bf16[240,128]{1,0:T(8,128)(2,1)S(1)} collective-permute-done((bf16[240,128]{1,0:T(8,128)(2,1)S(1)}, bf16[240,128]{1,0:T(8,128)(2,1)S(1)}, u32[]{:S(2)}, u32[]{:S(2)}) %collective-permute-start.19) | collective-permute-done | bytes 61472 | tf_op jit(solution)/shard_map/ppermute | solution.py:904
  81.2 1.4 %unpack.1 = (f32[9,2,64]{2,1,0:T(2,128)}, f32[64]{0:T(128)}, f32[5,9,64,64]{3,2,1,0:T(8,128)}, f32[5,64]{1,0:T(8,128)}, f32[9,64,64]{2,1,0:T(8,128)}, /*index=5*/f32[64]{0:T(128)}) custom-call(f32[5,8,128]{2,1,0:T(8,128)S(1)} %get-tuple-element.56.flags, bf16[960,128]{1,0:T(8,128)(2,1)S(1)} %arrange.1.mine, bf16[960,128]{1,0:T(8,128)(2,1)S(1)} %collective-permute-done.21.other), custom_call_target="tpu_custom_call" | custom-call | flops 10000000 | bytes 1000000 | tf_op jit(solution)/shard_map/unpack/pallas_call | solution.py:764
  (42 shorter events, 13.4 us)
Async XLA Ops:
  0.6 7.5 %collective-permute-start = (f32[2,2,16,128]{3,2,1,0:T(8,128)}, f32[2,2,16,128]{3,2,1,0:T(8,128)S(1)}, u32[]{:S(2)}, u32[]{:S(2)}) collective-permute-start(f32[2,2,16,128]{3,2,1,0:T(8,128)} %refs_0_.1), channel_id=1, source_target_pairs={{0,1},{1,0},{2,3},{3,2},{4,5},{5,4},{6,7},{7,6},{8,9},{9,8},{10,11... | collective-permute-start | bytes 98312 | tf_op jit(solution)/shard_map/ppermute | solution.py:904
  1.2 7.0 %collective-permute-start.1 = (f32[2,2,16,128]{3,2,1,0:T(8,128)}, f32[2,2,16,128]{3,2,1,0:T(8,128)S(1)}, u32[]{:S(2)}, u32[]{:S(2)}) collective-permute-start(f32[2,2,16,128]{3,2,1,0:T(8,128)} %refs_0_.1), channel_id=1, source_target_pairs={{0,7},{1,2},{2,1},{3,4},{4,3},{5,6},{6,5},{7,0},{8,15},{9,10},{10,... | collective-permute-start | bytes 98312 | tf_op jit(solution)/shard_map/ppermute | solution.py:929
  5.9 4.1 %collective-permute-start.2 = (f32[2,2,16,128]{3,2,1,0:T(8,128)}, f32[2,2,16,128]{3,2,1,0:T(8,128)S(1)}, u32[]{:S(2)}, u32[]{:S(2)}) collective-permute-start(f32[2,2,16,128]{3,2,1,0:T(8,128)} %refs_0_.1), channel_id=1, source_target_pairs={{0,6},{1,3},{2,0},{3,5},{4,2},{5,7},{6,4},{7,1},{8,14},{9,11},{10,... | collective-permute-start | bytes 98312 | tf_op jit(solution)/shard_map/ppermute | solution.py:929
  6.3 3.7 %collective-permute-start.3 = (f32[2,2,16,128]{3,2,1,0:T(8,128)}, f32[2,2,16,128]{3,2,1,0:T(8,128)S(1)}, u32[]{:S(2)}, u32[]{:S(2)}) collective-permute-start(f32[2,2,16,128]{3,2,1,0:T(8,128)} %refs_1_.2), channel_id=1, source_target_pairs={{0,1},{1,0},{2,3},{3,2},{4,5},{5,4},{6,7},{7,6},{8,9},{9,8},{10,11... | collective-permute-start | bytes 98312 | tf_op jit(solution)/shard_map/ppermute | solution.py:904
  17.9 4.8 %collective-permute-start.4 = (f32[4,32,128]{2,1,0:T(8,128)S(1)}, f32[4,32,128]{2,1,0:T(8,128)S(1)}, u32[]{:S(2)}, u32[]{:S(2)}) collective-permute-start(f32[4,32,128]{2,1,0:T(8,128)S(1)} %get-tuple-element.65.refs_0_), channel_id=1, source_target_pairs={{0,6},{1,7},{2,0},{3,1},{4,2},{5,3},{6,4},{7,5},{8,14},{9,15},{10,... | collective-permute-start | bytes 196616 | tf_op jit(solution)/shard_map/ppermute | solution.py:909
  20.1 6.3 %collective-permute-start.5 = (f32[4,32,128]{2,1,0:T(8,128)S(1)}, f32[4,32,128]{2,1,0:T(8,128)S(1)}, u32[]{:S(2)}, u32[]{:S(2)}) collective-permute-start(f32[4,32,128]{2,1,0:T(8,128)S(1)} %get-tuple-element.65.refs_0_), channel_id=1, source_target_pairs={{0,4},{1,5},{2,6},{3,7},{4,0},{5,1},{6,2},{7,3},{8,12},{9,13},{10,... | collective-permute-start | bytes 196616 | tf_op jit(solution)/shard_map/ppermute | solution.py:909
  20.1 6.3 %collective-permute-start.6 = (f32[4,32,128]{2,1,0:T(8,128)S(1)}, f32[4,32,128]{2,1,0:T(8,128)S(1)}, u32[]{:S(2)}, u32[]{:S(2)}) collective-permute-start(f32[4,32,128]{2,1,0:T(8,128)S(1)} %get-tuple-element.65.refs_0_), channel_id=1, source_target_pairs={{0,2},{1,3},{2,4},{3,5},{4,6},{5,7},{6,0},{7,1},{8,10},{9,11},{10,... | collective-permute-start | bytes 196616 | tf_op jit(solution)/shard_map/ppermute | solution.py:909
  39.8 7.5 %collective-permute-start.7 = (f32[4,32,128]{2,1,0:T(8,128)S(1)}, f32[4,32,128]{2,1,0:T(8,128)S(1)}, u32[]{:S(2)}, u32[]{:S(2)}) collective-permute-start(f32[4,32,128]{2,1,0:T(8,128)S(1)} %finish.1.refs_0_), channel_id=1, source_target_pairs={{0,6},{1,7},{2,0},{3,1},{4,2},{5,3},{6,4},{7,5},{8,14},{9,15},{10,... | collective-permute-start | bytes 196616 | tf_op jit(solution)/shard_map/ppermute | solution.py:909
  41.6 6.4 %collective-permute-start.8 = (f32[4,32,128]{2,1,0:T(8,128)S(1)}, f32[4,32,128]{2,1,0:T(8,128)S(1)}, u32[]{:S(2)}, u32[]{:S(2)}) collective-permute-start(f32[4,32,128]{2,1,0:T(8,128)S(1)} %finish.1.refs_0_), channel_id=1, source_target_pairs={{0,4},{1,5},{2,6},{3,7},{4,0},{5,1},{6,2},{7,3},{8,12},{9,13},{10,... | collective-permute-start | bytes 196616 | tf_op jit(solution)/shard_map/ppermute | solution.py:909
  41.6 6.4 %collective-permute-start.9 = (f32[4,32,128]{2,1,0:T(8,128)S(1)}, f32[4,32,128]{2,1,0:T(8,128)S(1)}, u32[]{:S(2)}, u32[]{:S(2)}) collective-permute-start(f32[4,32,128]{2,1,0:T(8,128)S(1)} %finish.1.refs_0_), channel_id=1, source_target_pairs={{0,2},{1,3},{2,4},{3,5},{4,6},{5,7},{6,0},{7,1},{8,10},{9,11},{10,... | collective-permute-start | bytes 196616 | tf_op jit(solution)/shard_map/ppermute | solution.py:909
  54.6 1.8 %collective-permute-start.11 = (bf16[960,128]{1,0:T(8,128)(2,1)S(1)}, bf16[960,128]{1,0:T(8,128)(2,1)S(1)}, u32[]{:S(2)}, u32[]{:S(2)}) collective-permute-start(bf16[960,128]{1,0:T(8,128)(2,1)S(1)} %half.2.refs_4_), channel_id=1, source_target_pairs={{0,1},{1,0},{2,3},{3,2},{4,5},{5,4},{6,7},{7,6},{8,9},{9,8},{10,11... | collective-permute-start | bytes 737288 | tf_op jit(solution)/shard_map/ppermute | solution.py:904
  56.5 5.7 %collective-permute-start.14 = (bf16[240,128]{1,0:T(8,128)(2,1)S(1)}, bf16[240,128]{1,0:T(8,128)(2,1)S(1)}, u32[]{:S(2)}, u32[]{:S(2)}) collective-permute-start(bf16[240,128]{1,0:T(8,128)(2,1)S(1)} %get-tuple-element.97), channel_id=1, source_target_pairs={{0,24},{8,16},{16,8},{24,0},{1,25},{9,17},{17,9},{25,1},{2,26},{10... | collective-permute-start | bytes 184328 | tf_op jit(solution)/shard_map/ppermute | solution.py:904
  59.0 4.5 %collective-permute-start.13 = (bf16[240,128]{1,0:T(8,128)(2,1)S(1)}, bf16[240,128]{1,0:T(8,128)(2,1)S(1)}, u32[]{:S(2)}, u32[]{:S(2)}) collective-permute-start(bf16[240,128]{1,0:T(8,128)(2,1)S(1)} %get-tuple-element.96), channel_id=1, source_target_pairs={{0,16},{8,24},{16,0},{24,8},{1,17},{9,25},{17,1},{25,9},{2,18},{10... | collective-permute-start | bytes 184328 | tf_op jit(solution)/shard_map/ppermute | solution.py:904
  59.5 4.2 %collective-permute-start.12 = (bf16[240,128]{1,0:T(8,128)(2,1)S(1)}, bf16[240,128]{1,0:T(8,128)(2,1)S(1)}, u32[]{:S(2)}, u32[]{:S(2)}) collective-permute-start(bf16[240,128]{1,0:T(8,128)(2,1)S(1)} %get-tuple-element.95), channel_id=1, source_target_pairs={{0,8},{8,0},{16,24},{24,16},{1,9},{9,1},{17,25},{25,17},{2,10},{10... | collective-permute-start | bytes 184328 | tf_op jit(solution)/shard_map/ppermute | solution.py:904
  63.8 6.8 %collective-permute-start.17 = (bf16[240,128]{1,0:T(8,128)(2,1)S(1)}, bf16[240,128]{1,0:T(8,128)(2,1)S(1)}, u32[]{:S(2)}, u32[]{:S(2)}) collective-permute-start(bf16[240,128]{1,0:T(8,128)(2,1)S(1)} %add_convert_fusion.1), channel_id=1, source_target_pairs={{0,6},{1,7},{2,4},{3,5},{4,2},{5,3},{6,0},{7,1},{8,14},{9,15},{10,... | collective-permute-start | bytes 184328 | tf_op jit(solution)/shard_map/ppermute | solution.py:904
  65.5 6.8 %collective-permute-start.16 = (bf16[240,128]{1,0:T(8,128)(2,1)S(1)}, bf16[240,128]{1,0:T(8,128)(2,1)S(1)}, u32[]{:S(2)}, u32[]{:S(2)}) collective-permute-start(bf16[240,128]{1,0:T(8,128)(2,1)S(1)} %add_convert_fusion.1), channel_id=1, source_target_pairs={{0,4},{1,5},{2,6},{3,7},{4,0},{5,1},{6,2},{7,3},{8,12},{9,13},{10,... | collective-permute-start | bytes 184328 | tf_op jit(solution)/shard_map/ppermute | solution.py:904
  66.1 6.1 %collective-permute-start.15 = (bf16[240,128]{1,0:T(8,128)(2,1)S(1)}, bf16[240,128]{1,0:T(8,128)(2,1)S(1)}, u32[]{:S(2)}, u32[]{:S(2)}) collective-permute-start(bf16[240,128]{1,0:T(8,128)(2,1)S(1)} %add_convert_fusion.1), channel_id=1, source_target_pairs={{0,2},{1,3},{2,0},{3,1},{4,6},{5,7},{6,4},{7,5},{8,10},{9,11},{10,... | collective-permute-start | bytes 184328 | tf_op jit(solution)/shard_map/ppermute | solution.py:904
  72.3 4.3 %collective-permute-start.18 = (bf16[240,128]{1,0:T(8,128)(2,1)S(1)}, bf16[240,128]{1,0:T(8,128)(2,1)S(1)}, u32[]{:S(2)}, u32[]{:S(2)}) collective-permute-start(bf16[240,128]{1,0:T(8,128)(2,1)S(1)} %add_convert_fusion.refs_0_), channel_id=1, source_target_pairs={{0,8},{8,0},{16,24},{24,16},{1,9},{9,1},{17,25},{25,17},{2,10},{10... | collective-permute-start | bytes 184328 | tf_op jit(solution)/shard_map/ppermute | solution.py:904
  73.7 4.8 %collective-permute-start.19 = (bf16[240,128]{1,0:T(8,128)(2,1)S(1)}, bf16[240,128]{1,0:T(8,128)(2,1)S(1)}, u32[]{:S(2)}, u32[]{:S(2)}) collective-permute-start(bf16[240,128]{1,0:T(8,128)(2,1)S(1)} %add_convert_fusion.refs_0_), channel_id=1, source_target_pairs={{0,16},{8,24},{16,0},{24,8},{1,17},{9,25},{17,1},{25,9},{2,18},{10... | collective-permute-start | bytes 184328 | tf_op jit(solution)/shard_map/ppermute | solution.py:904
  74.4 5.1 %collective-permute-start.20 = (bf16[240,128]{1,0:T(8,128)(2,1)S(1)}, bf16[240,128]{1,0:T(8,128)(2,1)S(1)}, u32[]{:S(2)}, u32[]{:S(2)}) collective-permute-start(bf16[240,128]{1,0:T(8,128)(2,1)S(1)} %add_convert_fusion.refs_0_), channel_id=1, source_target_pairs={{0,24},{8,16},{16,8},{24,0},{1,25},{9,17},{17,9},{25,1},{2,26},{10... | collective-permute-start | bytes 184328 | tf_op jit(solution)/shard_map/ppermute | solution.py:904
  75.9 3.9 %collective-permute-start.10 = (f32[4,16,128]{2,1,0:T(8,128)S(1)}, f32[4,16,128]{2,1,0:T(8,128)S(1)}, u32[]{:S(2)}, u32[]{:S(2)}) collective-permute-start(f32[4,16,128]{2,1,0:T(8,128)S(1)} %get-tuple-element.107), channel_id=1, source_target_pairs={{0,1},{1,0},{2,3},{3,2},{4,5},{5,4},{6,7},{7,6},{8,9},{9,8},{10,11... | collective-permute-start | bytes 98312 | tf_op jit(solution)/shard_map/ppermute | solution.py:904
  79.6 1.6 %collective-permute-start.21 = (bf16[960,128]{1,0:T(8,128)(2,1)S(1)}, bf16[960,128]{1,0:T(8,128)(2,1)S(1)}, u32[]{:S(2)}, u32[]{:S(2)}) collective-permute-start(bf16[960,128]{1,0:T(8,128)(2,1)S(1)} %arrange.1.mine), channel_id=1, source_target_pairs={{0,1},{1,0},{2,3},{3,2},{4,5},{5,4},{6,7},{7,6},{8,9},{9,8},{10,11... | collective-permute-start | bytes 737288 | tf_op jit(solution)/shard_map/ppermute | solution.py:904

commit v4 on v3

--- a/solution.py
+++ b/solution.py
@@ -96,19 +96,74 @@
     return jnp.concatenate([x[N - MARGIN :], x[: count + MARGIN]], axis=0)
 
 
+def with_row_above(v, above):
+    first = lax.broadcasted_iota(jnp.int32, v.shape, 0) == 0
+    return jnp.where(first, jnp.broadcast_to(above, v.shape), rows(v, -1))
+
+
+def divergence(u, v, above):
+    return u - lanes(u, -1) + (v - with_row_above(v, above))
+
+
+def write_messages(fields, top, bottom, far):
+    count = fields[0].shape[0]
+    rest = count - MARGIN
+    zero = jnp.zeros((1, N), f32)
+    sources = [divergence(fields[2 * i], fields[2 * i + 1], zero) for i in range(2)]
+
+    def ends(row):
+        return [jnp.concatenate([fields[1][row : row + 1], fields[3][row : row + 1], jnp.zeros((6, N), f32)], axis=0)]
+
+    parts = [x[:MARGIN] for x in fields] + [x[MARGIN:] for x in sources if rest] + ends(count - 1)
+    top[...] = jnp.concatenate(parts, axis=0)
+    parts = [x[rest:] for x in fields] + [x[:rest] for x in sources if rest] + ends(max(rest - 1, 0))
+    bottom[...] = jnp.concatenate(parts, axis=0)
+    far[...] = jnp.concatenate(sources + ends(count - 1), axis=0)
+
+
+def read_messages(kind, block, messages):
+    count = block.shape[1]
+    rest = count - MARGIN
+    top, far, bottom = messages[0], messages[1:-1], messages[-1]
+    cut = lambda ref, start, size: ref[start : start + size, :]
+    u, v = block[2 * kind], block[2 * kind + 1]
+    top_u, top_v = [cut(top, (2 * kind + i) * MARGIN, MARGIN) for i in range(2)]
+    low_u, low_v = [cut(bottom, (2 * kind + i) * MARGIN, MARGIN) for i in range(2)]
+    source = [divergence(u, v, low_v[MARGIN - 1 :]), divergence(top_u, top_v, v[count - 1 :])]
+    fields = 4 * MARGIN
+    last = top_v[MARGIN - 1 :]
+    if rest:
+        source.append(cut(top, fields + kind * rest, rest))
+        last = cut(top, fields + 2 * rest + kind, 1)
+    first = lax.broadcasted_iota(jnp.int32, (count, N), 0) == 0
+    for ref in far:
+        x = cut(ref, kind * count, count)
+        source.append(x - jnp.where(first, jnp.broadcast_to(last, x.shape), 0.0))
+        last = cut(ref, 2 * count + kind, 1)
+    if rest:
+        x = cut(bottom, fields + kind * rest, rest)
+        source.append(x - jnp.where(first[:rest], jnp.broadcast_to(last, x.shape), 0.0))
+        last = cut(bottom, fields + 2 * rest + kind, 1)
+    source.append(divergence(low_u, low_v, last))
+    return [
+        jnp.concatenate([low_u, u, top_u], axis=0),
+        jnp.concatenate([low_v, v, top_v], axis=0),
+        jnp.concatenate(source, axis=0),
+    ]
+
+
 def project(fields, count, right, left, weight):
     number = len(fields)
-    source = [u - lanes(u, -1) + (v - rows(v, -1)) for u, v in fields]
-    x = times_right(jnp.concatenate(source, axis=0), right)
+    x = times_right(jnp.concatenate([source for _, _, source in fields], axis=0), right)
     x = jnp.concatenate([x[i * N : (i + 1) * N] for i in range(number)], axis=1)
     x = times_left(x, left) * jnp.concatenate([weight[...]] * number, axis=1)
     x = local(times_left(x, left), count)
     size = x.shape[0]
     x = times_right(jnp.concatenate([x[:, i * N : (i + 1) * N] for i in range(number)], axis=0), right)
     out = []
-    for i, (u, v) in enumerate(fields):
+    for i, (u, v, _) in enumerate(fields):
         p = -x[i * size : (i + 1) * size]
-        out.append((local(u, count) - (lanes(p, 1) - p), local(v, count) - (rows(p, 1) - p)))
+        out.append((u - (lanes(p, 1) - p), v - (rows(p, 1) - p)))
     return out
 
 
@@ -423,13 +478,16 @@
     lane = lax.broadcasted_iota(jnp.int32, (CH, N), 1)
     extra[...] = jnp.zeros((3 * CH, N), f32)
 
-    @pl.when(half == 1)
-    def _():
+    def first_layer():
         first, total = weight_product(count, 1, fields, feats, grads)
         first = jnp.concatenate([first, jnp.zeros((2 * CH, N - 32), f32)], axis=1)
         extra[:CH, :] = jnp.where(lane == 35, total, first[:CH])
         extra[CH : 2 * CH, :] = first[CH:]
 
+    if not isinstance(half, int):
+        pl.when(half == 1)(first_layer)
+    elif half == 1:
+        first_layer()
     parts, columns = [], extra[:CH, :]
     for i in range(3):
         product, total = weight_product(count, 2 + 3 * half + i, fields, feats, grads)
@@ -546,9 +604,10 @@
         cot[i] = jnp.concatenate(pair(own[1], cot_partner, i), axis=0)
 
 
-def network_kernel(
-    count, vel, extra, w_first, w_hidden, bias, mix, adder, block, interp, raw, clear, fields, feats, slopes, put, kept
-):
+def network_kernel(count, vel, extra, w_first, w_hidden, bias, mix, adder, *refs):
+    block, refs = refs[0], refs[1:]
+    messages = refs[:-8]
+    interp, raw, clear, fields, feats, slopes, put, kept = refs[-8:]
     interleave(vel, fields)
     clear_patches(count, fields, mix, clear, put)
     sums = []
@@ -563,31 +622,28 @@
     for i in range(0, len(sums), 4):
         interpolate(count + RAW - len(sums) + i, sums[i : i + 4], adder, put, interp)
     su, sv = provisional(count, vel[0], vel[1], interp)
-    block[0] = su
-    block[1] = sv
-    block[2] = extra[0]
-    block[3] = extra[1]
-
-
-def joined(gathered, i):
-    return jnp.concatenate([g[i] for g in gathered], axis=0)
+    out = [su, sv, extra[0], extra[1]]
+    for i in range(4):
+        block[i] = out[i]
+    if messages:
+        write_messages(out, *messages)
 
 
 def project_kernel(count, blocks, steps, flags, *refs):
-    gathered, refs = refs[:blocks], refs[blocks:]
+    block, messages, refs = refs[0], refs[1:blocks], refs[blocks:]
     forward, backward = steps
     mg = flags[backward][0:1, :]
-    fields = [(mg * joined(gathered, 2), mg * joined(gathered, 3))]
+    fields = [[mg * x for x in read_messages(1, block, messages)]]
     if forward is None:
         right, left, weight, gstar, own = refs
     else:
         vel, right, left, weight, gstar, own, ext = refs
-        fields.append((joined(gathered, 0), joined(gathered, 1)))
+        fields.append(read_messages(0, block, messages))
         mv = flags[forward][0:1, :]
     out = project(fields, count, right, left, weight)
     for i in range(2):
         gstar[i] = out[0][i]
-        own[i] = (1.0 - mg) * gathered[0][2 + i]
+        own[i] = (1.0 - mg) * block[2 + i]
         if forward is not None:
             ext[i] = vel[i] + mv * (out[1][i] - vel[i])
 
@@ -622,18 +678,19 @@
         input_gradient(count, b_first, gradient_window(grads, count, 1), gvel)
 
 
-def finish_kernel(count, front, base, gstar, interp, gvel, spread, out, lines):
+def finish_kernel(count, front, base, gstar, interp, gvel, spread, block, top, bottom, far, lines):
     change = velocity_gradients(count, gstar[0], gstar[1], interp, spread, lines)
-    for i in range(2):
-        out[i] = front[i]
-        out[2 + i] = base[i] + change[i] + gvel[i]
+    out = [front[0], front[1]] + [base[i] + change[i] + gvel[i] for i in range(2)]
+    for i in range(4):
+        block[i] = out[i]
+    write_messages(out, top, bottom, far)
 
 
 def last_kernel(count, blocks, flags, *refs):
-    gathered, refs = refs[:blocks], refs[blocks:]
+    block, messages, refs = refs[0], refs[1:blocks], refs[blocks:]
     now, right, left, weight, base, ext, gstar, interp, first, b_first, mix, raw, out = refs[:13]
     lines, spread, ginterp, gvel = refs[13:]
-    (news,) = project([(joined(gathered, 0), joined(gathered, 1))], count, right, left, weight)
+    (news,) = project([read_messages(0, block, messages)], count, right, left, weight)
     own = slice(MARGIN, MARGIN + count)
     mask = flags[STEPS - 1][0:1, :]
     for i in range(2):
@@ -658,14 +715,12 @@
 
 
 def weights_kernel(count, fields, feats, grads, buffer, extra):
-    def both(half, _):
-        def put(q, value):
+    for half in range(2):
+
+        def put(q, value, half=half):
             buffer[place(half * HALF + q * 3 * CH, 3 * CH), :] = value
 
         weight_half(count, half, fields, feats, grads, put, extra)
-        return 0
-
-    lax.fori_loop(0, 2, both, 0)
 
 
 def half_kernel(count, side, previous, fields, feats, grads, out, extra):
@@ -818,14 +873,19 @@
     )(*inputs, *after)
 
 
+def message_arrays(count):
+    near = 4 * MARGIN + 2 * (count - MARGIN) + 8
+    return [array(f32, near, N), array(f32, near, N), array(f32, 2 * count + 8, N)]
+
+
 def run_assemble(count, flags, fields):
     out = [array(f32, 2, count + 2 * MARGIN, N), array(f32, 2, count, N)]
     return call(assemble_kernel, "assemble", 10**6, [flags, *fields], out)
 
 
-def run_network(count, vel, extra, weights):
+def run_network(count, vel, extra, weights, last=False):
     local_rows, mid = count + 2 * MARGIN, count + 2 * MID
-    out = [array(f32, 4, count, N), array(f32, 4 * mid, N), array(f32, mid * CH, N), array(f32, mid * 32, N)]
+    out = [array(f32, 4, count, N), *([] if last else message_arrays(count)), array(f32, 4 * mid, N), array(f32, mid * CH, N), array(f32, mid * 32, N)]
     out += [array(f32, 2, 4 * local_rows, N)]
     out += [feature_array(count), gradient_array(count, LAYERS)]
     scratch = [field(4 * mid), field((count + 2 * LAYERS) * CH, 2)]
@@ -854,7 +914,8 @@
 
 def run_finish(count, *inputs):
     kernel = functools.partial(finish_kernel, count)
-    return call(kernel, "finish", 10**9, inputs, array(f32, 4, count, N), [field(4 * count, 2)])
+    out = [array(f32, 4, count, N), *message_arrays(count)]
+    return call(kernel, "finish", 10**9, inputs, out, [field(4 * count, 2)])
 
 
 def run_last(count, flags, gathered, *inputs):
@@ -909,8 +970,10 @@
     return lax.ppermute(x, "strip", [(i, (i - 2 * ahead) % count) for i in range(count)])
 
 
-def gather_groups(x):
-    return [x] + [from_group(x, k) for k in range(1, lax.axis_size("strip") // 2)]
+def gather_groups(block, top, bottom, far):
+    groups = lax.axis_size("strip") // 2
+    others = [from_group(far, k) for k in range(2, groups - 1)]
+    return [block, from_group(top, 1), *others, from_group(bottom, -1)]
 
 
 def margins(velocity, partner, core):
@@ -967,14 +1030,13 @@
     weights = (w_first, w_hidden, bias, mix, adder)
 
     v0, cot = run_assemble(count, flags, (own, partner, cross, same, cot_partner))
-    block, interp0, raw0, clear0, fields0, feats0, slopes0 = run_network(count, v0, cot, weights)
-    gathered = gather_groups(block)
+    block, *sent, interp0, raw0, clear0, fields0, feats0, slopes0 = run_network(count, v0, cot, weights)
+    gathered = gather_groups(block, *sent)
     b_first, b_hidden, tables = run_prepare_back(params, interp0)
     gstar1, base, v1 = run_project(count, (0, 1), flags, gathered, tables, v0)
-    block, interp1, raw1, clear1, fields1, feats1, slopes1 = run_network(count, v1, cot, weights)
+    block, interp1, raw1, clear1, fields1, feats1, slopes1 = run_network(count, v1, cot, weights, last=True)
     grads1, gvel, spread = run_back(count, v1, gstar1, clear1, b_first, b_hidden, slopes1, mix, raw1)
-    block = run_finish(count, block, base, gstar1, interp1, gvel, spread)
-    gathered = gather_groups(block)
+    gathered = gather_groups(*run_finish(count, block, base, gstar1, interp1, gvel, spread))
     buffer = run_weights(count, fields1, feats1, grads1)
     gstar0, base = run_project(count, (None, 0), flags, gathered, tables)
     grads0, first = run_back(count, v0, gstar0, clear0, b_first, b_hidden, slopes0)

time: 82.8 us -> 82.1 us (level)
  transfers between devices with their start and end apart: 22 -> 22, of which waited for: 11 -> 12; matrix products, arithmetic and copies ran while one was open for 1% -> 1% of each run, Pallas kernels for 14% -> 14%
where the time goes in v4:
time: 82.1 us; the launch traced here: 81.9 us
  Pallas kernels  41 us (50%)
  starting transfers between devices  23.7 us (29%)
  waiting for transfers between devices  15.6 us (19%)
    pallas_call x15, Pallas kernels, call(): pl.pallas_call(kernel, in_specs=[VMEM] * len(inputs), out_specs=jax.tree....  37.3 us
    ppermute x14, starting transfers between devices, swap(): return lax.ppermute(x, axis, [(i, i ^ offset) for i in range(count)])  12.2 us
    ppermute x14, waiting for transfers between devices, swap(): return lax.ppermute(x, axis, [(i, i ^ offset) for i in range(count)])  9.48 us
    ppermute x6, starting transfers between devices, from_group(): lax.ppermute(x, 'strip', [(i, (i - 2 * ahead) % count) for i in range(cou...  6.29 us
    ppermute x1, starting transfers between devices, margins(): lax.ppermute(velocity, 'strip', cross)  4.71 us
    ppermute x6, waiting for transfers between devices, from_group(): lax.ppermute(x, 'strip', [(i, (i - 2 * ahead) % count) for i in range(cou...  4.32 us
    pallas_call x2, Pallas kernels, call_from_hbm(): pl.pallas_call(kernel, in_specs=[hbm] * len(inputs) + [VMEM] * len(after)...  3.69 us
    ppermute x1, waiting for transfers between devices, margins(): lax.ppermute(velocity, 'strip', same)  1.82 us
  transfers between devices with their start and end apart: 22, of which 12 were waited for; matrix products, arithmetic and copies ran while one was open for 1% of the time, Pallas kernels for 14%

profile of v4, /device:TPU:0, one launch (start us, length us, event | category | flops | bytes accessed | tf_op | source)
XLA Modules:
  0.0 81.9 jit_solution(12625446469876265966)
XLA Ops:
  1.2 4.7 %collective-permute-start.1 = (f32[2,2,16,128]{3,2,1,0:T(8,128)}, f32[2,2,16,128]{3,2,1,0:T(8,128)S(1)}, u32[]{:S(2)}, u32[]{:S(2)}) collective-permute-start(f32[2,2,16,128]{3,2,1,0:T(8,128)} %refs_0_.1), channel_id=1, source_target_pairs={{0,7},{1,2},{2,1},{3,4},{4,3},{5,6},{6,5},{7,0},{8,15},{9,10},{10,... | collective-permute-start | bytes 98312 | tf_op jit(solution)/shard_map/ppermute | solution.py:992
  6.3 1.8 %prepare.1 = (f32[2,2,16,128]{3,2,1,0:T(8,128)S(1)}, bf16[128,32]{1,0:T(8,128)(2,1)S(1)}, bf16[6,384,256]{2,1,0:T(8,128)(2,1)S(1)}, f32[7,64,128]{2,1,0:T(8,128)...) custom-call(f32[2,2,16,128]{3,2,1,0:T(8,128)} %refs_0_.1, ...), custom_call_target="tpu_custom_call" | custom-call | flops 1000000000 | bytes 1000000 | tf_op jit(solution)/shard_map/prepare/pallas_call | solution.py:864
  8.2 1.8 %collective-permute-done.2.same = f32[2,2,16,128]{3,2,1,0:T(8,128)S(1)} collective-permute-done((f32[2,2,16,128]{3,2,1,0:T(8,128)}, f32[2,2,16,128]{3,2,1,0:T(8,128)S(1)}, u32[]{:S(2)}, u32[]{:S(2)}) %collective-permute-start.2) | collective-permute-done | bytes 32800 | tf_op jit(solution)/shard_map/ppermute | solution.py:992
  10.0 8.1 %network.2 = (f32[4,32,128]{2,1,0:T(8,128)S(1)}, f32[104,128]{1,0:T(8,128)S(1)}, f32[104,128]{1,0:T(8,128)S(1)}, f32[72,128]{1,0:T(8,128)S(1)}, f32[192,128]{1,0...) custom-call(f32[2,64,128]{2,1,0:T(8,128)S(1)} %get-tuple-element.65., ...), custom_call_target="tpu_custom_call" | custom-call | flops 4000000000 | bytes 1000000 | tf_op jit(solution)/shard_map/network/pallas_call | solution.py:819
  18.2 2.3 %collective-permute-start.4 = (f32[104,128]{1,0:T(8,128)S(1)}, f32[104,128]{1,0:T(8,128)S(1)}, u32[]{:S(2)}, u32[]{:S(2)}) collective-permute-start(f32[104,128]{1,0:T(8,128)S(1)} %get-tuple-element.73), channel_id=1, source_target_pairs={{0,6},{1,7},{2,0},{3,1},{4,2},{5,3},{6,4},{7,5},{8,14},{9,15},{10,... | collective-permute-start | bytes 159752 | tf_op jit(solution)/shard_map/ppermute | solution.py:970
  21.1 1.9 %prepare_back.1 = (bf16[16,256]{1,0:T(8,128)(2,1)S(1)}, bf16[6,384,256]{2,1,0:T(8,128)(2,1)S(1)}, bf16[384,128]{1,0:T(8,128)(2,1)S(1)}, bf16[128,384]{1,0:T(8,128)(2,1)S(1)}, f32[128,128]{1,0:T(8,128)S(1)}) custom-call(bf16[9,2,64]{2,1,0:T(2,128)(2,1)} %bitcast.12, bf16[5,9,64,64]{3,2,1,0:T(8,128)(2,1)} %refs_1_.3, bf16[9,64,64]{2,1,0:T(8,128)(2,1)} %refs_2_.1, ...), custom_call_target="tpu_custom_call" | custom-call | flops 1000000000 | bytes 1000000 | tf_op jit(solution)/shard_map/prepare_back/pallas_call | solution.py:864
  22.9 2.4 %collective-permute-done.5.refs_2_ = f32[72,128]{1,0:T(8,128)S(1)} collective-permute-done((f32[72,128]{1,0:T(8,128)S(1)}, f32[72,128]{1,0:T(8,128)S(1)}, u32[]{:S(2)}, u32[]{:S(2)}) %collective-permute-start.5) | collective-permute-done | bytes 36896 | tf_op jit(solution)/shard_map/ppermute | solution.py:970
  27.3 8.1 %network.3 = (f32[4,32,128]{2,1,0:T(8,128)S(1)}, f32[192,128]{1,0:T(8,128)S(1)}, f32[3072,128]{1,0:T(8,128)S(1)}, f32[1536,128]{1,0:T(8,128)S(1)}, f32[2,256,128...) custom-call(f32[2,64,128]{2,1,0:T(8,128)S(1)} %get-tuple-element.80.vel.ext.refs_4_, ...), custom_call_target="tpu_custom_call" | custom-call | flops 4000000000 | bytes 1000000 | tf_op jit(solution)/shard_map/network/pallas_call | solution.py:819
  35.3 4.4 %back.2 = (bf16[21504,128]{1,0:T(8,128)(2,1)S(1)}, f32[2,32,128]{2,1,0:T(8,128)S(1)}, f32[2,4,192,128]{3,2,1,0:T(8,128)S(1)}) custom-call(f32[2,64,128]{2,1,0:T(8,128)S(1)} %get-tuple-element.80.vel.ext.refs_4_, f32[2,64,128]{2,1,0:T(8,128)S(1)} %get-tuple-element.83.gstar, f32[1536,128]{1,0:T(8,128)S(1)} %get-tuple-element.85.clear, ...), custom_call_target="tpu_custom_call" | custom-call | flops 4000000000 | bytes 1000000 | tf_op jit(solution)/shard_map/back/pallas_call | solution.py:819
  41.4 1.9 %collective-permute-start.9 = (f32[104,128]{1,0:T(8,128)S(1)}, f32[104,128]{1,0:T(8,128)S(1)}, u32[]{:S(2)}, u32[]{:S(2)}) collective-permute-start(f32[104,128]{1,0:T(8,128)S(1)} %get-tuple-element.95), channel_id=1, source_target_pairs={{0,2},{1,3},{2,4},{3,5},{4,6},{5,7},{6,0},{7,1},{8,10},{9,11},{10,... | collective-permute-start | bytes 159752 | tf_op jit(solution)/shard_map/ppermute | solution.py:970
  43.4 3.1 %weights.1.previous.refs_0_ = f32[1920,128]{1,0:T(8,128)S(1)} custom-call(f32[2,256,128]{2,1,0:T(8,128)S(1)} %get-tuple-element.102.fields, bf16[21504,128]{1,0:T(8,128)(2,1)S(1)} %get-tuple-element.103.feats, bf16[21504,128]{1,0:T(8,128)(2,1)S(1)} %get-tuple-element.104.grads), custom_call_target="tpu_custom_call" | custom-call | flops 3000000000 | bytes 1000000 | tf_op jit(solution)/shard_map/weights/pallas_call | solution.py:819
  48.1 3.8 %back.3 = (bf16[21504,128]{1,0:T(8,128)(2,1)S(1)}, bf16[2176,128]{1,0:T(8,128)(2,1)S(1)}) custom-call(f32[2,64,128]{2,1,0:T(8,128)S(1)} %get-tuple-element.65.vel.refs_4_.ext.refs_9_, f32[2,64,128]{2,1,0:T(8,128)S(1)} %get-tuple-element.97.gstar.refs_10_, f32[1536,128]{1,0:T(8,128)S(1)} %get-tuple-element.98.clear, ...), custom_call_target="tpu_custom_call" | custom-call | flops 4000000000 | bytes 1000000 | tf_op jit(solution)/shard_map/back/pallas_call | solution.py:819
  51.9 2.0 %half.2.refs_4_ = bf16[960,128]{1,0:T(8,128)(2,1)S(1)} custom-call(f32[1920,128]{1,0:T(8,128)S(1)} %weights.1.previous.refs_0_, f32[2,256,128]{2,1,0:T(8,128)S(1)} %get-tuple-element.105.fields.refs_1_, bf16[21504,128]{1,0:T(8,128)(2,1)S(1)} %get-tuple-element.106.feats.refs_2_, bf16[21504,128]{1,0:T(8,128)(2,1)S(1)} %get-tuple-element.107.grads.refs_3_), custom_call_target="tpu_custom_call" | custom-call | flops 1000000000 | bytes 1000000 | tf_op jit(solution)/shard_map/half/pallas_call | solution.py:819
  54.0 2.0 %half.3.keep = bf16[960,128]{1,0:T(8,128)(2,1)S(1)} custom-call(f32[1920,128]{1,0:T(8,128)S(1)} %weights.1.previous.refs_0_, f32[2,256,128]{2,1,0:T(8,128)S(1)} %get-tuple-element.105.fields.refs_1_, bf16[21504,128]{1,0:T(8,128)(2,1)S(1)} %get-tuple-element.106.feats.refs_2_, bf16[21504,128]{1,0:T(8,128)(2,1)S(1)} %get-tuple-element.107.grads.refs_3_, ...), custom_call_target="tpu_custom_call" | custom-call | flops 1000000000 | bytes 1000000 | tf_op jit(solution)/shard_map/half/pallas_call | solution.py:819
  56.1 2.5 %collective-permute-start.14 = (bf16[240,128]{1,0:T(8,128)(2,1)S(1)}, bf16[240,128]{1,0:T(8,128)(2,1)S(1)}, u32[]{:S(2)}, u32[]{:S(2)}) collective-permute-start(bf16[240,128]{1,0:T(8,128)(2,1)S(1)} %get-tuple-element.111), channel_id=1, source_target_pairs={{0,24},{8,16},{16,8},{24,0},{1,25},{9,17},{17,9},{25,1},{2,26},{10... | collective-permute-start | bytes 184328 | tf_op jit(solution)/shard_map/ppermute | solution.py:965
  59.6 2.1 %collective-permute-done.14 = bf16[240,128]{1,0:T(8,128)(2,1)S(1)} collective-permute-done((bf16[240,128]{1,0:T(8,128)(2,1)S(1)}, bf16[240,128]{1,0:T(8,128)(2,1)S(1)}, u32[]{:S(2)}, u32[]{:S(2)}) %collective-permute-start.14) | collective-permute-done | bytes 61472 | tf_op jit(solution)/shard_map/ppermute | solution.py:965
  61.7 1.3 %collective-permute-done.13 = bf16[240,128]{1,0:T(8,128)(2,1)S(1)} collective-permute-done((bf16[240,128]{1,0:T(8,128)(2,1)S(1)}, bf16[240,128]{1,0:T(8,128)(2,1)S(1)}, u32[]{:S(2)}, u32[]{:S(2)}) %collective-permute-start.13) | collective-permute-done | bytes 61472 | tf_op jit(solution)/shard_map/ppermute | solution.py:965
  63.4 1.4 %collective-permute-start.17 = (bf16[240,128]{1,0:T(8,128)(2,1)S(1)}, bf16[240,128]{1,0:T(8,128)(2,1)S(1)}, u32[]{:S(2)}, u32[]{:S(2)}) collective-permute-start(bf16[240,128]{1,0:T(8,128)(2,1)S(1)} %add_convert_fusion.1), channel_id=1, source_target_pairs={{0,6},{1,7},{2,4},{3,5},{4,2},{5,3},{6,0},{7,1},{8,14},{9,15},{10,... | collective-permute-start | bytes 184328 | tf_op jit(solution)/shard_map/ppermute | solution.py:965
  65.0 2.8 %collective-permute-start.15 = (bf16[240,128]{1,0:T(8,128)(2,1)S(1)}, bf16[240,128]{1,0:T(8,128)(2,1)S(1)}, u32[]{:S(2)}, u32[]{:S(2)}) collective-permute-start(bf16[240,128]{1,0:T(8,128)(2,1)S(1)} %add_convert_fusion.1), channel_id=1, source_target_pairs={{0,2},{1,3},{2,0},{3,1},{4,6},{5,7},{6,4},{7,5},{8,10},{9,11},{10,... | collective-permute-start | bytes 184328 | tf_op jit(solution)/shard_map/ppermute | solution.py:965
  67.8 2.4 %last.1 = f32[4,32,128]{2,1,0:T(8,128)S(1)} custom-call(f32[5,8,128]{2,1,0:T(8,128)S(1)} %get-tuple-element.63.flags, f32[4,32,128]{2,1,0:T(8,128)S(1)} %get-tuple-element.92.refs_0_, f32[104,128]{1,0:T(8,128)S(1)} %collective-permute-done.7.refs_1_, f32[72,128]{1,0:T(8,128)S(1)} %collective-permute-done.8.refs_2_, ...), custom_call_target="tpu_custom_call" | custom-call | flops 1000000000 | bytes 1000000 | tf_op jit(solution)/shard_map/last/pallas_call | solution.py:819
  71.3 1.8 %collective-permute-start.18 = (bf16[240,128]{1,0:T(8,128)(2,1)S(1)}, bf16[240,128]{1,0:T(8,128)(2,1)S(1)}, u32[]{:S(2)}, u32[]{:S(2)}) collective-permute-start(bf16[240,128]{1,0:T(8,128)(2,1)S(1)} %add_convert_fusion.refs_0_), channel_id=1, source_target_pairs={{0,8},{8,0},{16,24},{24,16},{1,9},{9,1},{17,25},{25,17},{2,10},{10... | collective-permute-start | bytes 184328 | tf_op jit(solution)/shard_map/ppermute | solution.py:965
  73.6 1.3 %collective-permute-start.20 = (bf16[240,128]{1,0:T(8,128)(2,1)S(1)}, bf16[240,128]{1,0:T(8,128)(2,1)S(1)}, u32[]{:S(2)}, u32[]{:S(2)}) collective-permute-start(bf16[240,128]{1,0:T(8,128)(2,1)S(1)} %add_convert_fusion.refs_0_), channel_id=1, source_target_pairs={{0,24},{8,16},{16,8},{24,0},{1,25},{9,17},{17,9},{25,1},{2,26},{10... | collective-permute-start | bytes 184328 | tf_op jit(solution)/shard_map/ppermute | solution.py:965
  75.6 2.3 %collective-permute-done.19.refs_2_ = bf16[240,128]{1,0:T(8,128)(2,1)S(1)} collective-permute-done((bf16[240,128]{1,0:T(8,128)(2,1)S(1)}, bf16[240,128]{1,0:T(8,128)(2,1)S(1)}, u32[]{:S(2)}, u32[]{:S(2)}) %collective-permute-start.19) | collective-permute-done | bytes 61472 | tf_op jit(solution)/shard_map/ppermute | solution.py:965
  80.4 1.4 %unpack.1 = (f32[9,2,64]{2,1,0:T(2,128)}, f32[64]{0:T(128)}, f32[5,9,64,64]{3,2,1,0:T(8,128)}, f32[5,64]{1,0:T(8,128)}, f32[9,64,64]{2,1,0:T(8,128)}, /*index=5*/f32[64]{0:T(128)}) custom-call(f32[5,8,128]{2,1,0:T(8,128)S(1)} %get-tuple-element.63.flags, bf16[960,128]{1,0:T(8,128)(2,1)S(1)} %arrange.1.mine, bf16[960,128]{1,0:T(8,128)(2,1)S(1)} %collective-permute-done.21.other), custom_call_target="tpu_custom_call" | custom-call | flops 10000000 | bytes 1000000 | tf_op jit(solution)/shard_map/unpack/pallas_call | solution.py:819
  (42 shorter events, 13.5 us)
Async XLA Ops:
  0.6 7.5 %collective-permute-start = (f32[2,2,16,128]{3,2,1,0:T(8,128)}, f32[2,2,16,128]{3,2,1,0:T(8,128)S(1)}, u32[]{:S(2)}, u32[]{:S(2)}) collective-permute-start(f32[2,2,16,128]{3,2,1,0:T(8,128)} %refs_0_.1), channel_id=1, source_target_pairs={{0,1},{1,0},{2,3},{3,2},{4,5},{5,4},{6,7},{7,6},{8,9},{9,8},{10,11... | collective-permute-start | bytes 98312 | tf_op jit(solution)/shard_map/ppermute | solution.py:965
  1.2 7.0 %collective-permute-start.1 = (f32[2,2,16,128]{3,2,1,0:T(8,128)}, f32[2,2,16,128]{3,2,1,0:T(8,128)S(1)}, u32[]{:S(2)}, u32[]{:S(2)}) collective-permute-start(f32[2,2,16,128]{3,2,1,0:T(8,128)} %refs_0_.1), channel_id=1, source_target_pairs={{0,7},{1,2},{2,1},{3,4},{4,3},{5,6},{6,5},{7,0},{8,15},{9,10},{10,... | collective-permute-start | bytes 98312 | tf_op jit(solution)/shard_map/ppermute | solution.py:992
  5.9 4.1 %collective-permute-start.2 = (f32[2,2,16,128]{3,2,1,0:T(8,128)}, f32[2,2,16,128]{3,2,1,0:T(8,128)S(1)}, u32[]{:S(2)}, u32[]{:S(2)}) collective-permute-start(f32[2,2,16,128]{3,2,1,0:T(8,128)} %refs_0_.1), channel_id=1, source_target_pairs={{0,6},{1,3},{2,0},{3,5},{4,2},{5,7},{6,4},{7,1},{8,14},{9,11},{10,... | collective-permute-start | bytes 98312 | tf_op jit(solution)/shard_map/ppermute | solution.py:992
  6.3 3.7 %collective-permute-start.3 = (f32[2,2,16,128]{3,2,1,0:T(8,128)}, f32[2,2,16,128]{3,2,1,0:T(8,128)S(1)}, u32[]{:S(2)}, u32[]{:S(2)}) collective-permute-start(f32[2,2,16,128]{3,2,1,0:T(8,128)} %refs_1_.2), channel_id=1, source_target_pairs={{0,1},{1,0},{2,3},{3,2},{4,5},{5,4},{6,7},{7,6},{8,9},{9,8},{10,11... | collective-permute-start | bytes 98312 | tf_op jit(solution)/shard_map/ppermute | solution.py:965
  18.2 7.1 %collective-permute-start.4 = (f32[104,128]{1,0:T(8,128)S(1)}, f32[104,128]{1,0:T(8,128)S(1)}, u32[]{:S(2)}, u32[]{:S(2)}) collective-permute-start(f32[104,128]{1,0:T(8,128)S(1)} %get-tuple-element.73), channel_id=1, source_target_pairs={{0,6},{1,7},{2,0},{3,1},{4,2},{5,3},{6,4},{7,5},{8,14},{9,15},{10,... | collective-permute-start | bytes 159752 | tf_op jit(solution)/shard_map/ppermute | solution.py:970
  20.4 4.9 %collective-permute-start.5 = (f32[72,128]{1,0:T(8,128)S(1)}, f32[72,128]{1,0:T(8,128)S(1)}, u32[]{:S(2)}, u32[]{:S(2)}) collective-permute-start(f32[72,128]{1,0:T(8,128)S(1)} %get-tuple-element.74), channel_id=1, source_target_pairs={{0,4},{1,5},{2,6},{3,7},{4,0},{5,1},{6,2},{7,3},{8,12},{9,13},{10,... | collective-permute-start | bytes 110600 | tf_op jit(solution)/shard_map/ppermute | solution.py:970
  20.4 5.9 %collective-permute-start.6 = (f32[104,128]{1,0:T(8,128)S(1)}, f32[104,128]{1,0:T(8,128)S(1)}, u32[]{:S(2)}, u32[]{:S(2)}) collective-permute-start(f32[104,128]{1,0:T(8,128)S(1)} %get-tuple-element.75), channel_id=1, source_target_pairs={{0,2},{1,3},{2,4},{3,5},{4,6},{5,7},{6,0},{7,1},{8,10},{9,11},{10,... | collective-permute-start | bytes 159752 | tf_op jit(solution)/shard_map/ppermute | solution.py:970
  40.0 6.5 %collective-permute-start.7 = (f32[104,128]{1,0:T(8,128)S(1)}, f32[104,128]{1,0:T(8,128)S(1)}, u32[]{:S(2)}, u32[]{:S(2)}) collective-permute-start(f32[104,128]{1,0:T(8,128)S(1)} %get-tuple-element.93), channel_id=1, source_target_pairs={{0,6},{1,7},{2,0},{3,1},{4,2},{5,3},{6,4},{7,5},{8,14},{9,15},{10,... | collective-permute-start | bytes 159752 | tf_op jit(solution)/shard_map/ppermute | solution.py:970
  40.9 5.5 %collective-permute-start.8 = (f32[72,128]{1,0:T(8,128)S(1)}, f32[72,128]{1,0:T(8,128)S(1)}, u32[]{:S(2)}, u32[]{:S(2)}) collective-permute-start(f32[72,128]{1,0:T(8,128)S(1)} %get-tuple-element.94), channel_id=1, source_target_pairs={{0,4},{1,5},{2,6},{3,7},{4,0},{5,1},{6,2},{7,3},{8,12},{9,13},{10,... | collective-permute-start | bytes 110600 | tf_op jit(solution)/shard_map/ppermute | solution.py:970
  41.4 5.9 %collective-permute-start.9 = (f32[104,128]{1,0:T(8,128)S(1)}, f32[104,128]{1,0:T(8,128)S(1)}, u32[]{:S(2)}, u32[]{:S(2)}) collective-permute-start(f32[104,128]{1,0:T(8,128)S(1)} %get-tuple-element.95), channel_id=1, source_target_pairs={{0,2},{1,3},{2,4},{3,5},{4,6},{5,7},{6,0},{7,1},{8,10},{9,11},{10,... | collective-permute-start | bytes 159752 | tf_op jit(solution)/shard_map/ppermute | solution.py:970
  53.9 2.0 %collective-permute-start.11 = (bf16[960,128]{1,0:T(8,128)(2,1)S(1)}, bf16[960,128]{1,0:T(8,128)(2,1)S(1)}, u32[]{:S(2)}, u32[]{:S(2)}) collective-permute-start(bf16[960,128]{1,0:T(8,128)(2,1)S(1)} %half.2.refs_4_), channel_id=1, source_target_pairs={{0,1},{1,0},{2,3},{3,2},{4,5},{5,4},{6,7},{7,6},{8,9},{9,8},{10,11... | collective-permute-start | bytes 737288 | tf_op jit(solution)/shard_map/ppermute | solution.py:965
  56.1 5.7 %collective-permute-start.14 = (bf16[240,128]{1,0:T(8,128)(2,1)S(1)}, bf16[240,128]{1,0:T(8,128)(2,1)S(1)}, u32[]{:S(2)}, u32[]{:S(2)}) collective-permute-start(bf16[240,128]{1,0:T(8,128)(2,1)S(1)} %get-tuple-element.111), channel_id=1, source_target_pairs={{0,24},{8,16},{16,8},{24,0},{1,25},{9,17},{17,9},{25,1},{2,26},{10... | collective-permute-start | bytes 184328 | tf_op jit(solution)/shard_map/ppermute | solution.py:965
  58.6 4.5 %collective-permute-start.13 = (bf16[240,128]{1,0:T(8,128)(2,1)S(1)}, bf16[240,128]{1,0:T(8,128)(2,1)S(1)}, u32[]{:S(2)}, u32[]{:S(2)}) collective-permute-start(bf16[240,128]{1,0:T(8,128)(2,1)S(1)} %get-tuple-element.110), channel_id=1, source_target_pairs={{0,16},{8,24},{16,0},{24,8},{1,17},{9,25},{17,1},{25,9},{2,18},{10... | collective-permute-start | bytes 184328 | tf_op jit(solution)/shard_map/ppermute | solution.py:965
  59.1 4.2 %collective-permute-start.12 = (bf16[240,128]{1,0:T(8,128)(2,1)S(1)}, bf16[240,128]{1,0:T(8,128)(2,1)S(1)}, u32[]{:S(2)}, u32[]{:S(2)}) collective-permute-start(bf16[240,128]{1,0:T(8,128)(2,1)S(1)} %get-tuple-element.109), channel_id=1, source_target_pairs={{0,8},{8,0},{16,24},{24,16},{1,9},{9,1},{17,25},{25,17},{2,10},{10... | collective-permute-start | bytes 184328 | tf_op jit(solution)/shard_map/ppermute | solution.py:965
  63.4 6.8 %collective-permute-start.17 = (bf16[240,128]{1,0:T(8,128)(2,1)S(1)}, bf16[240,128]{1,0:T(8,128)(2,1)S(1)}, u32[]{:S(2)}, u32[]{:S(2)}) collective-permute-start(bf16[240,128]{1,0:T(8,128)(2,1)S(1)} %add_convert_fusion.1), channel_id=1, source_target_pairs={{0,6},{1,7},{2,4},{3,5},{4,2},{5,3},{6,0},{7,1},{8,14},{9,15},{10,... | collective-permute-start | bytes 184328 | tf_op jit(solution)/shard_map/ppermute | solution.py:965
  64.8 6.5 %collective-permute-start.16 = (bf16[240,128]{1,0:T(8,128)(2,1)S(1)}, bf16[240,128]{1,0:T(8,128)(2,1)S(1)}, u32[]{:S(2)}, u32[]{:S(2)}) collective-permute-start(bf16[240,128]{1,0:T(8,128)(2,1)S(1)} %add_convert_fusion.1), channel_id=1, source_target_pairs={{0,4},{1,5},{2,6},{3,7},{4,0},{5,1},{6,2},{7,3},{8,12},{9,13},{10,... | collective-permute-start | bytes 184328 | tf_op jit(solution)/shard_map/ppermute | solution.py:965
  65.0 6.3 %collective-permute-start.15 = (bf16[240,128]{1,0:T(8,128)(2,1)S(1)}, bf16[240,128]{1,0:T(8,128)(2,1)S(1)}, u32[]{:S(2)}, u32[]{:S(2)}) collective-permute-start(bf16[240,128]{1,0:T(8,128)(2,1)S(1)} %add_convert_fusion.1), channel_id=1, source_target_pairs={{0,2},{1,3},{2,0},{3,1},{4,6},{5,7},{6,4},{7,5},{8,10},{9,11},{10,... | collective-permute-start | bytes 184328 | tf_op jit(solution)/shard_map/ppermute | solution.py:965
  71.3 4.3 %collective-permute-start.18 = (bf16[240,128]{1,0:T(8,128)(2,1)S(1)}, bf16[240,128]{1,0:T(8,128)(2,1)S(1)}, u32[]{:S(2)}, u32[]{:S(2)}) collective-permute-start(bf16[240,128]{1,0:T(8,128)(2,1)S(1)} %add_convert_fusion.refs_0_), channel_id=1, source_target_pairs={{0,8},{8,0},{16,24},{24,16},{1,9},{9,1},{17,25},{25,17},{2,10},{10... | collective-permute-start | bytes 184328 | tf_op jit(solution)/shard_map/ppermute | solution.py:965
  73.2 4.8 %collective-permute-start.19 = (bf16[240,128]{1,0:T(8,128)(2,1)S(1)}, bf16[240,128]{1,0:T(8,128)(2,1)S(1)}, u32[]{:S(2)}, u32[]{:S(2)}) collective-permute-start(bf16[240,128]{1,0:T(8,128)(2,1)S(1)} %add_convert_fusion.refs_0_), channel_id=1, source_target_pairs={{0,16},{8,24},{16,0},{24,8},{1,17},{9,25},{17,1},{25,9},{2,18},{10... | collective-permute-start | bytes 184328 | tf_op jit(solution)/shard_map/ppermute | solution.py:965
  73.6 5.1 %collective-permute-start.20 = (bf16[240,128]{1,0:T(8,128)(2,1)S(1)}, bf16[240,128]{1,0:T(8,128)(2,1)S(1)}, u32[]{:S(2)}, u32[]{:S(2)}) collective-permute-start(bf16[240,128]{1,0:T(8,128)(2,1)S(1)} %add_convert_fusion.refs_0_), channel_id=1, source_target_pairs={{0,24},{8,16},{16,8},{24,0},{1,25},{9,17},{17,9},{25,1},{2,26},{10... | collective-permute-start | bytes 184328 | tf_op jit(solution)/shard_map/ppermute | solution.py:965
  74.9 4.0 %collective-permute-start.10 = (f32[4,16,128]{2,1,0:T(8,128)S(1)}, f32[4,16,128]{2,1,0:T(8,128)S(1)}, u32[]{:S(2)}, u32[]{:S(2)}) collective-permute-start(f32[4,16,128]{2,1,0:T(8,128)S(1)} %get-tuple-element.121), channel_id=1, source_target_pairs={{0,1},{1,0},{2,3},{3,2},{4,5},{5,4},{6,7},{7,6},{8,9},{9,8},{10,11... | collective-permute-start | bytes 98312 | tf_op jit(solution)/shard_map/ppermute | solution.py:965
  78.8 1.6 %collective-permute-start.21 = (bf16[960,128]{1,0:T(8,128)(2,1)S(1)}, bf16[960,128]{1,0:T(8,128)(2,1)S(1)}, u32[]{:S(2)}, u32[]{:S(2)}) collective-permute-start(bf16[960,128]{1,0:T(8,128)(2,1)S(1)} %arrange.1.mine), channel_id=1, source_target_pairs={{0,1},{1,0},{2,3},{3,2},{4,5},{5,4},{6,7},{7,6},{8,9},{9,8},{10,11... | collective-permute-start | bytes 737288 | tf_op jit(solution)/shard_map/ppermute | solution.py:965

commit v5 on v4

--- a/solution.py
+++ b/solution.py
@@ -105,20 +105,23 @@
     return u - lanes(u, -1) + (v - with_row_above(v, above))
 
 
-def write_messages(fields, top, bottom, far):
-    count = fields[0].shape[0]
+def write_messages(kind, u, v, top, bottom, far):
+    count = u.shape[0]
     rest = count - MARGIN
-    zero = jnp.zeros((1, N), f32)
-    sources = [divergence(fields[2 * i], fields[2 * i + 1], zero) for i in range(2)]
-
-    def ends(row):
-        return [jnp.concatenate([fields[1][row : row + 1], fields[3][row : row + 1], jnp.zeros((6, N), f32)], axis=0)]
-
-    parts = [x[:MARGIN] for x in fields] + [x[MARGIN:] for x in sources if rest] + ends(count - 1)
-    top[...] = jnp.concatenate(parts, axis=0)
-    parts = [x[rest:] for x in fields] + [x[:rest] for x in sources if rest] + ends(max(rest - 1, 0))
-    bottom[...] = jnp.concatenate(parts, axis=0)
-    far[...] = jnp.concatenate(sources + ends(count - 1), axis=0)
+    fields = 4 * MARGIN
+    source = divergence(u, v, jnp.zeros((1, N), f32))
+    for i, x in enumerate((u, v)):
+        at = slice((2 * kind + i) * MARGIN, (2 * kind + i + 1) * MARGIN)
+        top[at, :] = x[:MARGIN]
+        bottom[at, :] = x[rest:]
+    if rest:
+        at = slice(fields + kind * rest, fields + (kind + 1) * rest)
+        top[at, :] = source[MARGIN:]
+        bottom[at, :] = source[:rest]
+        bottom[fields + 2 * rest + kind : fields + 2 * rest + kind + 1, :] = v[rest - 1 : rest]
+    top[fields + 2 * rest + kind : fields + 2 * rest + kind + 1, :] = v[count - 1 :]
+    far[kind * count : (kind + 1) * count, :] = source
+    far[2 * count + kind : 2 * count + kind + 1, :] = v[count - 1 :]
 
 
 def read_messages(kind, block, messages):
@@ -608,6 +611,8 @@
     block, refs = refs[0], refs[1:]
     messages = refs[:-8]
     interp, raw, clear, fields, feats, slopes, put, kept = refs[-8:]
+    if messages:
+        write_messages(1, extra[0], extra[1], *messages)
     interleave(vel, fields)
     clear_patches(count, fields, mix, clear, put)
     sums = []
@@ -626,7 +631,7 @@
     for i in range(4):
         block[i] = out[i]
     if messages:
-        write_messages(out, *messages)
+        write_messages(0, su, sv, *messages)
 
 
 def project_kernel(count, blocks, steps, flags, *refs):
@@ -683,7 +688,8 @@
     out = [front[0], front[1]] + [base[i] + change[i] + gvel[i] for i in range(2)]
     for i in range(4):
         block[i] = out[i]
-    write_messages(out, top, bottom, far)
+    for kind in range(2):
+        write_messages(kind, out[2 * kind], out[2 * kind + 1], top, bottom, far)
 
 
 def last_kernel(count, blocks, flags, *refs):

time: 82.1 us -> 82 us (level)
  no operation moved by 1% of the time
where the time goes in v5:
time: 82 us; the launch traced here: 81.9 us
  Pallas kernels  41 us (50%)
  starting transfers between devices  23.7 us (29%)
  waiting for transfers between devices  15.6 us (19%)
    pallas_call x15, Pallas kernels, call(): pl.pallas_call(kernel, in_specs=[VMEM] * len(inputs), out_specs=jax.tree....  37.3 us
    ppermute x14, starting transfers between devices, swap(): return lax.ppermute(x, axis, [(i, i ^ offset) for i in range(count)])  12.2 us
    ppermute x14, waiting for transfers between devices, swap(): return lax.ppermute(x, axis, [(i, i ^ offset) for i in range(count)])  9.48 us
    ppermute x6, starting transfers between devices, from_group(): lax.ppermute(x, 'strip', [(i, (i - 2 * ahead) % count) for i in range(cou...  6.28 us
    ppermute x1, starting transfers between devices, margins(): lax.ppermute(velocity, 'strip', cross)  4.71 us
    ppermute x6, waiting for transfers between devices, from_group(): lax.ppermute(x, 'strip', [(i, (i - 2 * ahead) % count) for i in range(cou...  4.33 us
    pallas_call x2, Pallas kernels, call_from_hbm(): pl.pallas_call(kernel, in_specs=[hbm] * len(inputs) + [VMEM] * len(after)...  3.69 us
    ppermute x1, waiting for transfers between devices, margins(): lax.ppermute(velocity, 'strip', same)  1.82 us
  transfers between devices with their start and end apart: 22, of which 12 were waited for; matrix products, arithmetic and copies ran while one was open for 1% of the time, Pallas kernels for 14%

profile of v5, /device:TPU:0, one launch (start us, length us, event | category | flops | bytes accessed | tf_op | source)
XLA Modules:
  0.0 81.9 jit_solution(16485764025937886392)
XLA Ops:
  1.2 4.7 %collective-permute-start.1 = (f32[2,2,16,128]{3,2,1,0:T(8,128)}, f32[2,2,16,128]{3,2,1,0:T(8,128)S(1)}, u32[]{:S(2)}, u32[]{:S(2)}) collective-permute-start(f32[2,2,16,128]{3,2,1,0:T(8,128)} %refs_0_.1), channel_id=1, source_target_pairs={{0,7},{1,2},{2,1},{3,4},{4,3},{5,6},{6,5},{7,0},{8,15},{9,10},{10,... | collective-permute-start | bytes 98312 | tf_op jit(solution)/shard_map/ppermute | solution.py:998
  6.3 1.8 %prepare.1 = (f32[2,2,16,128]{3,2,1,0:T(8,128)S(1)}, bf16[128,32]{1,0:T(8,128)(2,1)S(1)}, bf16[6,384,256]{2,1,0:T(8,128)(2,1)S(1)}, f32[7,64,128]{2,1,0:T(8,128)...) custom-call(f32[2,2,16,128]{3,2,1,0:T(8,128)} %refs_0_.1, ...), custom_call_target="tpu_custom_call" | custom-call | flops 1000000000 | bytes 1000000 | tf_op jit(solution)/shard_map/prepare/pallas_call | solution.py:870
  8.2 1.8 %collective-permute-done.2.same = f32[2,2,16,128]{3,2,1,0:T(8,128)S(1)} collective-permute-done((f32[2,2,16,128]{3,2,1,0:T(8,128)}, f32[2,2,16,128]{3,2,1,0:T(8,128)S(1)}, u32[]{:S(2)}, u32[]{:S(2)}) %collective-permute-start.2) | collective-permute-done | bytes 32800 | tf_op jit(solution)/shard_map/ppermute | solution.py:998
  10.0 8.1 %network.2 = (f32[4,32,128]{2,1,0:T(8,128)S(1)}, f32[104,128]{1,0:T(8,128)S(1)}, f32[104,128]{1,0:T(8,128)S(1)}, f32[72,128]{1,0:T(8,128)S(1)}, f32[192,128]{1,0...) custom-call(f32[2,64,128]{2,1,0:T(8,128)S(1)} %get-tuple-element.65., ...), custom_call_target="tpu_custom_call" | custom-call | flops 4000000000 | bytes 1000000 | tf_op jit(solution)/shard_map/network/pallas_call | solution.py:825
  18.1 2.3 %collective-permute-start.4 = (f32[104,128]{1,0:T(8,128)S(1)}, f32[104,128]{1,0:T(8,128)S(1)}, u32[]{:S(2)}, u32[]{:S(2)}) collective-permute-start(f32[104,128]{1,0:T(8,128)S(1)} %get-tuple-element.73), channel_id=1, source_target_pairs={{0,6},{1,7},{2,0},{3,1},{4,2},{5,3},{6,4},{7,5},{8,14},{9,15},{10,... | collective-permute-start | bytes 159752 | tf_op jit(solution)/shard_map/ppermute | solution.py:976
  21.0 1.9 %prepare_back.1 = (bf16[16,256]{1,0:T(8,128)(2,1)S(1)}, bf16[6,384,256]{2,1,0:T(8,128)(2,1)S(1)}, bf16[384,128]{1,0:T(8,128)(2,1)S(1)}, bf16[128,384]{1,0:T(8,128)(2,1)S(1)}, f32[128,128]{1,0:T(8,128)S(1)}) custom-call(bf16[9,2,64]{2,1,0:T(2,128)(2,1)} %bitcast.12, bf16[5,9,64,64]{3,2,1,0:T(8,128)(2,1)} %refs_1_.3, bf16[9,64,64]{2,1,0:T(8,128)(2,1)} %refs_2_.1, ...), custom_call_target="tpu_custom_call" | custom-call | flops 1000000000 | bytes 1000000 | tf_op jit(solution)/shard_map/prepare_back/pallas_call | solution.py:870
  22.9 2.4 %collective-permute-done.5.refs_2_ = f32[72,128]{1,0:T(8,128)S(1)} collective-permute-done((f32[72,128]{1,0:T(8,128)S(1)}, f32[72,128]{1,0:T(8,128)S(1)}, u32[]{:S(2)}, u32[]{:S(2)}) %collective-permute-start.5) | collective-permute-done | bytes 36896 | tf_op jit(solution)/shard_map/ppermute | solution.py:976
  27.3 8.1 %network.3 = (f32[4,32,128]{2,1,0:T(8,128)S(1)}, f32[192,128]{1,0:T(8,128)S(1)}, f32[3072,128]{1,0:T(8,128)S(1)}, f32[1536,128]{1,0:T(8,128)S(1)}, f32[2,256,128...) custom-call(f32[2,64,128]{2,1,0:T(8,128)S(1)} %get-tuple-element.80.vel.ext.refs_4_, ...), custom_call_target="tpu_custom_call" | custom-call | flops 4000000000 | bytes 1000000 | tf_op jit(solution)/shard_map/network/pallas_call | solution.py:825
  35.3 4.4 %back.2 = (bf16[21504,128]{1,0:T(8,128)(2,1)S(1)}, f32[2,32,128]{2,1,0:T(8,128)S(1)}, f32[2,4,192,128]{3,2,1,0:T(8,128)S(1)}) custom-call(f32[2,64,128]{2,1,0:T(8,128)S(1)} %get-tuple-element.80.vel.ext.refs_4_, f32[2,64,128]{2,1,0:T(8,128)S(1)} %get-tuple-element.83.gstar, f32[1536,128]{1,0:T(8,128)S(1)} %get-tuple-element.85.clear, ...), custom_call_target="tpu_custom_call" | custom-call | flops 4000000000 | bytes 1000000 | tf_op jit(solution)/shard_map/back/pallas_call | solution.py:825
  41.4 1.9 %collective-permute-start.9 = (f32[104,128]{1,0:T(8,128)S(1)}, f32[104,128]{1,0:T(8,128)S(1)}, u32[]{:S(2)}, u32[]{:S(2)}) collective-permute-start(f32[104,128]{1,0:T(8,128)S(1)} %get-tuple-element.95), channel_id=1, source_target_pairs={{0,2},{1,3},{2,4},{3,5},{4,6},{5,7},{6,0},{7,1},{8,10},{9,11},{10,... | collective-permute-start | bytes 159752 | tf_op jit(solution)/shard_map/ppermute | solution.py:976
  43.4 3.1 %weights.1.previous.refs_0_ = f32[1920,128]{1,0:T(8,128)S(1)} custom-call(f32[2,256,128]{2,1,0:T(8,128)S(1)} %get-tuple-element.102.fields, bf16[21504,128]{1,0:T(8,128)(2,1)S(1)} %get-tuple-element.103.feats, bf16[21504,128]{1,0:T(8,128)(2,1)S(1)} %get-tuple-element.104.grads), custom_call_target="tpu_custom_call" | custom-call | flops 3000000000 | bytes 1000000 | tf_op jit(solution)/shard_map/weights/pallas_call | solution.py:825
  48.1 3.8 %back.3 = (bf16[21504,128]{1,0:T(8,128)(2,1)S(1)}, bf16[2176,128]{1,0:T(8,128)(2,1)S(1)}) custom-call(f32[2,64,128]{2,1,0:T(8,128)S(1)} %get-tuple-element.65.vel.refs_4_.ext.refs_9_, f32[2,64,128]{2,1,0:T(8,128)S(1)} %get-tuple-element.97.gstar.refs_10_, f32[1536,128]{1,0:T(8,128)S(1)} %get-tuple-element.98.clear, ...), custom_call_target="tpu_custom_call" | custom-call | flops 4000000000 | bytes 1000000 | tf_op jit(solution)/shard_map/back/pallas_call | solution.py:825
  51.9 2.0 %half.2.refs_4_ = bf16[960,128]{1,0:T(8,128)(2,1)S(1)} custom-call(f32[1920,128]{1,0:T(8,128)S(1)} %weights.1.previous.refs_0_, f32[2,256,128]{2,1,0:T(8,128)S(1)} %get-tuple-element.105.fields.refs_1_, bf16[21504,128]{1,0:T(8,128)(2,1)S(1)} %get-tuple-element.106.feats.refs_2_, bf16[21504,128]{1,0:T(8,128)(2,1)S(1)} %get-tuple-element.107.grads.refs_3_), custom_call_target="tpu_custom_call" | custom-call | flops 1000000000 | bytes 1000000 | tf_op jit(solution)/shard_map/half/pallas_call | solution.py:825
  54.0 2.0 %half.3.keep = bf16[960,128]{1,0:T(8,128)(2,1)S(1)} custom-call(f32[1920,128]{1,0:T(8,128)S(1)} %weights.1.previous.refs_0_, f32[2,256,128]{2,1,0:T(8,128)S(1)} %get-tuple-element.105.fields.refs_1_, bf16[21504,128]{1,0:T(8,128)(2,1)S(1)} %get-tuple-element.106.feats.refs_2_, bf16[21504,128]{1,0:T(8,128)(2,1)S(1)} %get-tuple-element.107.grads.refs_3_, ...), custom_call_target="tpu_custom_call" | custom-call | flops 1000000000 | bytes 1000000 | tf_op jit(solution)/shard_map/half/pallas_call | solution.py:825
  56.1 2.5 %collective-permute-start.14 = (bf16[240,128]{1,0:T(8,128)(2,1)S(1)}, bf16[240,128]{1,0:T(8,128)(2,1)S(1)}, u32[]{:S(2)}, u32[]{:S(2)}) collective-permute-start(bf16[240,128]{1,0:T(8,128)(2,1)S(1)} %get-tuple-element.111), channel_id=1, source_target_pairs={{0,24},{8,16},{16,8},{24,0},{1,25},{9,17},{17,9},{25,1},{2,26},{10... | collective-permute-start | bytes 184328 | tf_op jit(solution)/shard_map/ppermute | solution.py:971
  59.6 2.1 %collective-permute-done.14 = bf16[240,128]{1,0:T(8,128)(2,1)S(1)} collective-permute-done((bf16[240,128]{1,0:T(8,128)(2,1)S(1)}, bf16[240,128]{1,0:T(8,128)(2,1)S(1)}, u32[]{:S(2)}, u32[]{:S(2)}) %collective-permute-start.14) | collective-permute-done | bytes 61472 | tf_op jit(solution)/shard_map/ppermute | solution.py:971
  61.7 1.3 %collective-permute-done.13 = bf16[240,128]{1,0:T(8,128)(2,1)S(1)} collective-permute-done((bf16[240,128]{1,0:T(8,128)(2,1)S(1)}, bf16[240,128]{1,0:T(8,128)(2,1)S(1)}, u32[]{:S(2)}, u32[]{:S(2)}) %collective-permute-start.13) | collective-permute-done | bytes 61472 | tf_op jit(solution)/shard_map/ppermute | solution.py:971
  63.4 1.5 %collective-permute-start.17 = (bf16[240,128]{1,0:T(8,128)(2,1)S(1)}, bf16[240,128]{1,0:T(8,128)(2,1)S(1)}, u32[]{:S(2)}, u32[]{:S(2)}) collective-permute-start(bf16[240,128]{1,0:T(8,128)(2,1)S(1)} %add_convert_fusion.1), channel_id=1, source_target_pairs={{0,6},{1,7},{2,4},{3,5},{4,2},{5,3},{6,0},{7,1},{8,14},{9,15},{10,... | collective-permute-start | bytes 184328 | tf_op jit(solution)/shard_map/ppermute | solution.py:971
  65.0 2.8 %collective-permute-start.15 = (bf16[240,128]{1,0:T(8,128)(2,1)S(1)}, bf16[240,128]{1,0:T(8,128)(2,1)S(1)}, u32[]{:S(2)}, u32[]{:S(2)}) collective-permute-start(bf16[240,128]{1,0:T(8,128)(2,1)S(1)} %add_convert_fusion.1), channel_id=1, source_target_pairs={{0,2},{1,3},{2,0},{3,1},{4,6},{5,7},{6,4},{7,5},{8,10},{9,11},{10,... | collective-permute-start | bytes 184328 | tf_op jit(solution)/shard_map/ppermute | solution.py:971
  67.8 2.4 %last.1 = f32[4,32,128]{2,1,0:T(8,128)S(1)} custom-call(f32[5,8,128]{2,1,0:T(8,128)S(1)} %get-tuple-element.63.flags, f32[4,32,128]{2,1,0:T(8,128)S(1)} %get-tuple-element.92.refs_0_, f32[104,128]{1,0:T(8,128)S(1)} %collective-permute-done.7.refs_1_, f32[72,128]{1,0:T(8,128)S(1)} %collective-permute-done.8.refs_2_, ...), custom_call_target="tpu_custom_call" | custom-call | flops 1000000000 | bytes 1000000 | tf_op jit(solution)/shard_map/last/pallas_call | solution.py:825
  71.3 1.8 %collective-permute-start.18 = (bf16[240,128]{1,0:T(8,128)(2,1)S(1)}, bf16[240,128]{1,0:T(8,128)(2,1)S(1)}, u32[]{:S(2)}, u32[]{:S(2)}) collective-permute-start(bf16[240,128]{1,0:T(8,128)(2,1)S(1)} %add_convert_fusion.refs_0_), channel_id=1, source_target_pairs={{0,8},{8,0},{16,24},{24,16},{1,9},{9,1},{17,25},{25,17},{2,10},{10... | collective-permute-start | bytes 184328 | tf_op jit(solution)/shard_map/ppermute | solution.py:971
  73.6 1.3 %collective-permute-start.20 = (bf16[240,128]{1,0:T(8,128)(2,1)S(1)}, bf16[240,128]{1,0:T(8,128)(2,1)S(1)}, u32[]{:S(2)}, u32[]{:S(2)}) collective-permute-start(bf16[240,128]{1,0:T(8,128)(2,1)S(1)} %add_convert_fusion.refs_0_), channel_id=1, source_target_pairs={{0,24},{8,16},{16,8},{24,0},{1,25},{9,17},{17,9},{25,1},{2,26},{10... | collective-permute-start | bytes 184328 | tf_op jit(solution)/shard_map/ppermute | solution.py:971
  75.6 2.3 %collective-permute-done.19.refs_2_ = bf16[240,128]{1,0:T(8,128)(2,1)S(1)} collective-permute-done((bf16[240,128]{1,0:T(8,128)(2,1)S(1)}, bf16[240,128]{1,0:T(8,128)(2,1)S(1)}, u32[]{:S(2)}, u32[]{:S(2)}) %collective-permute-start.19) | collective-permute-done | bytes 61472 | tf_op jit(solution)/shard_map/ppermute | solution.py:971
  80.4 1.4 %unpack.1 = (f32[9,2,64]{2,1,0:T(2,128)}, f32[64]{0:T(128)}, f32[5,9,64,64]{3,2,1,0:T(8,128)}, f32[5,64]{1,0:T(8,128)}, f32[9,64,64]{2,1,0:T(8,128)}, /*index=5*/f32[64]{0:T(128)}) custom-call(f32[5,8,128]{2,1,0:T(8,128)S(1)} %get-tuple-element.63.flags, bf16[960,128]{1,0:T(8,128)(2,1)S(1)} %arrange.1.mine, bf16[960,128]{1,0:T(8,128)(2,1)S(1)} %collective-permute-done.21.other), custom_call_target="tpu_custom_call" | custom-call | flops 10000000 | bytes 1000000 | tf_op jit(solution)/shard_map/unpack/pallas_call | solution.py:825
  (42 shorter events, 13.5 us)
Async XLA Ops:
  0.6 7.5 %collective-permute-start = (f32[2,2,16,128]{3,2,1,0:T(8,128)}, f32[2,2,16,128]{3,2,1,0:T(8,128)S(1)}, u32[]{:S(2)}, u32[]{:S(2)}) collective-permute-start(f32[2,2,16,128]{3,2,1,0:T(8,128)} %refs_0_.1), channel_id=1, source_target_pairs={{0,1},{1,0},{2,3},{3,2},{4,5},{5,4},{6,7},{7,6},{8,9},{9,8},{10,11... | collective-permute-start | bytes 98312 | tf_op jit(solution)/shard_map/ppermute | solution.py:971
  1.2 7.0 %collective-permute-start.1 = (f32[2,2,16,128]{3,2,1,0:T(8,128)}, f32[2,2,16,128]{3,2,1,0:T(8,128)S(1)}, u32[]{:S(2)}, u32[]{:S(2)}) collective-permute-start(f32[2,2,16,128]{3,2,1,0:T(8,128)} %refs_0_.1), channel_id=1, source_target_pairs={{0,7},{1,2},{2,1},{3,4},{4,3},{5,6},{6,5},{7,0},{8,15},{9,10},{10,... | collective-permute-start | bytes 98312 | tf_op jit(solution)/shard_map/ppermute | solution.py:998
  5.9 4.1 %collective-permute-start.2 = (f32[2,2,16,128]{3,2,1,0:T(8,128)}, f32[2,2,16,128]{3,2,1,0:T(8,128)S(1)}, u32[]{:S(2)}, u32[]{:S(2)}) collective-permute-start(f32[2,2,16,128]{3,2,1,0:T(8,128)} %refs_0_.1), channel_id=1, source_target_pairs={{0,6},{1,3},{2,0},{3,5},{4,2},{5,7},{6,4},{7,1},{8,14},{9,11},{10,... | collective-permute-start | bytes 98312 | tf_op jit(solution)/shard_map/ppermute | solution.py:998
  6.3 3.7 %collective-permute-start.3 = (f32[2,2,16,128]{3,2,1,0:T(8,128)}, f32[2,2,16,128]{3,2,1,0:T(8,128)S(1)}, u32[]{:S(2)}, u32[]{:S(2)}) collective-permute-start(f32[2,2,16,128]{3,2,1,0:T(8,128)} %refs_1_.2), channel_id=1, source_target_pairs={{0,1},{1,0},{2,3},{3,2},{4,5},{5,4},{6,7},{7,6},{8,9},{9,8},{10,11... | collective-permute-start | bytes 98312 | tf_op jit(solution)/shard_map/ppermute | solution.py:971
  18.1 7.1 %collective-permute-start.4 = (f32[104,128]{1,0:T(8,128)S(1)}, f32[104,128]{1,0:T(8,128)S(1)}, u32[]{:S(2)}, u32[]{:S(2)}) collective-permute-start(f32[104,128]{1,0:T(8,128)S(1)} %get-tuple-element.73), channel_id=1, source_target_pairs={{0,6},{1,7},{2,0},{3,1},{4,2},{5,3},{6,4},{7,5},{8,14},{9,15},{10,... | collective-permute-start | bytes 159752 | tf_op jit(solution)/shard_map/ppermute | solution.py:976
  20.4 4.9 %collective-permute-start.5 = (f32[72,128]{1,0:T(8,128)S(1)}, f32[72,128]{1,0:T(8,128)S(1)}, u32[]{:S(2)}, u32[]{:S(2)}) collective-permute-start(f32[72,128]{1,0:T(8,128)S(1)} %get-tuple-element.74), channel_id=1, source_target_pairs={{0,4},{1,5},{2,6},{3,7},{4,0},{5,1},{6,2},{7,3},{8,12},{9,13},{10,... | collective-permute-start | bytes 110600 | tf_op jit(solution)/shard_map/ppermute | solution.py:976
  20.4 5.9 %collective-permute-start.6 = (f32[104,128]{1,0:T(8,128)S(1)}, f32[104,128]{1,0:T(8,128)S(1)}, u32[]{:S(2)}, u32[]{:S(2)}) collective-permute-start(f32[104,128]{1,0:T(8,128)S(1)} %get-tuple-element.75), channel_id=1, source_target_pairs={{0,2},{1,3},{2,4},{3,5},{4,6},{5,7},{6,0},{7,1},{8,10},{9,11},{10,... | collective-permute-start | bytes 159752 | tf_op jit(solution)/shard_map/ppermute | solution.py:976
  40.0 6.5 %collective-permute-start.7 = (f32[104,128]{1,0:T(8,128)S(1)}, f32[104,128]{1,0:T(8,128)S(1)}, u32[]{:S(2)}, u32[]{:S(2)}) collective-permute-start(f32[104,128]{1,0:T(8,128)S(1)} %get-tuple-element.93), channel_id=1, source_target_pairs={{0,6},{1,7},{2,0},{3,1},{4,2},{5,3},{6,4},{7,5},{8,14},{9,15},{10,... | collective-permute-start | bytes 159752 | tf_op jit(solution)/shard_map/ppermute | solution.py:976
  40.9 5.6 %collective-permute-start.8 = (f32[72,128]{1,0:T(8,128)S(1)}, f32[72,128]{1,0:T(8,128)S(1)}, u32[]{:S(2)}, u32[]{:S(2)}) collective-permute-start(f32[72,128]{1,0:T(8,128)S(1)} %get-tuple-element.94), channel_id=1, source_target_pairs={{0,4},{1,5},{2,6},{3,7},{4,0},{5,1},{6,2},{7,3},{8,12},{9,13},{10,... | collective-permute-start | bytes 110600 | tf_op jit(solution)/shard_map/ppermute | solution.py:976
  41.4 5.9 %collective-permute-start.9 = (f32[104,128]{1,0:T(8,128)S(1)}, f32[104,128]{1,0:T(8,128)S(1)}, u32[]{:S(2)}, u32[]{:S(2)}) collective-permute-start(f32[104,128]{1,0:T(8,128)S(1)} %get-tuple-element.95), channel_id=1, source_target_pairs={{0,2},{1,3},{2,4},{3,5},{4,6},{5,7},{6,0},{7,1},{8,10},{9,11},{10,... | collective-permute-start | bytes 159752 | tf_op jit(solution)/shard_map/ppermute | solution.py:976
  53.9 2.0 %collective-permute-start.11 = (bf16[960,128]{1,0:T(8,128)(2,1)S(1)}, bf16[960,128]{1,0:T(8,128)(2,1)S(1)}, u32[]{:S(2)}, u32[]{:S(2)}) collective-permute-start(bf16[960,128]{1,0:T(8,128)(2,1)S(1)} %half.2.refs_4_), channel_id=1, source_target_pairs={{0,1},{1,0},{2,3},{3,2},{4,5},{5,4},{6,7},{7,6},{8,9},{9,8},{10,11... | collective-permute-start | bytes 737288 | tf_op jit(solution)/shard_map/ppermute | solution.py:971
  56.1 5.7 %collective-permute-start.14 = (bf16[240,128]{1,0:T(8,128)(2,1)S(1)}, bf16[240,128]{1,0:T(8,128)(2,1)S(1)}, u32[]{:S(2)}, u32[]{:S(2)}) collective-permute-start(bf16[240,128]{1,0:T(8,128)(2,1)S(1)} %get-tuple-element.111), channel_id=1, source_target_pairs={{0,24},{8,16},{16,8},{24,0},{1,25},{9,17},{17,9},{25,1},{2,26},{10... | collective-permute-start | bytes 184328 | tf_op jit(solution)/shard_map/ppermute | solution.py:971
  58.6 4.5 %collective-permute-start.13 = (bf16[240,128]{1,0:T(8,128)(2,1)S(1)}, bf16[240,128]{1,0:T(8,128)(2,1)S(1)}, u32[]{:S(2)}, u32[]{:S(2)}) collective-permute-start(bf16[240,128]{1,0:T(8,128)(2,1)S(1)} %get-tuple-element.110), channel_id=1, source_target_pairs={{0,16},{8,24},{16,0},{24,8},{1,17},{9,25},{17,1},{25,9},{2,18},{10... | collective-permute-start | bytes 184328 | tf_op jit(solution)/shard_map/ppermute | solution.py:971
  59.1 4.2 %collective-permute-start.12 = (bf16[240,128]{1,0:T(8,128)(2,1)S(1)}, bf16[240,128]{1,0:T(8,128)(2,1)S(1)}, u32[]{:S(2)}, u32[]{:S(2)}) collective-permute-start(bf16[240,128]{1,0:T(8,128)(2,1)S(1)} %get-tuple-element.109), channel_id=1, source_target_pairs={{0,8},{8,0},{16,24},{24,16},{1,9},{9,1},{17,25},{25,17},{2,10},{10... | collective-permute-start | bytes 184328 | tf_op jit(solution)/shard_map/ppermute | solution.py:971
  63.4 6.8 %collective-permute-start.17 = (bf16[240,128]{1,0:T(8,128)(2,1)S(1)}, bf16[240,128]{1,0:T(8,128)(2,1)S(1)}, u32[]{:S(2)}, u32[]{:S(2)}) collective-permute-start(bf16[240,128]{1,0:T(8,128)(2,1)S(1)} %add_convert_fusion.1), channel_id=1, source_target_pairs={{0,6},{1,7},{2,4},{3,5},{4,2},{5,3},{6,0},{7,1},{8,14},{9,15},{10,... | collective-permute-start | bytes 184328 | tf_op jit(solution)/shard_map/ppermute | solution.py:971
  64.8 6.5 %collective-permute-start.16 = (bf16[240,128]{1,0:T(8,128)(2,1)S(1)}, bf16[240,128]{1,0:T(8,128)(2,1)S(1)}, u32[]{:S(2)}, u32[]{:S(2)}) collective-permute-start(bf16[240,128]{1,0:T(8,128)(2,1)S(1)} %add_convert_fusion.1), channel_id=1, source_target_pairs={{0,4},{1,5},{2,6},{3,7},{4,0},{5,1},{6,2},{7,3},{8,12},{9,13},{10,... | collective-permute-start | bytes 184328 | tf_op jit(solution)/shard_map/ppermute | solution.py:971
  65.0 6.3 %collective-permute-start.15 = (bf16[240,128]{1,0:T(8,128)(2,1)S(1)}, bf16[240,128]{1,0:T(8,128)(2,1)S(1)}, u32[]{:S(2)}, u32[]{:S(2)}) collective-permute-start(bf16[240,128]{1,0:T(8,128)(2,1)S(1)} %add_convert_fusion.1), channel_id=1, source_target_pairs={{0,2},{1,3},{2,0},{3,1},{4,6},{5,7},{6,4},{7,5},{8,10},{9,11},{10,... | collective-permute-start | bytes 184328 | tf_op jit(solution)/shard_map/ppermute | solution.py:971
  71.3 4.3 %collective-permute-start.18 = (bf16[240,128]{1,0:T(8,128)(2,1)S(1)}, bf16[240,128]{1,0:T(8,128)(2,1)S(1)}, u32[]{:S(2)}, u32[]{:S(2)}) collective-permute-start(bf16[240,128]{1,0:T(8,128)(2,1)S(1)} %add_convert_fusion.refs_0_), channel_id=1, source_target_pairs={{0,8},{8,0},{16,24},{24,16},{1,9},{9,1},{17,25},{25,17},{2,10},{10... | collective-permute-start | bytes 184328 | tf_op jit(solution)/shard_map/ppermute | solution.py:971
  73.2 4.8 %collective-permute-start.19 = (bf16[240,128]{1,0:T(8,128)(2,1)S(1)}, bf16[240,128]{1,0:T(8,128)(2,1)S(1)}, u32[]{:S(2)}, u32[]{:S(2)}) collective-permute-start(bf16[240,128]{1,0:T(8,128)(2,1)S(1)} %add_convert_fusion.refs_0_), channel_id=1, source_target_pairs={{0,16},{8,24},{16,0},{24,8},{1,17},{9,25},{17,1},{25,9},{2,18},{10... | collective-permute-start | bytes 184328 | tf_op jit(solution)/shard_map/ppermute | solution.py:971
  73.6 5.1 %collective-permute-start.20 = (bf16[240,128]{1,0:T(8,128)(2,1)S(1)}, bf16[240,128]{1,0:T(8,128)(2,1)S(1)}, u32[]{:S(2)}, u32[]{:S(2)}) collective-permute-start(bf16[240,128]{1,0:T(8,128)(2,1)S(1)} %add_convert_fusion.refs_0_), channel_id=1, source_target_pairs={{0,24},{8,16},{16,8},{24,0},{1,25},{9,17},{17,9},{25,1},{2,26},{10... | collective-permute-start | bytes 184328 | tf_op jit(solution)/shard_map/ppermute | solution.py:971
  74.9 4.0 %collective-permute-start.10 = (f32[4,16,128]{2,1,0:T(8,128)S(1)}, f32[4,16,128]{2,1,0:T(8,128)S(1)}, u32[]{:S(2)}, u32[]{:S(2)}) collective-permute-start(f32[4,16,128]{2,1,0:T(8,128)S(1)} %get-tuple-element.121), channel_id=1, source_target_pairs={{0,1},{1,0},{2,3},{3,2},{4,5},{5,4},{6,7},{7,6},{8,9},{9,8},{10,11... | collective-permute-start | bytes 98312 | tf_op jit(solution)/shard_map/ppermute | solution.py:971
  78.8 1.6 %collective-permute-start.21 = (bf16[960,128]{1,0:T(8,128)(2,1)S(1)}, bf16[960,128]{1,0:T(8,128)(2,1)S(1)}, u32[]{:S(2)}, u32[]{:S(2)}) collective-permute-start(bf16[960,128]{1,0:T(8,128)(2,1)S(1)} %arrange.1.mine), channel_id=1, source_target_pairs={{0,1},{1,0},{2,3},{3,2},{4,5},{5,4},{6,7},{7,6},{8,9},{9,8},{10,11... | collective-permute-start | bytes 737288 | tf_op jit(solution)/shard_map/ppermute | solution.py:971
